TPU v7x, 32 devices: a whole 2x2x4 slice. The times are simulated.
32 devices in a mesh: tm: 8 (over y, x, core), panel: 4 (over z).
Axes of the slice: x: 2, y: 2, z: 4, core: 2. Of those that a mesh axis runs over, the one named last changes fastest.
Arguments:
- forward_element: bfloat16 [3, 8, 1024, 1024], P(None, 'tm', 'panel'), may hold values from -1 to 1
- backward_element: bfloat16 [3, 8, 1024, 1024], P(None, 'tm', 'panel'), may hold values from -1 to 1
Outputs:
- forward_joint: bfloat16 [3, 8, 1024, 1024], P(None, 'tm', 'panel')
- backward_joint: bfloat16 [3, 8, 1024, 1024], P(None, 'tm', 'panel')
All inputs are finite; a program needn't handle non-finite values.
Results may differ from a plain program's by a relative error of at most 0.0067.
Values may be sent and summed in bfloat16 or wider, within the bound.
No kernel may reach another device: no remote copies, remote signals or barrier semaphores. Data moves between devices by JAX's collectives and lax.ppermute only.
A program may use at most 128 MiB of HBM per device.

v0:
```python
import jax
import jax.numpy as jnp
from jax import lax
from jax.sharding import PartitionSpec as P

LEVELS = 2


def passed_along(block, axis, distance):
    devices = range(lax.axis_size(axis))
    route = [(i - distance, i) for i in devices if i - distance in devices]
    return lax.ppermute(block, axis, route)


def matmul(left, right):
    return jnp.dot(left, right, preferred_element_type=jnp.float32)


def combine(
    partner_cov,
    partner_trans,
    partner_info_rows,
    local_trans,
    local_info,
    local_cov_rows,
    row_start,
):
    row_count = local_cov_rows.shape[0]
    width = local_trans.shape[0]
    identity = jnp.eye(width, dtype=jnp.float32)
    kernel = matmul(partner_cov, local_info).astype(jnp.bfloat16)
    first_iterate = (identity - kernel).astype(jnp.bfloat16)
    second_iterate = (identity + kernel - matmul(kernel, first_iterate)).astype(jnp.bfloat16)
    local_rows = lax.dynamic_slice_in_dim(local_trans, row_start, row_count, 0)
    factor = matmul(matmul(local_rows, first_iterate).astype(jnp.bfloat16), second_iterate).astype(
        jnp.bfloat16
    )
    joint_trans = matmul(factor, partner_trans).astype(jnp.bfloat16)
    middle = matmul(factor, partner_cov).astype(jnp.bfloat16)
    joint_cov = (
        lax.dot_general(
            middle, local_trans, (((1,), (1,)), ((), ())), preferred_element_type=jnp.float32
        )
        + local_cov_rows
    ).astype(jnp.bfloat16)
    columns = lax.dynamic_slice_in_dim(partner_trans, row_start, row_count, 1)
    upper_rows = lax.dot_general(
        columns, local_info, (((0,), (0,)), ((), ())), preferred_element_type=jnp.float32
    ).astype(jnp.bfloat16)
    upper_rows = matmul(upper_rows, first_iterate).astype(jnp.bfloat16)
    upper_rows = matmul(upper_rows, second_iterate).astype(jnp.bfloat16)
    joint_info = (matmul(upper_rows, partner_trans) + partner_info_rows).astype(jnp.bfloat16)
    return jnp.stack([joint_cov, joint_trans, joint_info])


def advance(element, stride):
    row_count = element.shape[1]
    row_start = lax.axis_index("panel") * row_count
    gathered = lax.all_gather(element, "panel", axis=1, tiled=True)
    shifted = passed_along(gathered[:2], "tm", stride)
    shifted_info = passed_along(element[2], "tm", stride)
    partner_cov, partner_trans = (shifted[0], shifted[1])
    local_trans, local_info = (gathered[1], gathered[2])
    combined = combine(
        partner_cov, partner_trans, shifted_info, local_trans, local_info, element[0], row_start
    )
    position = lax.axis_index("tm")
    chain_length = lax.axis_size("tm")
    if stride > 0:
        usable = position >= stride
    else:
        usable = position < chain_length + stride
    return jnp.where(usable, combined, element)


def shards(forward_element, backward_element):
    forward = forward_element[:, 0]
    backward = backward_element[:, 0]
    for level_index in range(LEVELS):
        stride = 1 << level_index
        forward = advance(forward, stride)
        backward = advance(backward, -stride)
    return (forward[:, None], backward[:, None])


def solution(mesh):
    return jax.shard_map(
        shards,
        mesh=mesh,
        in_specs=(P(None, "tm", "panel", None), P(None, "tm", "panel", None)),
        out_specs=(P(None, "tm", "panel", None), P(None, "tm", "panel", None)),
        check_vma=False,
    )
```

profile of v0, /device:TPU:10, one launch (start us, length us, event | category | flops | bytes accessed | tf_op | source)
XLA Modules:
  0.0 642.1 jit_solution(4177408600352240591)
XLA Ops:
  8.7 114.6 %all-gather.11.cloned.1.call-done = bf16[3,1,1024,1024]{3,2,1,0:T(8,128)(2,1)} async-done(((bf16[3,1,256,1024]{3,2,1,0:T(8,128)(2,1)}), bf16[3,1,1024,1024]{3,2,1,0:T(8,128)(2,1)}) %all-gather.11.cloned.1.call-update) | async-done | bytes 6291472 | tf_op jit(solution)/shard_map/all_gather | solution.py:59
  123.3 4.6 slice_bitcast_fusion.1
  129.9 3.5 collective-permute-start.1
  133.4 3.4 slice.122
  136.8 41.2 %collective-permute-done = bf16[2,1024,1024]{2,1,0:T(8,128)(2,1)} collective-permute-done((bf16[2,1024,1024]{2,1,0:T(8,128)(2,1)}, bf16[2,1024,1024]{2,1,0:T(8,128)(2,1)}, u32[]{:S(2)}, u32[]{:S(2)}) %collective-permute-start) | collective-permute-done | bytes 4194336 | tf_op jit(solution)/shard_map/ppermute | solution.py:12
  178.1 4.6 convolution_convert_fusion.3
  184.0 3.7 fusion.2
  187.7 4.5 convolution_convert_fusion.11
  194.7 3.3 slice.126
  198.1 4.5 fusion.123
  202.5 3.7 fusion.162
  206.2 3.8 fusion.165
  211.6 26.9 %all-gather.13.cloned.1.call-done = bf16[3,1,1024,1024]{3,2,1,0:T(8,128)(2,1)} async-done(((bf16[3,1,256,1024]{3,2,1,0:T(8,128)(2,1)}), bf16[3,1,1024,1024]{3,2,1,0:T(8,128)(2,1)}) %all-gather.13.cloned.1.call-update) | async-done | bytes 6291472 | tf_op jit(solution)/shard_map/all_gather | solution.py:59
  238.5 4.6 slice_bitcast_fusion
  248.3 3.4 slice.134
  251.7 39.6 %collective-permute-done.4 = bf16[2,1024,1024]{2,1,0:T(8,128)(2,1)} collective-permute-done((bf16[2,1024,1024]{2,1,0:T(8,128)(2,1)}, bf16[2,1024,1024]{2,1,0:T(8,128)(2,1)}, u32[]{:S(2)}, u32[]{:S(2)}) %collective-permute-start.4) | collective-permute-done | bytes 4194336 | tf_op jit(solution)/shard_map/ppermute | solution.py:12
  291.3 4.5 convolution_convert_fusion.1
  297.2 3.7 fusion.8
  300.9 4.5 convolution_convert_fusion.7
  305.5 3.3 fusion.114
  308.7 3.1 slice.138
  311.9 4.5 fusion.135
  316.4 4.5 fusion.150
  320.9 4.5 fusion.153
  328.2 26.0 %all-gather.7.cloned.1.call-done = bf16[3,1024,1024]{2,1,0:T(8,128)(2,1)} async-done(((bf16[3,256,1024]{2,1,0:T(8,128)(2,1)}), bf16[3,1024,1024]{2,1,0:T(8,128)(2,1)}) %all-gather.7.cloned.1.call-update) | async-done | bytes 6291472 | tf_op jit(solution)/shard_map/all_gather | solution.py:59
  354.2 4.6 slice.128
  358.8 3.4 collective-permute-start.2
  362.2 107.0 %all-gather.9.cloned.1.call-done = bf16[3,1024,1024]{2,1,0:T(8,128)(2,1)} async-done(((bf16[3,256,1024]{2,1,0:T(8,128)(2,1)}), bf16[3,1024,1024]{2,1,0:T(8,128)(2,1)}) %all-gather.9.cloned.1.call-update) | async-done | bytes 6291472 | tf_op jit(solution)/shard_map/all_gather | solution.py:59
  469.2 4.6 slice.140
  477.9 4.5 collective-permute-start.3
  486.7 3.1 slice.127
  492.8 4.5 convolution_convert_fusion.2
  497.4 3.8 fusion.5
  501.2 69.2 %collective-permute-done.6 = bf16[2,1024,1024]{2,1,0:T(8,128)(2,1)} collective-permute-done((bf16[2,1024,1024]{2,1,0:T(8,128)(2,1)}, bf16[2,1024,1024]{2,1,0:T(8,128)(2,1)}, u32[]{:S(2)}, u32[]{:S(2)}) %collective-permute-start.6) | collective-permute-done | bytes 4194336 | tf_op jit(solution)/shard_map/ppermute | solution.py:12
  570.4 4.5 convolution_convert_fusion
  576.3 3.8 fusion.11
  580.1 4.5 convolution_convert_fusion.9
  584.6 4.5 convolution_convert_fusion.5
  592.1 4.5 fusion.129
  596.6 3.3 fusion.183
  599.9 4.8 fusion.168
  604.7 4.5 fusion.171
  609.2 3.3 maximum_select_fusion.1
  612.5 3.1 slice.144
  615.6 4.5 fusion.141
  620.1 3.1 fusion.180
  623.3 4.3 fusion.174
  627.6 4.7 fusion.177
  (54 shorter events, 36.6 us)
Async XLA Ops:
  7.2 116.2 %all-gather.11.cloned.1.call-start = ((), (), s32[]{:S(2)}) async-start(), calls=%async_computation.2 | async-start | bytes 7864320 | tf_op jit(solution)/shard_map/all_gather | solution.py:59
  7.9 230.6 %all-gather.13.cloned.1.call-start = ((), (), s32[]{:S(2)}) async-start(), calls=%async_computation.3 | async-start | bytes 7864320 | tf_op jit(solution)/shard_map/all_gather | solution.py:59
  8.6 121.2 %copy-start = (bf16[3,1,256,1024]{3,2,1,0:T(8,128)(2,1)S(1)}, bf16[3,1,256,1024]{3,2,1,0:T(8,128)(2,1)}, u32[]{:S(2)}) copy-start(bf16[3,1,256,1024]{3,2,1,0:T(8,128)(2,1)} %param.2) | copy-start | bytes 4718596
  8.7 345.5 %all-gather.7.cloned.1.call-start = ((), (), s32[]{:S(2)}) async-start(), calls=%async_computation | async-start | bytes 7864320 | tf_op jit(solution)/shard_map/all_gather | solution.py:59
  127.9 50.1 %collective-permute-start = (bf16[2,1024,1024]{2,1,0:T(8,128)(2,1)}, bf16[2,1024,1024]{2,1,0:T(8,128)(2,1)}, u32[]{:S(2)}, u32[]{:S(2)}) collective-permute-start(bf16[2,1024,1024]{2,1,0:T(8,128)(2,1)} %slice_bitcast_fusion.1), channel_id=1, source_target_pairs={{0,4},{4,8},{8,12},{12,16},{16,20},{20,24},{24,28},{1,5},{5,9},{9,... | collective-permute-start | bytes 12582920 | tf_op jit(solution)/shard_map/ppermute | solution.py:12
  129.9 72.6 %collective-permute-start.1 = (bf16[256,1024]{1,0:T(8,128)(2,1)S(1)}, bf16[256,1024]{1,0:T(8,128)(2,1)S(1)}, u32[]{:S(2)}, u32[]{:S(2)}) collective-permute-start(bf16[256,1024]{1,0:T(8,128)(2,1)S(1)} %slice_bitcast_fusion.63), channel_id=1, source_target_pairs={{0,4},{4,8},{8,12},{12,16},{16,20},{20,24},{24,28},{1,5},{5,9},{9,... | collective-permute-start | bytes 1572872 | tf_op jit(solution)/shard_map/ppermute | solution.py:12
  182.7 1.3 copy-start.11
  194.7 15.4 %copy-start.2 = (bf16[256,1024]{1,0:T(8,128)(2,1)}, bf16[256,1024]{1,0:T(8,128)(2,1)S(1)}, u32[]{:S(2)}) copy-start(bf16[256,1024]{1,0:T(8,128)(2,1)S(1)} %fusion.108) | copy-start | bytes 1572868
  206.2 3.9 copy-start.3
  210.1 1.4 copy-start.4
  211.5 33.5 %copy-start.1 = (bf16[3,1,256,1024]{3,2,1,0:T(8,128)(2,1)S(1)}, bf16[3,1,256,1024]{3,2,1,0:T(8,128)(2,1)}, u32[]{:S(2)}) copy-start(bf16[3,1,256,1024]{3,2,1,0:T(8,128)(2,1)} %param.3) | copy-start | bytes 4718596
  211.5 257.7 %all-gather.9.cloned.1.call-start = ((), (), s32[]{:S(2)}) async-start(), calls=%async_computation.1 | async-start | bytes 7864320 | tf_op jit(solution)/shard_map/all_gather | solution.py:59
  243.1 48.2 %collective-permute-start.4 = (bf16[2,1024,1024]{2,1,0:T(8,128)(2,1)}, bf16[2,1024,1024]{2,1,0:T(8,128)(2,1)}, u32[]{:S(2)}, u32[]{:S(2)}) collective-permute-start(bf16[2,1024,1024]{2,1,0:T(8,128)(2,1)} %slice_bitcast_fusion), channel_id=1, source_target_pairs={{4,0},{8,4},{12,8},{16,12},{20,16},{24,20},{28,24},{5,1},{9,5},{13... | collective-permute-start | bytes 12582920 | tf_op jit(solution)/shard_map/ppermute | solution.py:12
  245.8 70.6 %collective-permute-start.5 = (bf16[256,1024]{1,0:T(8,128)(2,1)}, bf16[256,1024]{1,0:T(8,128)(2,1)}, u32[]{:S(2)}, u32[]{:S(2)}) collective-permute-start(bf16[256,1024]{1,0:T(8,128)(2,1)} %slice_bitcast_fusion.62), channel_id=1, source_target_pairs={{4,0},{8,4},{12,8},{16,12},{20,16},{24,20},{28,24},{5,1},{9,5},{13... | collective-permute-start | bytes 1572872 | tf_op jit(solution)/shard_map/ppermute | solution.py:12
  295.9 1.3 copy-start.12
  358.8 134.0 %collective-permute-start.2 = (bf16[2,1024,1024]{2,1,0:T(8,128)(2,1)}, bf16[2,1024,1024]{2,1,0:T(8,128)(2,1)}, u32[]{:S(2)}, u32[]{:S(2)}) collective-permute-start(bf16[2,1024,1024]{2,1,0:T(8,128)(2,1)} %slice.128), channel_id=1, source_target_pairs={{0,8},{4,12},{8,16},{12,20},{16,24},{20,28},{1,9},{5,13},{9,17},{1... | collective-permute-start | bytes 12582920 | tf_op jit(solution)/shard_map/ppermute | solution.py:12
  473.8 96.6 %collective-permute-start.6 = (bf16[2,1024,1024]{2,1,0:T(8,128)(2,1)}, bf16[2,1024,1024]{2,1,0:T(8,128)(2,1)}, u32[]{:S(2)}, u32[]{:S(2)}) collective-permute-start(bf16[2,1024,1024]{2,1,0:T(8,128)(2,1)} %slice.140), channel_id=1, source_target_pairs={{8,0},{12,4},{16,8},{20,12},{24,16},{28,20},{9,1},{13,5},{17,9},{2... | collective-permute-start | bytes 12582920 | tf_op jit(solution)/shard_map/ppermute | solution.py:12
  477.9 126.7 %collective-permute-start.3 = (bf16[256,1024]{1,0:T(8,128)(2,1)}, bf16[256,1024]{1,0:T(8,128)(2,1)}, u32[]{:S(2)}, u32[]{:S(2)}) collective-permute-start(bf16[256,1024]{1,0:T(8,128)(2,1)} %slice_bitcast_fusion.60), channel_id=1, source_target_pairs={{0,8},{4,12},{8,16},{12,20},{16,24},{20,28},{1,9},{5,13},{9,17},{1... | collective-permute-start | bytes 1572872 | tf_op jit(solution)/shard_map/ppermute | solution.py:12
  484.3 143.3 %collective-permute-start.7 = (bf16[256,1024]{1,0:T(8,128)(2,1)}, bf16[256,1024]{1,0:T(8,128)(2,1)}, u32[]{:S(2)}, u32[]{:S(2)}) collective-permute-start(bf16[256,1024]{1,0:T(8,128)(2,1)} %slice_bitcast_fusion.58), channel_id=1, source_target_pairs={{8,0},{12,4},{16,8},{20,12},{24,16},{28,20},{9,1},{13,5},{17,9},{2... | collective-permute-start | bytes 1572872 | tf_op jit(solution)/shard_map/ppermute | solution.py:12
  497.4 3.8 copy-start.10
  575.0 1.4 copy-start.9
  615.6 4.5 copy-start.8
  627.6 4.7 copy-start.5
  627.6 4.7 copy-start.6
  627.6 4.7 copy-start.7
Sparse Core Ops, SparseCore 0:
  9.6 113.7 all-gather.10
  124.9 113.5 all-gather.12
  240.6 113.5 all-gather.6
  355.6 113.5 all-gather.8
where the time goes:
time: 654 us; the launch traced here: 642 us
  waiting for transfers between devices  426 us (65%)
  matrix products  116 us (18%)
  local copies, waits for them, and re-layouts  52.7 us (8%)
  starting transfers between devices  22.4 us (3%)
  between operations  14.5 us (2%)
  other arithmetic  10.2 us (2%)
    all_gather x4, waiting for transfers between devices, advance(): gathered = lax.all_gather(element, 'panel', axis=1, tiled=True)  275 us
    ppermute x8, waiting for transfers between devices, passed_along(): return lax.ppermute(block, axis, route)  150 us
    dot_general x24, matrix products, matmul(): return jnp.dot(left, right, preferred_element_type=jnp.float32)  98.8 us
    ppermute x8, starting transfers between devices, passed_along(): return lax.ppermute(block, axis, route)  22.2 us
    slice x4, local copies, waits for them, and re-layouts, advance(): shifted = passed_along(gathered[:2], 'tm', stride)  18.4 us
    dot_general x4, matrix products, combine(): lax.dot_general(middle, local_trans, (((1,), (1,)), ((), ())), preferred_...  17.4 us
  transfers between devices with their start and end apart: 12, of which 7 were waited for; matrix products, arithmetic and copies ran while one was open for 26% of the time, Pallas kernels for 0%

commit v1 on v0

v1 whole, which is shorter than its diff:
```python
import functools

import jax
import jax.numpy as jnp
from jax import lax
from jax.experimental import pallas as pl
from jax.experimental.pallas import tpu as pltpu
from jax.sharding import PartitionSpec as P

AXES = ("tm", "panel")
VMEM_BYTES = 60 * 2**20
ANY = pl.BlockSpec(memory_space=pl.ANY)


class Plan:
    def __init__(self, groups, panels):
        self.groups, self.panels, self.half = groups, panels, panels // 2
        assert groups % 2 == 0 and panels % 4 == 0
        columns = range(groups // 2)
        half = self.half

        def table(forward_routes):
            last = groups * panels - 1
            routes = [(a * panels + b, c * panels + d) for (a, b), (c, d) in forward_routes]
            return routes + [(last - source, last - target) for source, target in routes]

        def in_range(routes):
            return [route for route in routes if route[1][0] < groups]

        everyone = [(t, z) for t in range(groups) for z in range(panels)]
        self.cross = [(t * panels + z, t * panels + (z + half) % panels) for t, z in everyone]
        self.core = [(t * panels + z, (t ^ 1) * panels + z) for t, z in everyone]
        self.gather = {}
        for d in range(1, half):
            routes = []
            for c in columns:
                even, odd = 2 * c, 2 * c + 1
                routes += [((even, (layer + d) % half), (even, layer)) for layer in (0, 1)]
                routes += [((odd, (1 + d) % half), (odd, 1)), ((odd, d), (odd + 2, 0))]
            self.gather[d] = table(in_range(routes))
        self.onward = table(in_range([((2 * c + 1, 0), (2 * c + 3, 0)) for c in columns]))
        q_devices = [(2 * c + layer, layer) for c in columns for layer in (0, 1)]
        p_devices = [(2 * c + 1 - layer, layer) for c in columns for layer in (0, 1)]
        self.next_q = table(in_range([((t, z), (t + 2, z)) for t, z in q_devices]))
        self.next_all = table(in_range([((t, z), (t + 2, z)) for t, z in q_devices + p_devices]))
        self.home_q, self.home_all = [], []
        last_t, last_z = groups - 1, panels - 1
        for j in range(panels):
            q_routes, p_routes = [], []
            for t, z in q_devices:
                q_routes += [((t, z), (t, j)), ((last_t - t, last_z - z), (last_t - t, (j + half) % panels))]
            for t, z in p_devices:
                segment = t ^ 1 if (t % 2) != z else t
                p_routes += [
                    ((t, z), (segment, (j + 1) % panels)),
                    ((last_t - t, last_z - z), (last_t - segment, (j + half + 1) % panels)),
                ]
            flat = lambda routes: [(a * panels + b, c * panels + d) for (a, b), (c, d) in routes]
            self.home_q.append(flat(q_routes))
            self.home_all.append(flat(q_routes + p_routes))


class Place:
    def __init__(self, plan):
        t, z = lax.axis_index("tm"), lax.axis_index("panel")
        self.plan = plan
        self.z = z
        self.forward = z < plan.half
        self.layer = jnp.where(self.forward, z, plan.panels - 1 - z)
        self.t = jnp.where(self.forward, t, plan.groups - 1 - t)
        core = lax.rem(self.t, 2)
        self.is_q = lax.rem(core + self.layer, 2) == 0
        self.is_p = jnp.logical_not(self.is_q)
        self.special = jnp.logical_and(core == 1, self.layer == 0)
        self.segment = self.t - core + self.layer

    def source(self, d):
        layer = lax.rem(self.layer + d, self.plan.half)
        return jnp.where(self.forward, layer, self.plan.panels - 1 - layer)


def call(kernel, out_shapes, operands, scratch=(), flops=0, out_space=pl.ANY):
    moved = sum(x.size * x.dtype.itemsize for x in list(operands) + list(out_shapes))
    return pl.pallas_call(
        kernel,
        out_shape=list(out_shapes),
        in_specs=[ANY] * len(operands),
        out_specs=[pl.BlockSpec(memory_space=out_space)] * len(out_shapes),
        scratch_shapes=list(scratch),
        compiler_params=pltpu.CompilerParams(vmem_limit_bytes=VMEM_BYTES),
        cost_estimate=pl.CostEstimate(flops=flops, bytes_accessed=moved, transcendentals=0),
    )(*operands)


def bf16(*shape):
    return jax.ShapeDtypeStruct(shape, jnp.bfloat16)


def assemble_kernel(plan, kind, *refs):
    half = plan.half
    own, s1_q, s1_p, onward_local, onward_crossed = refs[:5]
    local, crossed = refs[5 : 5 + half - 1], refs[5 + half - 1 : 5 + 2 * (half - 1)]
    out, sems = refs[-2], refs[-1]
    place = Place(plan)
    rows = out.shape[0] // plan.panels
    index = {
        "A": 1,
        "first": jnp.where(place.is_q, 2, 0),
        "third": jnp.where(place.is_q, 0, 2),
    }[kind]

    def target(block):
        return out.at[pl.ds(pl.multiple_of(block * rows, rows), rows), :]

    def put(source, block, sem):
        return pltpu.make_async_copy(source, target(block), sems.at[sem])

    ordinary = jnp.logical_not(place.special)
    here = place.source(0)
    there = lax.rem(here + half, plan.panels)
    pl.when(ordinary)(lambda: put(own.at[index], here, 0).start())
    pl.when(place.special)(lambda: put(onward_local.at[index], here, 0).start())
    pl.when(jnp.logical_and(ordinary, place.is_q))(lambda: put(s1_q, there, 1).start())
    pl.when(jnp.logical_and(ordinary, place.is_p))(lambda: put(s1_p, there, 1).start())
    pl.when(place.special)(lambda: put(onward_crossed, there, 1).start())
    rest = []
    for d in range(1, half):
        block = place.source(d)
        rest.append(put(local[d - 1].at[index], block, 2 * d))
        rest.append(put(crossed[d - 1], lax.rem(block + half, plan.panels), 2 * d + 1))
    for copy in rest:
        copy.start()
    put(s1_q, here, 0).wait()
    put(s1_q, there, 1).wait()
    for copy in rest:
        copy.wait()


def dot(a, b):
    return jnp.dot(a, b, preferred_element_type=jnp.float32)


def dot_dims(a, b, dims):
    return lax.dot_general(a, b, (dims, ((), ())), preferred_element_type=jnp.float32)


def identity(n):
    return (
        lax.broadcasted_iota(jnp.int32, (n, n), 0) == lax.broadcasted_iota(jnp.int32, (n, n), 1)
    ).astype(jnp.float32)


def store_blocks(plan, place, shift, result, outs, sems, condition):
    rows = result.shape[0] // plan.panels
    if len(outs) == 1:
        copies = [pltpu.make_async_copy(result, outs[0], sems.at[0])]
    else:
        base = jnp.where(place.forward, 0, plan.half) + shift
        copies = []
        for j, out in enumerate(outs):
            block = lax.rem(base + j, plan.panels)
            source = result.at[pl.ds(pl.multiple_of(block * rows, rows), rows), :]
            copies.append(pltpu.make_async_copy(source, out, sems.at[j]))

    def run():
        for copy in copies:
            copy.start()
        for copy in copies:
            copy.wait()

    pl.when(condition)(run)


def first_kernel(plan, stride, cp_q, jq_q, cp_p, jq_p, aq_ref, cq_ref, *refs):
    count = len(refs) - 10
    outs, (v_ref, r_ref) = refs[:count], refs[count : count + 2]
    cp, jq, aq, cq, x1, r, u, sems = refs[count + 2 :]
    place = Place(plan)
    usable = place.segment >= stride
    n = cp.shape[0]

    def fetch(source, target, i):
        return pltpu.make_async_copy(source, target, sems.at[i])

    @pl.when(place.is_q)
    def _():
        fetch(cp_q, cp, 0).start()
        fetch(jq_q, jq, 1).start()
        fetch(aq_ref, aq, 2).start()
        fetch(cq_ref, cq, 3).start()

    @pl.when(place.is_p)
    def _():
        fetch(cp_p, cp, 0).start()
        fetch(jq_p, jq, 1).start()

    fetch(cp_q, cp, 0).wait()
    fetch(jq_q, jq, 1).wait()

    @pl.when(usable)
    def _():
        u[...] = dot(cp[...], jq[...]).astype(jnp.bfloat16)
        x1[...] = (identity(n) - u[...]).astype(jnp.bfloat16)
        r[...] = (identity(n) + u[...] - dot(u[...], x1[...])).astype(jnp.bfloat16)

    @pl.when(place.is_q)
    def _():
        fetch(aq_ref, aq, 2).wait()
        fetch(cq_ref, cq, 3).wait()

    @pl.when(jnp.logical_and(usable, place.is_q))
    def _():
        u[...] = dot(aq[...], x1[...]).astype(jnp.bfloat16)
        x1[...] = dot(u[...], r[...]).astype(jnp.bfloat16)
        u[...] = dot(x1[...], cp[...]).astype(jnp.bfloat16)
        cq[...] = (dot_dims(u[...], aq[...], ((1,), (1,))) + cq[...]).astype(jnp.bfloat16)

    fetch(x1, v_ref, 0).start()
    fetch(r, r_ref, 1).start()
    store_blocks(plan, place, 0, cq, outs, sems.at[pl.ds(2, plan.panels)], place.is_q)
    fetch(x1, v_ref, 0).wait()
    fetch(r, r_ref, 1).wait()


def second_kernel(plan, stride, ap_q, ap_p, v_ref, r_ref, aq_ref, jq_ref, jp_ref, *refs):
    outs = refs[:-6]
    ap, v, r, jq, jp, sems = refs[-6:]
    place = Place(plan)
    usable = place.segment >= stride

    def fetch(source, target, i):
        return pltpu.make_async_copy(source, target, sems.at[i])

    @pl.when(place.is_q)
    def _():
        fetch(ap_q, ap, 0).start()
        fetch(v_ref, v, 1).start()
        fetch(aq_ref, jq, 2).start()

    @pl.when(place.is_p)
    def _():
        fetch(ap_p, ap, 0).start()
        fetch(v_ref, v, 1).start()
        fetch(jq_ref, jq, 2).start()
        fetch(r_ref, r, 3).start()
        fetch(jp_ref, jp, 4).start()

    fetch(ap_q, ap, 0).wait()
    fetch(v_ref, v, 1).wait()
    fetch(jq_ref, jq, 2).wait()

    @pl.when(place.is_p)
    def _():
        fetch(r_ref, r, 3).wait()
        fetch(jp_ref, jp, 4).wait()

    @pl.when(jnp.logical_and(usable, place.is_q))
    def _():
        jq[...] = dot(v[...], ap[...]).astype(jnp.bfloat16)

    @pl.when(jnp.logical_and(usable, place.is_p))
    def _():
        jq[...] = dot_dims(ap[...], jq[...], ((0,), (0,))).astype(jnp.bfloat16)
        v[...] = dot(jq[...], v[...]).astype(jnp.bfloat16)
        r[...] = dot(v[...], r[...]).astype(jnp.bfloat16)
        jq[...] = (dot(r[...], ap[...]) + jp[...]).astype(jnp.bfloat16)

    store_blocks(plan, place, jnp.where(place.is_q, 0, 1), jq, outs, sems, place.layer >= 0)


def home_kernel(plan, *refs):
    panels, half = plan.panels, plan.half
    c_rounds, aj_rounds = refs[:panels], refs[panels : 2 * panels]
    f_out, b_out, sems = refs[2 * panels :]
    z = lax.axis_index("panel")
    parts = [
        (c_rounds, 0, f_out.at[0]),
        (aj_rounds, 0, f_out.at[1]),
        (aj_rounds, 1, f_out.at[2]),
        (c_rounds, half, b_out.at[0]),
        (aj_rounds, half, b_out.at[1]),
        (aj_rounds, half + 1, b_out.at[2]),
    ]
    for i, (rounds, shift, target) in enumerate(parts):
        which = lax.rem(z - shift + 2 * panels, panels)
        for j, block in enumerate(rounds):
            pl.when(which == j)(pltpu.make_async_copy(block, target, sems.at[i]).start)
    for i, (rounds, shift, target) in enumerate(parts):
        pltpu.make_async_copy(rounds[0], target, sems.at[i]).wait()


def shards(plan, forward_element, backward_element):
    forward, backward = forward_element[:, 0], backward_element[:, 0]
    rows, n = forward.shape[1:]
    panels, half = plan.panels, plan.half
    full, block = bf16(n, n), bf16(rows, n)
    square = pltpu.VMEM((n, n), jnp.bfloat16)
    dma = pltpu.SemaphoreType.DMA

    def send(x, routes):
        return lax.ppermute(x, AXES, routes)

    t, z = lax.axis_index("tm"), lax.axis_index("panel")
    layer = jnp.where(z < half, z, panels - 1 - z)
    core = jnp.where(z < half, t, plan.groups - 1 - t) % 2
    to_q = {d: layer == (core + d) % half for d in range(1, half)}
    own = jnp.where(z < half, forward, backward)
    other_c, other_a, other_j = [jnp.where(z < half, backward[i], forward[i]) for i in range(3)]

    s1_a = send(other_a, plan.cross)
    s1_c = send(other_c, plan.cross)
    s1_j = send(other_j, plan.cross)
    steps = range(1, half)
    local = [send(own, plan.gather[d]) for d in steps]
    onward_local = send(own, plan.onward)
    crossed_a = [send(s1_a, plan.gather[d]) for d in steps]
    onward_a = send(s1_a, plan.onward)
    crossed_first = [send(jnp.where(to_q[d], s1_j, s1_c), plan.gather[d]) for d in steps]
    onward_first = send(s1_c, plan.onward)
    crossed_third = [send(jnp.where(to_q[d], s1_c, s1_j), plan.gather[d]) for d in steps]
    onward_third = send(s1_j, plan.onward)

    def assemble(kind, s1_q, s1_p, onward_crossed, crossed):
        return call(
            functools.partial(assemble_kernel, plan, kind),
            [full],
            [own, s1_q, s1_p, onward_local, onward_crossed, *local, *crossed],
            [dma((panels,))],
            out_space=pltpu.VMEM,
        )[0]

    a_own = assemble("A", s1_a, s1_a, onward_a, crossed_a)
    a_swap = send(a_own, plan.core)
    first_own = assemble("first", s1_j, s1_c, onward_first, crossed_first)
    first_swap = send(first_own, plan.core)
    third = assemble("third", s1_c, s1_j, onward_third, crossed_third)

    def first(stride, outs, cp_q, jq_q, cp_p, jq_p, aq, cq):
        return call(
            functools.partial(first_kernel, plan, stride),
            [*outs, full, full],
            [cp_q, jq_q, cp_p, jq_p, aq, cq],
            [square] * 7 + [dma((2 + panels,))],
            flops=12 * n**3,
        )

    def second(stride, outs, ap_q, ap_p, v, r, aq, jq, jp):
        return call(
            functools.partial(second_kernel, plan, stride),
            outs,
            [ap_q, ap_p, v, r, aq, jq, jp],
            [square] * 5 + [dma((max(5, panels),))],
            flops=8 * n**3,
        )

    c_new, v, r = first(1, [full], first_swap, first_own, first_own, first_swap, a_own, third)
    c_next = send(c_new, plan.next_q)
    (aj_new,) = second(1, [full], a_swap, a_own, v, r, a_own, first_swap, third)
    aj_next = send(aj_new, plan.next_all)
    aj_swap = send(aj_new, plan.core)
    c_next_swap = send(c_next, plan.core)

    *c_blocks, v, r = first(2, [block] * panels, c_next, aj_swap, c_next_swap, aj_new, aj_new, c_new)
    c_home = [send(x, routes) for x, routes in zip(c_blocks, plan.home_q)]
    aj_next_swap = send(aj_next, plan.core)
    aj_blocks = second(2, [block] * panels, aj_next, aj_next_swap, v, r, aj_new, aj_new, aj_next)
    aj_home = [send(x, routes) for x, routes in zip(aj_blocks, plan.home_all)]

    f_out, b_out = call(
        functools.partial(home_kernel, plan),
        [bf16(3, rows, n)] * 2,
        [*c_home, *aj_home],
        [dma((6,))],
        out_space=pltpu.VMEM,
    )
    return f_out[:, None], b_out[:, None]


def solution(mesh):
    plan = Plan(mesh.shape["tm"], mesh.shape["panel"])
    spec = P(None, "tm", "panel", None)
    return jax.shard_map(
        functools.partial(shards, plan),
        mesh=mesh,
        in_specs=(spec, spec),
        out_specs=(spec, spec),
        check_vma=False,
    )
```

time: 654 us -> 347 us (0.53); the launches traced: 642 us -> 346 us
  waiting for transfers between devices: 426 us -> 179 us
  matrix products: 116 us -> 0 us
  starting transfers between devices: 22.4 us -> 96.8 us
  Pallas kernels: 0 us -> 58.8 us
  local copies, waits for them, and re-layouts: 52.7 us -> 4.47 us
  between operations: 14.5 us -> 1.24 us
    all_gather x4 -> x0, waiting for transfers between devices: 275 us -> none  [advance(): gathered = lax.all_gather(element, 'panel', axis=1, tiled=True)]
    dot_general x28 -> x0, matrix products: 116 us -> none  [the longest x24 98.8 us: matmul(): return jnp.dot(left, right, preferred_element_type=jnp.float32)]
    ppermute x8 -> x26, starting transfers between devices: 22.2 us -> 96.8 us  [send(): return lax.ppermute(x, AXES, routes)]
    pallas_call x0 -> x8, Pallas kernels: none -> 58.8 us  [call(): pl.pallas_call(kernel, out_shape=list(out_shapes), in_specs=[ANY] * len(o...]
    slice x12 -> x0, local copies, waits for them, and re-layouts: 44 us -> none  [the longest x4 18.4 us: advance(): shifted = passed_along(gathered[:2], 'tm', stride)]
    ppermute x8 -> x26, waiting for transfers between devices: 150 us -> 179 us  [send(): return lax.ppermute(x, AXES, routes)]
  transfers between devices with their start and end apart: 12 -> 26, of which waited for: 7 -> 11; matrix products, arithmetic and copies ran while one was open for 26% -> 1% of each run, Pallas kernels for 0% -> 11%
where the time goes in v1:
time: 347 us; the launch traced here: 346 us
  waiting for transfers between devices  179 us (52%)
  starting transfers between devices  96.8 us (28%)
  Pallas kernels  58.8 us (17%)
  other arithmetic  5.47 us (2%)
  local copies, waits for them, and re-layouts  4.47 us (1%)
    ppermute x26, waiting for transfers between devices, send(): return lax.ppermute(x, AXES, routes)  179 us
    ppermute x26, starting transfers between devices, send(): return lax.ppermute(x, AXES, routes)  96.8 us
    pallas_call x8, Pallas kernels, call(): pl.pallas_call(kernel, out_shape=list(out_shapes), in_specs=[ANY] * len(o...  58.8 us
  transfers between devices with their start and end apart: 26, of which 11 were waited for; matrix products, arithmetic and copies ran while one was open for 1% of the time, Pallas kernels for 11%

profile of v1, /device:TPU:10, one launch (start us, length us, event | category | flops | bytes accessed | tf_op | source)
XLA Modules:
  0.0 346.1 jit_solution(3186079284862922906)
XLA Ops:
  0.7 2.2 fusion.refs_0_
  2.9 0.8 collective-permute-start.2
  3.6 2.4 collective-permute-start.4
  6.0 1.2 select_bitcast_fusion
  7.2 3.8 %collective-permute-start = (bf16[256,1024]{1,0:T(8,128)(2,1)}, bf16[256,1024]{1,0:T(8,128)(2,1)}, u32[]{:S(2)}, u32[]{:S(2)}) collective-permute-start(bf16[256,1024]{1,0:T(8,128)(2,1)} %get-tuple-element.35), channel_id=1, source_target_pairs={{0,2},{1,3},{2,0},{3,1},{4,6},{5,7},{6,4},{7,5},{8,10},{9,11},{10,... | collective-permute-start | bytes 1572872 | tf_op jit(solution)/shard_map/ppermute | solution.py:301
  11.1 45.4 %collective-permute-done.refs_1_.refs_2_ = bf16[256,1024]{1,0:T(8,128)(2,1)} collective-permute-done((bf16[256,1024]{1,0:T(8,128)(2,1)}, bf16[256,1024]{1,0:T(8,128)(2,1)}, u32[]{:S(2)}, u32[]{:S(2)}) %collective-permute-start) | collective-permute-done | bytes 524320 | tf_op jit(solution)/shard_map/ppermute | solution.py:301
  56.5 8.8 %collective-permute-done.1.refs_2_.refs_1_ = bf16[256,1024]{1,0:T(8,128)(2,1)} collective-permute-done((bf16[256,1024]{1,0:T(8,128)(2,1)}, bf16[256,1024]{1,0:T(8,128)(2,1)}, u32[]{:S(2)}, u32[]{:S(2)}) %collective-permute-start.1) | collective-permute-done | bytes 524320 | tf_op jit(solution)/shard_map/ppermute | solution.py:301
  65.3 2.1 broadcast_select_fusion
  67.3 1.9 collective-permute-start.5
  69.2 0.7 collective-permute-start.3
  69.9 11.2 %collective-permute-done.5.refs_6_ = bf16[256,1024]{1,0:T(8,128)(2,1)S(1)} collective-permute-done((bf16[256,1024]{1,0:T(8,128)(2,1)S(1)}, bf16[256,1024]{1,0:T(8,128)(2,1)S(1)}, u32[]{:S(2)}, u32[]{:S(2)}) %collective-permute-start.5) | collective-permute-done | bytes 524320 | tf_op jit(solution)/shard_map/ppermute | solution.py:301
  81.1 0.8 copy-done.10
  82.2 1.0 copy-done.1
  83.1 2.9 shard_map.41.jq_q.cp_p
  86.1 6.8 %collective-permute-start.7 = (bf16[256,1024]{1,0:T(8,128)(2,1)}, bf16[256,1024]{1,0:T(8,128)(2,1)S(1)}, u32[]{:S(2)}, u32[]{:S(2)}) collective-permute-start(bf16[256,1024]{1,0:T(8,128)(2,1)} %get-tuple-element.34), channel_id=1, source_target_pairs={{0,2},{1,3},{2,0},{3,1},{4,6},{5,7},{6,4},{7,5},{8,10},{9,11},{10,... | collective-permute-start | bytes 1572872 | tf_op jit(solution)/shard_map/ppermute | solution.py:301
  92.9 20.9 %collective-permute-done.7.refs_1_.refs_2_ = bf16[256,1024]{1,0:T(8,128)(2,1)S(1)} collective-permute-done((bf16[256,1024]{1,0:T(8,128)(2,1)}, bf16[256,1024]{1,0:T(8,128)(2,1)S(1)}, u32[]{:S(2)}, u32[]{:S(2)}) %collective-permute-start.7) | collective-permute-done | bytes 524320 | tf_op jit(solution)/shard_map/ppermute | solution.py:301
  114.6 3.3 collective-permute-start.9
  117.9 2.6 collective-permute-start.11
  120.4 0.7 collective-permute-start.10
  121.2 9.1 %collective-permute-done.9.refs_6_ = bf16[256,1024]{1,0:T(8,128)(2,1)S(1)} collective-permute-done((bf16[256,1024]{1,0:T(8,128)(2,1)S(1)}, bf16[256,1024]{1,0:T(8,128)(2,1)S(1)}, u32[]{:S(2)}, u32[]{:S(2)}) %collective-permute-start.9) | collective-permute-done | bytes 524320 | tf_op jit(solution)/shard_map/ppermute | solution.py:301
  130.2 0.8 copy-done.9
  131.1 2.9 shard_map.42.aq_ref.ap_p
  134.0 2.2 collective-permute-start.13
  136.2 5.2 %collective-permute-done.11.refs_6_ = bf16[256,1024]{1,0:T(8,128)(2,1)S(1)} collective-permute-done((bf16[256,1024]{1,0:T(8,128)(2,1)}, bf16[256,1024]{1,0:T(8,128)(2,1)S(1)}, u32[]{:S(2)}, u32[]{:S(2)}) %collective-permute-start.11) | collective-permute-done | bytes 524320 | tf_op jit(solution)/shard_map/ppermute | solution.py:301
  141.5 0.8 copy-done.5
  142.3 0.8 copy-done.6
  143.1 3.0 shard_map.43.cq_ref.jp_ref
  146.1 8.8 %shard_map.44 = (bf16[1024,1024]{1,0:T(8,128)(2,1)}, bf16[1024,1024]{1,0:T(8,128)(2,1)}, bf16[1024,1024]{1,0:T(8,128)(2,1)}) custom-call(bf16[1024,1024]{1,0:T(8,128)(2,1)} %collective-permute-done.6.cp_q.jq_p.jq_ref, bf16[1024,1024]{1,0:T(8,128)(2,1)} %shard_map.41.jq_q.cp_p, bf16[1024,1024]{1,0:T(8,128)(2,1)} %shard_map.41.jq_q.cp_p, ...), custom_call_target="tpu_custom_call" | custom-call | flops 12884901888 | bytes 18874368 | tf_op jit(solution)/shard_map/pallas_call | solution.py:84
  154.9 0.8 collective-permute-start.12
  155.7 14.3 %shard_map.45.jq_p.aq_ref.jq_ref = bf16[1024,1024]{1,0:T(8,128)(2,1)} custom-call(bf16[1024,1024]{1,0:T(8,128)(2,1)} %collective-permute-done.13.ap_q, bf16[1024,1024]{1,0:T(8,128)(2,1)} %shard_map.42.aq_ref.ap_p, bf16[1024,1024]{1,0:T(8,128)(2,1)} %get-tuple-element.18.v_ref, bf16[1024,1024]{1,0:T(8,128)(2,1)} %get-tuple-element.19.r_ref, ...), custom_call_target="tpu_custom_call" | custom-call | flops 8589934592 | bytes 16777216 | tf_op jit(solution)/shard_map/pallas_call | solution.py:84
  170.0 4.3 %collective-permute-start.20 = (bf16[1024,1024]{1,0:T(8,128)(2,1)}, bf16[1024,1024]{1,0:T(8,128)(2,1)}, u32[]{:S(2)}, u32[]{:S(2)}) collective-permute-start(bf16[1024,1024]{1,0:T(8,128)(2,1)} %shard_map.45.jq_p.aq_ref.jq_ref), channel_id=1, source_target_pairs={{0,8},{5,13},{8,16},{13,21},{16,24},{21,29},{4,12},{1,9},{12,20},{... | collective-permute-start | bytes 6291464 | tf_op jit(solution)/shard_map/ppermute | solution.py:301
  174.3 2.6 collective-permute-start.14
  176.9 32.4 %collective-permute-start.15 = (bf16[1024,1024]{1,0:T(8,128)(2,1)S(1)}, bf16[1024,1024]{1,0:T(8,128)(2,1)}, u32[]{:S(2)}, u32[]{:S(2)}) collective-permute-start(bf16[1024,1024]{1,0:T(8,128)(2,1)S(1)} %collective-permute-done.12.cp_q), channel_id=1, source_target_pairs={{0,4},{1,5},{2,6},{3,7},{4,0},{5,1},{6,2},{7,3},{8,12},{9,13},{10,... | collective-permute-start | bytes 6291464 | tf_op jit(solution)/shard_map/ppermute | solution.py:301
  209.3 11.5 %collective-permute-done.20.ap_q.jp_ref = bf16[1024,1024]{1,0:T(8,128)(2,1)} collective-permute-done((bf16[1024,1024]{1,0:T(8,128)(2,1)}, bf16[1024,1024]{1,0:T(8,128)(2,1)}, u32[]{:S(2)}, u32[]{:S(2)}) %collective-permute-start.20) | collective-permute-done | bytes 2097184 | tf_op jit(solution)/shard_map/ppermute | solution.py:301
  220.8 16.5 %collective-permute-start.21 = (bf16[1024,1024]{1,0:T(8,128)(2,1)}, bf16[1024,1024]{1,0:T(8,128)(2,1)}, u32[]{:S(2)}, u32[]{:S(2)}) collective-permute-start(bf16[1024,1024]{1,0:T(8,128)(2,1)} %collective-permute-done.20.ap_q.jp_ref), channel_id=1, source_target_pairs={{0,4},{1,5},{2,6},{3,7},{4,0},{5,1},{6,2},{7,3},{8,12},{9,13},{10,... | collective-permute-start | bytes 6291464 | tf_op jit(solution)/shard_map/ppermute | solution.py:301
  237.3 9.1 %shard_map.46 = (bf16[256,1024]{1,0:T(8,128)(2,1)}, bf16[256,1024]{1,0:T(8,128)(2,1)}, bf16[256,1024]{1,0:T(8,128)(2,1)}, bf16[256,1024]{1,0:T(8,128)(2,1)}, bf1...) custom-call(bf16[1024,1024]{1,0:T(8,128)(2,1)} %copy-done.18, bf16[1024,1024]{1,0:T(8,128)(2,1)} %collective-permute-done.14.jq_q, ...), custom_call_target="tpu_custom_call" | custom-call | flops 12884901888 | bytes 18874368 | tf_op jit(solution)/shard_map/pallas_call | solution.py:84
  246.4 14.3 %shard_map.47 = (bf16[256,1024]{1,0:T(8,128)(2,1)}, bf16[256,1024]{1,0:T(8,128)(2,1)}, bf16[256,1024]{1,0:T(8,128)(2,1)}, bf16[256,1024]{1,0:T(8,128)(2,1)}) custom-call(bf16[1024,1024]{1,0:T(8,128)(2,1)} %collective-permute-done.20.ap_q.jp_ref, bf16[1024,1024]{1,0:T(8,128)(2,1)} %collective-permute-done.21.ap_p, ...), custom_call_target="tpu_custom_call" | custom-call | flops 8589934592 | bytes 16777216 | tf_op jit(solution)/shard_map/pallas_call | solution.py:84
  260.7 3.9 %collective-permute-start.22 = (bf16[256,1024]{1,0:T(8,128)(2,1)}, bf16[256,1024]{1,0:T(8,128)(2,1)S(1)}, u32[]{:S(2)}, u32[]{:S(2)}) collective-permute-start(bf16[256,1024]{1,0:T(8,128)(2,1)} %get-tuple-element.26), channel_id=1, source_target_pairs={{0,0},{31,30},{5,4},{26,26},{8,8},{23,22},{13,12},{18,18},{16,16},... | collective-permute-start | bytes 1572872 | tf_op jit(solution)/shard_map/ppermute | solution.py:301
  264.6 3.5 %collective-permute-start.23 = (bf16[256,1024]{1,0:T(8,128)(2,1)}, bf16[256,1024]{1,0:T(8,128)(2,1)S(1)}, u32[]{:S(2)}, u32[]{:S(2)}) collective-permute-start(bf16[256,1024]{1,0:T(8,128)(2,1)} %get-tuple-element.27), channel_id=1, source_target_pairs={{0,1},{31,31},{5,5},{26,27},{8,9},{23,23},{13,13},{18,19},{16,17},... | collective-permute-start | bytes 1572872 | tf_op jit(solution)/shard_map/ppermute | solution.py:301
  268.1 1.0 collective-permute-start.24
  269.1 1.9 collective-permute-start.25
  271.7 0.7 collective-permute-done.22.refs_4_
  272.5 1.3 collective-permute-start.17
  273.8 29.0 %collective-permute-done.23.refs_5_ = bf16[256,1024]{1,0:T(8,128)(2,1)S(1)} collective-permute-done((bf16[256,1024]{1,0:T(8,128)(2,1)}, bf16[256,1024]{1,0:T(8,128)(2,1)S(1)}, u32[]{:S(2)}, u32[]{:S(2)}) %collective-permute-start.23) | collective-permute-done | bytes 524320 | tf_op jit(solution)/shard_map/ppermute | solution.py:301
  303.5 21.8 %collective-permute-done.24.refs_6_ = bf16[256,1024]{1,0:T(8,128)(2,1)S(1)} collective-permute-done((bf16[256,1024]{1,0:T(8,128)(2,1)}, bf16[256,1024]{1,0:T(8,128)(2,1)S(1)}, u32[]{:S(2)}, u32[]{:S(2)}) %collective-permute-start.24) | collective-permute-done | bytes 524320 | tf_op jit(solution)/shard_map/ppermute | solution.py:301
  325.3 1.3 collective-permute-start.19
  326.6 15.6 %collective-permute-done.19.refs_3_ = bf16[256,1024]{1,0:T(8,128)(2,1)} collective-permute-done((bf16[256,1024]{1,0:T(8,128)(2,1)}, bf16[256,1024]{1,0:T(8,128)(2,1)}, u32[]{:S(2)}, u32[]{:S(2)}) %collective-permute-start.19) | collective-permute-done | bytes 524320 | tf_op jit(solution)/shard_map/ppermute | solution.py:301
  342.3 3.6 %shard_map.48 = (bf16[3,256,1024]{2,1,0:T(8,128)(2,1)}, bf16[3,256,1024]{2,1,0:T(8,128)(2,1)}) custom-call(bf16[256,1024]{1,0:T(8,128)(2,1)} %copy-done.15, bf16[256,1024]{1,0:T(8,128)(2,1)} %copy-done.16, bf16[256,1024]{1,0:T(8,128)(2,1)} %copy-done.17, bf16[256,1024]{1,0:T(8,128)(2,1)} %collective-permute-done.19.refs_3_, bf16[256,1024]{1,0:T(8,128)(2,1)} %copy-done.11, ...), custom_call_target="tpu_custom_call" | custom-call | bytes 7340032 | tf_op jit(solution)/shard_map/pallas_call | solution.py:84
  (53 shorter events, 2.4 us)
Async XLA Ops:
  0.6 5.4 %copy-start.2 = (bf16[3,1,256,1024]{3,2,1,0:T(8,128)(2,1)S(1)}, bf16[3,1,256,1024]{3,2,1,0:T(8,128)(2,1)}, u32[]{:S(2)}) copy-start(bf16[3,1,256,1024]{3,2,1,0:T(8,128)(2,1)} %param.3) | copy-start | bytes 4718596
  0.6 5.4 %copy-start.3 = (bf16[3,1,256,1024]{3,2,1,0:T(8,128)(2,1)S(1)}, bf16[3,1,256,1024]{3,2,1,0:T(8,128)(2,1)}, u32[]{:S(2)}) copy-start(bf16[3,1,256,1024]{3,2,1,0:T(8,128)(2,1)} %param.2) | copy-start | bytes 4718596
  2.9 4.4 %copy-start = (bf16[3,256,1024]{2,1,0:T(8,128)(2,1)}, bf16[3,256,1024]{2,1,0:T(8,128)(2,1)S(1)}, u32[]{:S(2)}) copy-start(bf16[3,256,1024]{2,1,0:T(8,128)(2,1)S(1)} %fusion.refs_0_) | copy-start | bytes 4718596
  2.9 78.3 %collective-permute-start.2 = (bf16[3,256,1024]{2,1,0:T(8,128)(2,1)S(1)}, bf16[3,256,1024]{2,1,0:T(8,128)(2,1)S(1)}, u32[]{:S(2)}, u32[]{:S(2)}) collective-permute-start(bf16[3,256,1024]{2,1,0:T(8,128)(2,1)S(1)} %fusion.refs_0_), channel_id=1, source_target_pairs={{4,12},{12,20},{20,28},{27,19},{19,11},{11,3}} | collective-permute-start | bytes 4718600 | tf_op jit(solution)/shard_map/ppermute | solution.py:301
  3.6 78.3 %collective-permute-start.4 = (bf16[3,256,1024]{2,1,0:T(8,128)(2,1)S(1)}, bf16[3,256,1024]{2,1,0:T(8,128)(2,1)}, u32[]{:S(2)}, u32[]{:S(2)}) collective-permute-start(bf16[3,256,1024]{2,1,0:T(8,128)(2,1)S(1)} %fusion.refs_0_), channel_id=1, source_target_pairs={{1,0},{0,1},{4,5},{5,12},{9,8},{8,9},{12,13},{13,20},{17,16},{16,1... | collective-permute-start | bytes 4718600 | tf_op jit(solution)/shard_map/ppermute | solution.py:301
  7.2 49.2 %collective-permute-start = (bf16[256,1024]{1,0:T(8,128)(2,1)}, bf16[256,1024]{1,0:T(8,128)(2,1)}, u32[]{:S(2)}, u32[]{:S(2)}) collective-permute-start(bf16[256,1024]{1,0:T(8,128)(2,1)} %get-tuple-element.35), channel_id=1, source_target_pairs={{0,2},{1,3},{2,0},{3,1},{4,6},{5,7},{6,4},{7,5},{8,10},{9,11},{10,... | collective-permute-start | bytes 1572872 | tf_op jit(solution)/shard_map/ppermute | solution.py:301
  11.1 54.2 %collective-permute-start.1 = (bf16[256,1024]{1,0:T(8,128)(2,1)}, bf16[256,1024]{1,0:T(8,128)(2,1)}, u32[]{:S(2)}, u32[]{:S(2)}) collective-permute-start(bf16[256,1024]{1,0:T(8,128)(2,1)} %get-tuple-element.36), channel_id=1, source_target_pairs={{0,2},{1,3},{2,0},{3,1},{4,6},{5,7},{6,4},{7,5},{8,10},{9,11},{10,... | collective-permute-start | bytes 1572872 | tf_op jit(solution)/shard_map/ppermute | solution.py:301
  67.3 13.8 %collective-permute-start.5 = (bf16[256,1024]{1,0:T(8,128)(2,1)S(1)}, bf16[256,1024]{1,0:T(8,128)(2,1)S(1)}, u32[]{:S(2)}, u32[]{:S(2)}) collective-permute-start(bf16[256,1024]{1,0:T(8,128)(2,1)S(1)} %get-tuple-element.38), channel_id=1, source_target_pairs={{1,0},{0,1},{4,5},{5,12},{9,8},{8,9},{12,13},{13,20},{17,16},{16,1... | collective-permute-start | bytes 1572872 | tf_op jit(solution)/shard_map/ppermute | solution.py:301
  69.2 11.9 %collective-permute-start.3 = (bf16[256,1024]{1,0:T(8,128)(2,1)}, bf16[256,1024]{1,0:T(8,128)(2,1)S(1)}, u32[]{:S(2)}, u32[]{:S(2)}) collective-permute-start(bf16[256,1024]{1,0:T(8,128)(2,1)} %collective-permute-done.1.refs_2_.refs_1_), channel_id=1, source_target_pairs={{4,12},{12,20},{20,28},{27,19},{19,11},{11,3}} | collective-permute-start | bytes 1572872 | tf_op jit(solution)/shard_map/ppermute | solution.py:301
  81.1 1.0 copy-start.8
  81.1 0.8 copy-start.10
  82.0 1.1 copy-start.1
  86.0 60.0 %collective-permute-start.6 = (bf16[1024,1024]{1,0:T(8,128)(2,1)}, bf16[1024,1024]{1,0:T(8,128)(2,1)}, u32[]{:S(2)}, u32[]{:S(2)}) collective-permute-start(bf16[1024,1024]{1,0:T(8,128)(2,1)} %shard_map.41.jq_q.cp_p), channel_id=1, source_target_pairs={{0,4},{1,5},{2,6},{3,7},{4,0},{5,1},{6,2},{7,3},{8,12},{9,13},{10,... | collective-permute-start | bytes 6291464 | tf_op jit(solution)/shard_map/ppermute | solution.py:301
  86.1 27.8 %collective-permute-start.7 = (bf16[256,1024]{1,0:T(8,128)(2,1)}, bf16[256,1024]{1,0:T(8,128)(2,1)S(1)}, u32[]{:S(2)}, u32[]{:S(2)}) collective-permute-start(bf16[256,1024]{1,0:T(8,128)(2,1)} %get-tuple-element.34), channel_id=1, source_target_pairs={{0,2},{1,3},{2,0},{3,1},{4,6},{5,7},{6,4},{7,5},{8,10},{9,11},{10,... | collective-permute-start | bytes 1572872 | tf_op jit(solution)/shard_map/ppermute | solution.py:301
  113.9 16.4 %copy-start.4 = (bf16[256,1024]{1,0:T(8,128)(2,1)}, bf16[256,1024]{1,0:T(8,128)(2,1)S(1)}, u32[]{:S(2)}) copy-start(bf16[256,1024]{1,0:T(8,128)(2,1)S(1)} %collective-permute-done.7.refs_1_.refs_2_) | copy-start | bytes 1572868
  113.9 7.3 %collective-permute-start.8 = (bf16[256,1024]{1,0:T(8,128)(2,1)S(1)}, bf16[256,1024]{1,0:T(8,128)(2,1)S(1)}, u32[]{:S(2)}, u32[]{:S(2)}) collective-permute-start(bf16[256,1024]{1,0:T(8,128)(2,1)S(1)} %collective-permute-done.7.refs_1_.refs_2_), channel_id=1, source_target_pairs={{4,12},{12,20},{20,28},{27,19},{19,11},{11,3}} | collective-permute-start | bytes 1572872 | tf_op jit(solution)/shard_map/ppermute | solution.py:301
  114.6 15.7 %collective-permute-start.9 = (bf16[256,1024]{1,0:T(8,128)(2,1)S(1)}, bf16[256,1024]{1,0:T(8,128)(2,1)S(1)}, u32[]{:S(2)}, u32[]{:S(2)}) collective-permute-start(bf16[256,1024]{1,0:T(8,128)(2,1)S(1)} %collective-permute-done.7.refs_1_.refs_2_), channel_id=1, source_target_pairs={{1,0},{0,1},{4,5},{5,12},{9,8},{8,9},{12,13},{13,20},{17,16},{16,1... | collective-permute-start | bytes 1572872 | tf_op jit(solution)/shard_map/ppermute | solution.py:301
  117.9 23.6 %collective-permute-start.11 = (bf16[256,1024]{1,0:T(8,128)(2,1)}, bf16[256,1024]{1,0:T(8,128)(2,1)S(1)}, u32[]{:S(2)}, u32[]{:S(2)}) collective-permute-start(bf16[256,1024]{1,0:T(8,128)(2,1)} %get-tuple-element.37), channel_id=1, source_target_pairs={{1,0},{0,1},{4,5},{5,12},{9,8},{8,9},{12,13},{13,20},{17,16},{16,1... | collective-permute-start | bytes 1572872 | tf_op jit(solution)/shard_map/ppermute | solution.py:301
  120.4 21.0 %collective-permute-start.10 = (bf16[256,1024]{1,0:T(8,128)(2,1)}, bf16[256,1024]{1,0:T(8,128)(2,1)S(1)}, u32[]{:S(2)}, u32[]{:S(2)}) collective-permute-start(bf16[256,1024]{1,0:T(8,128)(2,1)} %collective-permute-done.refs_1_.refs_2_), channel_id=1, source_target_pairs={{4,12},{12,20},{20,28},{27,19},{19,11},{11,3}} | collective-permute-start | bytes 1572872 | tf_op jit(solution)/shard_map/ppermute | solution.py:301
  121.1 9.1 %copy-start.7 = (bf16[256,1024]{1,0:T(8,128)(2,1)}, bf16[256,1024]{1,0:T(8,128)(2,1)S(1)}, u32[]{:S(2)}) copy-start(bf16[256,1024]{1,0:T(8,128)(2,1)S(1)} %collective-permute-done.8.refs_4_) | copy-start | bytes 1572868
  130.2 0.8 copy-start.9
  134.0 21.7 %collective-permute-start.13 = (bf16[1024,1024]{1,0:T(8,128)(2,1)}, bf16[1024,1024]{1,0:T(8,128)(2,1)}, u32[]{:S(2)}, u32[]{:S(2)}) collective-permute-start(bf16[1024,1024]{1,0:T(8,128)(2,1)} %shard_map.42.aq_ref.ap_p), channel_id=1, source_target_pairs={{0,4},{1,5},{2,6},{3,7},{4,0},{5,1},{6,2},{7,3},{8,12},{9,13},{10,... | collective-permute-start | bytes 6291464 | tf_op jit(solution)/shard_map/ppermute | solution.py:301
  141.5 0.8 copy-start.5
  142.3 0.8 copy-start.6
  154.9 22.0 %collective-permute-start.12 = (bf16[1024,1024]{1,0:T(8,128)(2,1)}, bf16[1024,1024]{1,0:T(8,128)(2,1)S(1)}, u32[]{:S(2)}, u32[]{:S(2)}) collective-permute-start(bf16[1024,1024]{1,0:T(8,128)(2,1)} %get-tuple-element.17.cq_ref), channel_id=1, source_target_pairs={{0,8},{5,13},{8,16},{13,21},{16,24},{21,29},{31,23},{26,18},{23,15... | collective-permute-start | bytes 6291464 | tf_op jit(solution)/shard_map/ppermute | solution.py:301
  170.0 50.8 %collective-permute-start.20 = (bf16[1024,1024]{1,0:T(8,128)(2,1)}, bf16[1024,1024]{1,0:T(8,128)(2,1)}, u32[]{:S(2)}, u32[]{:S(2)}) collective-permute-start(bf16[1024,1024]{1,0:T(8,128)(2,1)} %shard_map.45.jq_p.aq_ref.jq_ref), channel_id=1, source_target_pairs={{0,8},{5,13},{8,16},{13,21},{16,24},{21,29},{4,12},{1,9},{12,20},{... | collective-permute-start | bytes 6291464 | tf_op jit(solution)/shard_map/ppermute | solution.py:301
  174.3 63.0 %collective-permute-start.14 = (bf16[1024,1024]{1,0:T(8,128)(2,1)}, bf16[1024,1024]{1,0:T(8,128)(2,1)}, u32[]{:S(2)}, u32[]{:S(2)}) collective-permute-start(bf16[1024,1024]{1,0:T(8,128)(2,1)} %shard_map.45.jq_p.aq_ref.jq_ref), channel_id=1, source_target_pairs={{0,4},{1,5},{2,6},{3,7},{4,0},{5,1},{6,2},{7,3},{8,12},{9,13},{10,... | collective-permute-start | bytes 6291464 | tf_op jit(solution)/shard_map/ppermute | solution.py:301
  176.9 60.4 %copy-start.18 = (bf16[1024,1024]{1,0:T(8,128)(2,1)}, bf16[1024,1024]{1,0:T(8,128)(2,1)S(1)}, u32[]{:S(2)}) copy-start(bf16[1024,1024]{1,0:T(8,128)(2,1)S(1)} %collective-permute-done.12.cp_q) | copy-start | bytes 6291460
  176.9 60.4 %collective-permute-start.15 = (bf16[1024,1024]{1,0:T(8,128)(2,1)S(1)}, bf16[1024,1024]{1,0:T(8,128)(2,1)}, u32[]{:S(2)}, u32[]{:S(2)}) collective-permute-start(bf16[1024,1024]{1,0:T(8,128)(2,1)S(1)} %collective-permute-done.12.cp_q), channel_id=1, source_target_pairs={{0,4},{1,5},{2,6},{3,7},{4,0},{5,1},{6,2},{7,3},{8,12},{9,13},{10,... | collective-permute-start | bytes 6291464 | tf_op jit(solution)/shard_map/ppermute | solution.py:301
  220.8 25.6 %collective-permute-start.21 = (bf16[1024,1024]{1,0:T(8,128)(2,1)}, bf16[1024,1024]{1,0:T(8,128)(2,1)}, u32[]{:S(2)}, u32[]{:S(2)}) collective-permute-start(bf16[1024,1024]{1,0:T(8,128)(2,1)} %collective-permute-done.20.ap_q.jp_ref), channel_id=1, source_target_pairs={{0,4},{1,5},{2,6},{3,7},{4,0},{5,1},{6,2},{7,3},{8,12},{9,13},{10,... | collective-permute-start | bytes 6291464 | tf_op jit(solution)/shard_map/ppermute | solution.py:301
  260.7 11.8 %collective-permute-start.22 = (bf16[256,1024]{1,0:T(8,128)(2,1)}, bf16[256,1024]{1,0:T(8,128)(2,1)S(1)}, u32[]{:S(2)}, u32[]{:S(2)}) collective-permute-start(bf16[256,1024]{1,0:T(8,128)(2,1)} %get-tuple-element.26), channel_id=1, source_target_pairs={{0,0},{31,30},{5,4},{26,26},{8,8},{23,22},{13,12},{18,18},{16,16},... | collective-permute-start | bytes 1572872 | tf_op jit(solution)/shard_map/ppermute | solution.py:301
  264.6 38.2 %collective-permute-start.23 = (bf16[256,1024]{1,0:T(8,128)(2,1)}, bf16[256,1024]{1,0:T(8,128)(2,1)S(1)}, u32[]{:S(2)}, u32[]{:S(2)}) collective-permute-start(bf16[256,1024]{1,0:T(8,128)(2,1)} %get-tuple-element.27), channel_id=1, source_target_pairs={{0,1},{31,31},{5,5},{26,27},{8,9},{23,23},{13,13},{18,19},{16,17},... | collective-permute-start | bytes 1572872 | tf_op jit(solution)/shard_map/ppermute | solution.py:301
  268.1 57.2 %collective-permute-start.24 = (bf16[256,1024]{1,0:T(8,128)(2,1)}, bf16[256,1024]{1,0:T(8,128)(2,1)S(1)}, u32[]{:S(2)}, u32[]{:S(2)}) collective-permute-start(bf16[256,1024]{1,0:T(8,128)(2,1)} %get-tuple-element.28), channel_id=1, source_target_pairs={{0,2},{31,28},{5,6},{26,24},{8,10},{23,20},{13,14},{18,16},{16,18}... | collective-permute-start | bytes 1572872 | tf_op jit(solution)/shard_map/ppermute | solution.py:301
  269.1 57.4 %collective-permute-start.25 = (bf16[256,1024]{1,0:T(8,128)(2,1)}, bf16[256,1024]{1,0:T(8,128)(2,1)S(1)}, u32[]{:S(2)}, u32[]{:S(2)}) collective-permute-start(bf16[256,1024]{1,0:T(8,128)(2,1)} %get-tuple-element.29), channel_id=1, source_target_pairs={{0,3},{31,29},{5,7},{26,25},{8,11},{23,21},{13,15},{18,17},{16,19}... | collective-permute-start | bytes 1572872 | tf_op jit(solution)/shard_map/ppermute | solution.py:301
  271.1 55.5 %collective-permute-start.16 = (bf16[256,1024]{1,0:T(8,128)(2,1)}, bf16[256,1024]{1,0:T(8,128)(2,1)S(1)}, u32[]{:S(2)}, u32[]{:S(2)}) collective-permute-start(bf16[256,1024]{1,0:T(8,128)(2,1)} %get-tuple-element.20), channel_id=1, source_target_pairs={{0,0},{31,30},{5,4},{26,26},{8,8},{23,22},{13,12},{18,18},{16,16},... | collective-permute-start | bytes 1572872 | tf_op jit(solution)/shard_map/ppermute | solution.py:301
  272.5 69.8 %copy-start.11 = (bf16[256,1024]{1,0:T(8,128)(2,1)}, bf16[256,1024]{1,0:T(8,128)(2,1)S(1)}, u32[]{:S(2)}) copy-start(bf16[256,1024]{1,0:T(8,128)(2,1)S(1)} %collective-permute-done.22.refs_4_) | copy-start | bytes 1572868
  272.5 54.1 %collective-permute-start.17 = (bf16[256,1024]{1,0:T(8,128)(2,1)}, bf16[256,1024]{1,0:T(8,128)(2,1)S(1)}, u32[]{:S(2)}, u32[]{:S(2)}) collective-permute-start(bf16[256,1024]{1,0:T(8,128)(2,1)} %get-tuple-element.21), channel_id=1, source_target_pairs={{0,1},{31,31},{5,5},{26,27},{8,9},{23,23},{13,13},{18,19},{16,17},... | collective-permute-start | bytes 1572872 | tf_op jit(solution)/shard_map/ppermute | solution.py:301
  302.8 39.5 %copy-start.12 = (bf16[256,1024]{1,0:T(8,128)(2,1)}, bf16[256,1024]{1,0:T(8,128)(2,1)S(1)}, u32[]{:S(2)}) copy-start(bf16[256,1024]{1,0:T(8,128)(2,1)S(1)} %collective-permute-done.23.refs_5_) | copy-start | bytes 1572868
  302.8 23.8 %collective-permute-start.18 = (bf16[256,1024]{1,0:T(8,128)(2,1)}, bf16[256,1024]{1,0:T(8,128)(2,1)S(1)}, u32[]{:S(2)}, u32[]{:S(2)}) collective-permute-start(bf16[256,1024]{1,0:T(8,128)(2,1)} %get-tuple-element.22), channel_id=1, source_target_pairs={{0,2},{31,28},{5,6},{26,24},{8,10},{23,20},{13,14},{18,16},{16,18}... | collective-permute-start | bytes 1572872 | tf_op jit(solution)/shard_map/ppermute | solution.py:301
  325.3 17.0 %copy-start.13 = (bf16[256,1024]{1,0:T(8,128)(2,1)}, bf16[256,1024]{1,0:T(8,128)(2,1)S(1)}, u32[]{:S(2)}) copy-start(bf16[256,1024]{1,0:T(8,128)(2,1)S(1)} %collective-permute-done.24.refs_6_) | copy-start | bytes 1572868
  325.3 17.0 %collective-permute-start.19 = (bf16[256,1024]{1,0:T(8,128)(2,1)}, bf16[256,1024]{1,0:T(8,128)(2,1)}, u32[]{:S(2)}, u32[]{:S(2)}) collective-permute-start(bf16[256,1024]{1,0:T(8,128)(2,1)} %get-tuple-element.23), channel_id=1, source_target_pairs={{0,3},{31,29},{5,7},{26,25},{8,11},{23,21},{13,15},{18,17},{16,19}... | collective-permute-start | bytes 1572872 | tf_op jit(solution)/shard_map/ppermute | solution.py:301
  326.6 15.7 %copy-start.14 = (bf16[256,1024]{1,0:T(8,128)(2,1)}, bf16[256,1024]{1,0:T(8,128)(2,1)S(1)}, u32[]{:S(2)}) copy-start(bf16[256,1024]{1,0:T(8,128)(2,1)S(1)} %collective-permute-done.25.refs_7_) | copy-start | bytes 1572868
  326.6 15.7 %copy-start.15 = (bf16[256,1024]{1,0:T(8,128)(2,1)}, bf16[256,1024]{1,0:T(8,128)(2,1)S(1)}, u32[]{:S(2)}) copy-start(bf16[256,1024]{1,0:T(8,128)(2,1)S(1)} %collective-permute-done.16.refs_0_) | copy-start | bytes 1572868
  326.6 15.7 %copy-start.16 = (bf16[256,1024]{1,0:T(8,128)(2,1)}, bf16[256,1024]{1,0:T(8,128)(2,1)S(1)}, u32[]{:S(2)}) copy-start(bf16[256,1024]{1,0:T(8,128)(2,1)S(1)} %collective-permute-done.17.refs_1_) | copy-start | bytes 1572868
  326.6 15.7 %copy-start.17 = (bf16[256,1024]{1,0:T(8,128)(2,1)}, bf16[256,1024]{1,0:T(8,128)(2,1)S(1)}, u32[]{:S(2)}) copy-start(bf16[256,1024]{1,0:T(8,128)(2,1)S(1)} %collective-permute-done.18.refs_2_) | copy-start | bytes 1572868

commit v2 on v0

v2 whole, which is shorter than its diff:
```python
import functools

import jax
import jax.numpy as jnp
from jax import lax
from jax.experimental import pallas as pl
from jax.experimental.pallas import tpu as pltpu
from jax.sharding import PartitionSpec as P

AXES = ("tm", "panel")
VMEM_BYTES = 60 * 2**20
TILE = 512
HBM = pl.BlockSpec(memory_space=pltpu.HBM)


class Plan:
    def __init__(self, groups, panels):
        self.groups, self.panels, self.half = groups, panels, panels // 2
        assert groups % 2 == 0 and panels % 4 == 0
        columns = range(groups // 2)
        half = self.half

        def table(forward_routes):
            last = groups * panels - 1
            routes = [(a * panels + b, c * panels + d) for (a, b), (c, d) in forward_routes]
            return routes + [(last - source, last - target) for source, target in routes]

        def in_range(routes):
            return [route for route in routes if route[1][0] < groups]

        everyone = [(t, z) for t in range(groups) for z in range(panels)]
        self.cross = [(t * panels + z, t * panels + (z + half) % panels) for t, z in everyone]
        self.core = [(t * panels + z, (t ^ 1) * panels + z) for t, z in everyone]
        self.gather = {}
        for d in range(1, half):
            routes = []
            for c in columns:
                even, odd = 2 * c, 2 * c + 1
                routes += [((even, (layer + d) % half), (even, layer)) for layer in (0, 1)]
                routes += [((odd, (1 + d) % half), (odd, 1)), ((odd, d), (odd + 2, 0))]
            self.gather[d] = table(in_range(routes))
        self.onward = table(in_range([((2 * c + 1, 0), (2 * c + 3, 0)) for c in columns]))
        q_devices = [(2 * c + layer, layer) for c in columns for layer in (0, 1)]
        p_devices = [(2 * c + 1 - layer, layer) for c in columns for layer in (0, 1)]
        self.next_q, self.next_p = [
            table(in_range([((t, z), (t + 2, z)) for t, z in devices])) for devices in (q_devices, p_devices)
        ]
        self.home_q, self.home_p = [], []
        last_t, last_z = groups - 1, panels - 1
        for j in range(panels):
            for devices, shift, rounds in ((q_devices, 0, self.home_q), (p_devices, 1, self.home_p)):
                routes = []
                for t, z in devices:
                    segment = t - t % 2 + z
                    routes.append((t * panels + z, segment * panels + (z + j + shift) % panels))
                    t, z, segment = last_t - t, last_z - z, last_t - segment
                    routes.append((t * panels + z, segment * panels + (z + j + shift) % panels))
                rounds.append(routes)


class Place:
    def __init__(self, plan):
        t, z = lax.axis_index("tm"), lax.axis_index("panel")
        self.plan = plan
        self.z = z
        self.forward = z < plan.half
        self.layer = jnp.where(self.forward, z, plan.panels - 1 - z)
        self.t = jnp.where(self.forward, t, plan.groups - 1 - t)
        core = lax.rem(self.t, 2)
        self.is_q = lax.rem(core + self.layer, 2) == 0
        self.is_p = jnp.logical_not(self.is_q)
        self.special = jnp.logical_and(core == 1, self.layer == 0)
        self.segment = self.t - core + self.layer

    def source(self, d):
        layer = lax.rem(self.layer + d, self.plan.half)
        return jnp.where(self.forward, layer, self.plan.panels - 1 - layer)


def call(kernel, out_shapes, operands, scratch=(), out_space=pltpu.HBM, flops=1):
    return pl.pallas_call(
        kernel,
        out_shape=list(out_shapes),
        in_specs=[HBM] * len(operands),
        out_specs=[pl.BlockSpec(memory_space=out_space)] * len(out_shapes),
        scratch_shapes=list(scratch),
        compiler_params=pltpu.CompilerParams(vmem_limit_bytes=VMEM_BYTES),
        cost_estimate=pl.CostEstimate(flops=flops, bytes_accessed=1, transcendentals=0),
    )(*operands)


def bf16(*shape):
    return jax.ShapeDtypeStruct(shape, jnp.bfloat16)


def whole(plan, place, kind, near, far, target, sems):
    half = plan.half
    own, onward_local, *local = near
    s1, onward_far, *gathered = far
    rows = target.shape[0] // plan.panels
    index = {"first": jnp.where(place.is_q, 2, 0), "A": 1, "third": jnp.where(place.is_q, 0, 2)}[kind]
    part = {"first": lambda x: x, "A": lambda x: x.at[0], "third": lambda x: x.at[1]}[kind]

    def put(source, block, sem):
        rows_there = target.at[pl.ds(pl.multiple_of(block * rows, rows), rows), :]
        return pltpu.make_async_copy(source, rows_there, sems.at[sem])

    copies = []
    for d in range(half):
        block = place.source(d)
        beyond = lax.rem(block + half, plan.panels)
        here, there = (own, s1.at[index]) if d == 0 else (local[d - 1], part(gathered[d - 1]))
        copies += [put(here.at[index], block, 2 * d), put(there, beyond, 2 * d + 1)]
        if d == 0:
            special = [put(onward_local.at[index], block, 0), put(part(onward_far), beyond, 1)]

    def start():
        @pl.when(place.special)
        def _():
            for copy in special:
                copy.start()

        @pl.when(jnp.logical_not(place.special))
        def _():
            for copy in copies[:2]:
                copy.start()

        for copy in copies[2:]:
            copy.start()

    def wait():
        for copy in copies:
            copy.wait()

    return start, wait


def split_raw(plan, refs):
    return refs[: 1 + plan.half], refs[1 + plan.half : 2 + 2 * plan.half], refs[2 + 2 * plan.half :]


def assemble_kernel(plan, kind, *refs):
    near, far, (out, sems) = split_raw(plan, refs)
    start, wait = whole(plan, Place(plan), kind, near, far, out, sems)
    start()
    wait()


def product(out, a, b, finish=lambda acc, rows: acc, a_transposed=False, b_transposed=False, tile=TILE):
    n = out.shape[0]
    tile = min(tile, n)
    dims = (((0 if a_transposed else 1,), (1 if b_transposed else 0,)), ((), ()))

    @pl.loop(0, n // tile)
    def _(i):
        rows = pl.ds(pl.multiple_of(i * tile, tile), tile)
        left = a[:, rows] if a_transposed else a[rows, :]
        acc = lax.dot_general(left, b[...], dims, preferred_element_type=jnp.float32)
        out[rows, :] = finish(acc, rows).astype(jnp.bfloat16)


def identity(rows, n):
    shape = (rows.size, n)
    row = lax.broadcasted_iota(jnp.int32, shape, 0) + rows.start
    return (row == lax.broadcasted_iota(jnp.int32, shape, 1)).astype(jnp.float32)


def both(place, sems, sem, source_q, source_p, target):
    copy_q = pltpu.make_async_copy(source_q, target, sems.at[sem])
    copy_p = pltpu.make_async_copy(source_p, target, sems.at[sem])
    pl.when(place.is_q)(copy_q.start)
    pl.when(place.is_p)(copy_p.start)
    return copy_q.wait


def block_copies(plan, place, shift, result, outs, sems):
    rows = result.shape[0] // plan.panels
    base = place.z + shift
    copies = []
    for j, out in enumerate(outs):
        block = lax.rem(base + j, plan.panels)
        source = result.at[pl.ds(pl.multiple_of(block * rows, rows), rows), :]
        copies.append(pltpu.make_async_copy(source, out, sems.at[j]))
    return copies


def run(condition, copies):
    @pl.when(condition)
    def _():
        for copy in copies:
            copy.start()
        for copy in copies:
            copy.wait()


def iterates(n, cp, jq, u, x1, r):
    def first_iterate(acc, rows):
        x1[rows, :] = (identity(rows, n) - acc.astype(jnp.bfloat16)).astype(jnp.bfloat16)
        return acc

    product(u, cp, jq, first_iterate, tile=n)
    product(r, u, x1, lambda acc, rows: identity(rows, n) + u[rows, :] - acc, tile=n)


def iterate_kernel(plan, stride, *refs):
    half = plan.half
    mine, theirs = refs[: 1 + half], refs[1 + half : 2 + 2 * half]
    x1_ref, r_ref, other_ref, cp, jq, u, x1, r, sems = refs[2 + 2 * half :]
    place = Place(plan)
    rows = cp.shape[0] // plan.panels

    def copies(parts, target, first_sem):
        near, *far = parts
        result = []
        for d in range(half):
            block = place.source(d)
            for source, at in ((near.at[d], block), (far[d], lax.rem(block + half, plan.panels))):
                there = target.at[pl.ds(pl.multiple_of(at * rows, rows), rows), :]
                result.append(pltpu.make_async_copy(source, there, sems.at[first_sem + len(result)]))
        return result

    to_q = copies(theirs, cp, 0) + copies(mine, jq, plan.panels)
    to_p = copies(mine, cp, 0) + copies(theirs, jq, plan.panels)
    for condition, loads in ((place.is_q, to_q), (place.is_p, to_p)):
        @pl.when(condition)
        def _():
            for copy in loads:
                copy.start()

    for copy in to_q:
        copy.wait()
    store_q = pltpu.make_async_copy(cp, other_ref, sems.at[0])
    store_p = pltpu.make_async_copy(jq, other_ref, sems.at[0])
    pl.when(place.is_q)(store_q.start)
    pl.when(place.is_p)(store_p.start)

    @pl.when(place.segment >= stride)
    def _():
        iterates(cp.shape[0], cp, jq, u, x1, r)

    run(place.layer >= 0, [pltpu.make_async_copy(x1, x1_ref, sems.at[1]), pltpu.make_async_copy(r, r_ref, sems.at[2])])
    store_q.wait()


def combine_kernel(plan, stride, cp_ref, x1_ref, r_ref, jq_ref, *refs):
    near, far, refs = split_raw(plan, refs)
    cj_ref, v_ref, a, x1, r, jc, u, w, third, sems, a_sems, third_sems = refs
    place = Place(plan)
    usable = place.segment >= stride
    start_a, wait_a = whole(plan, place, "A", near, far, a, a_sems)
    start_third, wait_third = whole(plan, place, "third", near, far, third, third_sems)
    start_a()
    wait_jc = both(place, sems, 0, cp_ref, jq_ref, jc)
    load_x1 = pltpu.make_async_copy(x1_ref, x1, sems.at[1])
    load_r = pltpu.make_async_copy(r_ref, r, sems.at[2])
    load_x1.start()
    load_r.start()
    start_third()
    wait_a()

    @pl.when(place.is_q)
    def _():
        load_x1.wait()
        load_r.wait()

        @pl.when(usable)
        def _():
            product(u, a, x1)
            product(w, u, r)

        store_v = pltpu.make_async_copy(w, v_ref, sems.at[3])
        store_v.start()
        wait_jc()

        @pl.when(usable)
        def _():
            product(u, w, jc)

        wait_third()

        @pl.when(usable)
        def _():
            product(third, u, a, lambda acc, rows: acc + third[rows, :], b_transposed=True)

        run(place.is_q, [pltpu.make_async_copy(third, cj_ref, sems.at[4])])
        store_v.wait()

    @pl.when(place.is_p)
    def _():
        wait_jc()

        @pl.when(usable)
        def _():
            product(u, a, jc, a_transposed=True)

        load_x1.wait()
        load_r.wait()

        @pl.when(usable)
        def _():
            product(w, u, x1)
            product(u, w, r)

        wait_third()

        @pl.when(usable)
        def _():
            product(jc, u, a, lambda acc, rows: acc + third[rows, :])

        run(place.is_p, [pltpu.make_async_copy(jc, cj_ref, sems.at[4])])


def factor_kernel(plan, stride, v_ref, ap_ref, aq_ref, out, v, ap, sems):
    place = Place(plan)
    usable = place.segment >= stride

    @pl.when(place.is_q)
    def _():
        loads = [pltpu.make_async_copy(v_ref, v, sems.at[0]), pltpu.make_async_copy(ap_ref, ap, sems.at[1])]
        run(usable, loads)

        @pl.when(usable)
        def _():
            product(v, v, ap)

        run(jnp.logical_not(usable), [pltpu.make_async_copy(aq_ref, v, sems.at[0])])
        run(place.is_q, [pltpu.make_async_copy(v, out, sems.at[2])])


def front_kernel(plan, stride, cp_q, jq_q, cp_p, jq_p, aq_ref, cq_ref, *refs):
    blocks = refs[: plan.panels]
    v_ref, r_ref, cp, jq, aq, x1, r, u, cq, sems = refs[plan.panels :]
    place = Place(plan)
    usable = place.segment >= stride
    n = cp.shape[0]

    wait_cp = both(place, sems, 0, cp_q, cp_p, cp)
    wait_jq = both(place, sems, 1, jq_q, jq_p, jq)
    load_aq = pltpu.make_async_copy(aq_ref, aq, sems.at[2])
    load_cq = pltpu.make_async_copy(cq_ref, cq, sems.at[3])
    pl.when(place.is_q)(load_aq.start)
    pl.when(place.is_q)(load_cq.start)
    wait_cp()
    wait_jq()

    @pl.when(usable)
    def _():
        iterates(n, cp, jq, u, x1, r)

    store_v = pltpu.make_async_copy(x1, v_ref, sems.at[0])
    store_r = pltpu.make_async_copy(r, r_ref, sems.at[1])

    @pl.when(place.is_p)
    def _():
        run(place.is_p, [store_v, store_r])

    @pl.when(place.is_q)
    def _():
        load_aq.wait()

        @pl.when(usable)
        def _():
            product(u, aq, x1, tile=n)
            product(x1, u, r, tile=n)

        store_v.start()

        @pl.when(usable)
        def _():
            product(u, x1, cp, tile=n)

        load_cq.wait()

        @pl.when(usable)
        def _():
            product(cq, u, aq, lambda acc, rows: acc + cq[rows, :], b_transposed=True, tile=n)

        run(place.is_q, block_copies(plan, place, 0, cq, blocks, sems.at[pl.ds(4, plan.panels)]))
        store_v.wait()


def trans_kernel(plan, stride, ap_q, ap_p, v_ref, r_ref, aq_ref, jq_ref, *refs):
    blocks = refs[: plan.panels]
    h_ref, ap, v, r, jq, u, sems = refs[plan.panels :]
    place = Place(plan)
    usable = place.segment >= stride
    wait_ap = both(place, sems, 0, ap_q, ap_p, ap)
    wait_jq = both(place, sems, 1, aq_ref, jq_ref, jq)
    load_v = pltpu.make_async_copy(v_ref, v, sems.at[2])
    load_r = pltpu.make_async_copy(r_ref, r, sems.at[3])
    load_v.start()
    pl.when(place.is_p)(load_r.start)
    wait_ap()
    wait_jq()

    @pl.when(place.is_q)
    def _():
        load_v.wait()

        @pl.when(usable)
        def _():
            product(jq, v, ap)

    run(place.is_q, block_copies(plan, place, 0, jq, blocks, sems.at[pl.ds(4, plan.panels)]))

    @pl.when(place.is_p)
    def _():
        @pl.when(usable)
        def _():
            product(u, ap, jq, a_transposed=True)

        load_v.wait()

        @pl.when(usable)
        def _():
            product(jq, u, v)

        load_r.wait()

        @pl.when(usable)
        def _():
            product(u, jq, r)

    run(place.is_p, [pltpu.make_async_copy(u, h_ref, sems.at[0])])


def info_kernel(plan, stride, h_ref, ap_ref, jp_ref, jq_ref, *refs):
    blocks = refs[: plan.panels]
    h, ap, jp, sems = refs[plan.panels :]
    place = Place(plan)
    usable = place.segment >= stride

    @pl.when(place.is_p)
    def _():
        pairs = [(h_ref, h), (ap_ref, ap), (jp_ref, jp)]
        loads = [pltpu.make_async_copy(s, d, sems.at[i]) for i, (s, d) in enumerate(pairs)]
        load_jq = pltpu.make_async_copy(jq_ref, jp, sems.at[2])

        @pl.when(usable)
        def _():
            for copy in loads:
                copy.start()
            for copy in loads:
                copy.wait()
            product(jp, h, ap, lambda acc, rows: acc + jp[rows, :])

        run(jnp.logical_not(usable), [load_jq])

    run(place.is_p, block_copies(plan, place, 1, jp, blocks, sems.at[pl.ds(3, plan.panels)]))


def home_kernel(plan, *refs):
    panels = plan.panels
    c_rounds, a_rounds, j_rounds = [refs[i * panels : (i + 1) * panels] for i in range(3)]
    f_out, b_out, sems = refs[3 * panels :]
    t, z = lax.axis_index("tm"), lax.axis_index("panel")
    forward_source = lax.rem(t, 2)
    backward_source = panels - 1 - lax.rem(plan.groups - 1 - t, 2)
    waits = []
    for out, source in ((f_out, forward_source), (b_out, backward_source)):
        for i, (rounds, shift) in enumerate(((c_rounds, 0), (a_rounds, 0), (j_rounds, 1))):
            which = lax.rem(z - source - shift + 2 * panels, panels)
            sem = sems.at[len(waits)]
            for j, block in enumerate(rounds):
                pl.when(which == j)(pltpu.make_async_copy(block, out.at[i], sem).start)
            waits.append(pltpu.make_async_copy(rounds[0], out.at[i], sem))
    for copy in waits:
        copy.wait()


def after(x, *others):
    return lax.optimization_barrier((x, *others))[0]


def shards(plan, forward_element, backward_element):
    forward, backward = forward_element[:, 0], backward_element[:, 0]
    rows, n = forward.shape[1:]
    panels, half = plan.panels, plan.half
    full, block = bf16(n, n), bf16(rows, n)
    square = pltpu.VMEM((n, n), jnp.bfloat16)
    dma = pltpu.SemaphoreType.DMA

    def send(x, routes):
        return lax.ppermute(x, AXES, routes)

    def kernel(body, *static):
        return functools.partial(body, plan, *static)

    t, z = lax.axis_index("tm"), lax.axis_index("panel")
    layer = jnp.where(z < half, z, panels - 1 - z)
    core = jnp.where(z < half, t, plan.groups - 1 - t) % 2
    to_q = {d: layer == (core + d) % half for d in range(1, half)}
    own = jnp.where(z < half, forward, backward)
    other = jnp.where(z < half, backward, forward)

    steps = range(1, half)
    s1 = send(other, plan.cross)
    local = [send(own, plan.gather[d]) for d in steps]
    onward_local = send(own, plan.onward)
    s1 = after(s1, onward_local, *local)
    gathered_first = [send(jnp.where(to_q[d], s1[2], s1[0]), plan.gather[d]) for d in steps]
    onward_first = send(s1[0], plan.onward)
    s1 = after(s1, onward_first)
    gathered_rest = [
        send(jnp.stack([s1[1], jnp.where(to_q[d], s1[0], s1[2])]), plan.gather[d]) for d in steps
    ]
    onward_rest = send(s1[1:], plan.onward)
    near = [own, onward_local, *local]

    is_q, special = (core + layer) % 2 == 0, (core == 1) & (layer == 0)

    def first_of(x):
        return jnp.where(is_q, x[2], x[0])

    early = jnp.stack([jnp.where(special, onward_local[0], first_of(own)), *map(first_of, local)])
    late = [jnp.where(special, onward_first, first_of(s1)), *gathered_first]
    x1, r, first_swap = call(
        kernel(iterate_kernel, 1),
        [full] * 3,
        [early, *late, send(early, plan.core), *[send(x, plan.core) for x in late]],
        [square] * 5 + [dma((2 * panels,))],
    )
    far_rest = [after(s1, x1), onward_rest, *gathered_rest]
    (a_own,) = call(
        kernel(assemble_kernel, "A"), [full], [*near, *far_rest], [dma((panels,))], out_space=pltpu.VMEM
    )
    a_swap = send(a_own, plan.core)
    cj_new, v = call(
        kernel(combine_kernel, 1),
        [full] * 2,
        [first_swap, after(x1, a_own), r, first_swap, *near, *far_rest],
        [square] * 7 + [dma((5,)), dma((panels,)), dma((panels,))],
    )
    c_next = send(cj_new, plan.next_q)
    j_swap = send(cj_new, plan.core)
    (a_new,) = call(
        kernel(factor_kernel, 1), [full], [v, after(a_swap, cj_new), a_own], [square] * 2 + [dma((3,))], flops=2 * n**3
    )
    c_next_swap = send(after(c_next, a_new), plan.core)
    a_next = send(after(a_new, c_next), plan.next_q)
    j_next = send(after(cj_new, c_next_swap), plan.next_p)

    *c_blocks, v, r = call(
        kernel(front_kernel, 2),
        [block] * panels + [full] * 2,
        [c_next, j_swap, c_next_swap, cj_new, a_new, cj_new],
        [square] * 7 + [dma((4 + panels,))],
    )
    c_home = [send(x, routes) for x, routes in zip(c_blocks[1:], plan.home_q[1:])]
    a_next = after(a_next, v, c_home[0])
    a_next_swap = send(a_next, plan.core)
    *a_blocks, h = call(
        kernel(trans_kernel, 2),
        [block] * panels + [full],
        [a_next, a_next_swap, v, r, a_new, cj_new],
        [square] * 5 + [dma((4 + panels,))],
    )
    a_home = [send(x, routes) for x, routes in zip(a_blocks[1:], plan.home_q[1:])]
    j_blocks = call(
        kernel(info_kernel, 2),
        [block] * panels,
        [h, a_next_swap, after(j_next, h, *c_home, a_home[0]), cj_new],
        [square] * 3 + [dma((3 + panels,))],
    )
    j_home = [send(x, routes) for x, routes in zip(j_blocks, plan.home_p)]

    f_out, b_out = call(
        kernel(home_kernel),
        [bf16(3, rows, n)] * 2,
        [c_blocks[0], *c_home, a_blocks[0], *a_home, *j_home],
        [dma((6,))],
        out_space=pltpu.VMEM,
    )
    return f_out[:, None], b_out[:, None]


def solution(mesh):
    plan = Plan(mesh.shape["tm"], mesh.shape["panel"])
    spec = P(None, "tm", "panel", None)
    return jax.shard_map(
        functools.partial(shards, plan),
        mesh=mesh,
        in_specs=(spec, spec),
        out_specs=(spec, spec),
        check_vma=False,
    )
```

time: 654 us -> 283 us (0.43); the launches traced: 642 us -> 278 us
  waiting for transfers between devices: 426 us -> 134 us
  matrix products: 116 us -> 0 us
  Pallas kernels: 0 us -> 58 us
  starting transfers between devices: 22.4 us -> 73.1 us
  local copies, waits for them, and re-layouts: 52.7 us -> 4.32 us
  between operations: 14.5 us -> 1.21 us
    all_gather x4 -> x0, waiting for transfers between devices: 275 us -> none  [advance(): gathered = lax.all_gather(element, 'panel', axis=1, tiled=True)]
    dot_general x28 -> x0, matrix products: 116 us -> none  [the longest x24 98.8 us: matmul(): return jnp.dot(left, right, preferred_element_type=jnp.float32)]
    pallas_call x0 -> x8, Pallas kernels: none -> 58 us  [call(): pl.pallas_call(kernel, out_shape=list(out_shapes), in_specs=[HBM] * len(o...]
    ppermute x8 -> x27, starting transfers between devices: 22.2 us -> 73.1 us  [send(): return lax.ppermute(x, AXES, routes)]
    slice x12 -> x1, local copies, waits for them, and re-layouts: 44 us -> 1.05 us  [shards(): onward_rest = send(s1[1:], plan.onward)]
    ppermute x8 -> x27, waiting for transfers between devices: 150 us -> 134 us  [send(): return lax.ppermute(x, AXES, routes)]
  transfers between devices with their start and end apart: 12 -> 27, of which waited for: 7 -> 12; matrix products, arithmetic and copies ran while one was open for 26% -> 2% of each run, Pallas kernels for 0% -> 19%
where the time goes in v2:
time: 283 us; the launch traced here: 278 us
  waiting for transfers between devices  134 us (47%)
  starting transfers between devices  73.1 us (26%)
  Pallas kernels  58 us (20%)
  other arithmetic  7.03 us (2%)
  local copies, waits for them, and re-layouts  4.32 us (2%)
    ppermute x27, waiting for transfers between devices, send(): return lax.ppermute(x, AXES, routes)  134 us
    ppermute x27, starting transfers between devices, send(): return lax.ppermute(x, AXES, routes)  73.1 us
    pallas_call x8, Pallas kernels, call(): pl.pallas_call(kernel, out_shape=list(out_shapes), in_specs=[HBM] * len(o...  58 us
  transfers between devices with their start and end apart: 27, of which 12 were waited for; matrix products, arithmetic and copies ran while one was open for 2% of the time, Pallas kernels for 19%

profile of v2, /device:TPU:10, one launch (start us, length us, event | category | flops | bytes accessed | tf_op | source)
XLA Modules:
  0.0 277.8 jit_solution(6173373425340885605)
XLA Ops:
  0.6 3.2 %fusion = (bf16[3,256,1024]{2,1,0:T(8,128)(2,1)}, bf16[3,1,256,1024]{3,2,0,1:T(8,128)(2,1)S(1)}) fusion(bf16[3,1,256,1024]{3,2,1,0:T(8,128)(2,1)} %param.3, bf16[3,1,256,1024]{3,2,1,0:T(8,128)(2,1)} %param.2, pred[]{:T(512)S(6)} %lt.20), kind=kLoop, calls=%fused_computation.2 | loop fusion | flops 1572864 | bytes 6291457 | tf_op jit(solution)/shard_map/jit(_where)/select_n | solution.py:494
  3.9 2.3 collective-permute-start.1
  6.2 1.8 collective-permute-start
  8.0 3.3 %collective-permute-start.2 = (bf16[3,256,1024]{2,1,0:T(8,128)(2,1)}, bf16[3,256,1024]{2,1,0:T(8,128)(2,1)S(1)}, u32[]{:S(2)}, u32[]{:S(2)}) collective-permute-start(bf16[3,256,1024]{2,1,0:T(8,128)(2,1)} %get-tuple-element.68), channel_id=1, source_target_pairs={{0,2},{1,3},{2,0},{3,1},{4,6},{5,7},{6,4},{7,5},{8,10},{9,11},{10,... | collective-permute-start | bytes 4718600 | tf_op jit(solution)/shard_map/ppermute | solution.py:484
  11.3 59.6 %collective-permute-done.1.refs_2_ = bf16[3,256,1024]{2,1,0:T(8,128)(2,1)} collective-permute-done((bf16[3,256,1024]{2,1,0:T(8,128)(2,1)S(1)}, bf16[3,256,1024]{2,1,0:T(8,128)(2,1)}, u32[]{:S(2)}, u32[]{:S(2)}) %collective-permute-start.1) | collective-permute-done | bytes 1572896 | tf_op jit(solution)/shard_map/ppermute | solution.py:484
  71.0 7.1 %collective-permute-done.2.refs_3_ = bf16[3,256,1024]{2,1,0:T(8,128)(2,1)S(1)} collective-permute-done((bf16[3,256,1024]{2,1,0:T(8,128)(2,1)}, bf16[3,256,1024]{2,1,0:T(8,128)(2,1)S(1)}, u32[]{:S(2)}, u32[]{:S(2)}) %collective-permute-start.2) | collective-permute-done | bytes 1572896 | tf_op jit(solution)/shard_map/ppermute | solution.py:484
  78.1 0.7 collective-permute-start.3
  78.8 1.1 fusion.2
  80.0 1.3 slice_select_fusion
  81.5 7.5 %collective-permute-start.4 = (bf16[256,1024]{1,0:T(8,128)(2,1)S(1)}, bf16[256,1024]{1,0:T(8,128)(2,1)S(1)}, u32[]{:S(2)}, u32[]{:S(2)}) collective-permute-start(bf16[256,1024]{1,0:T(8,128)(2,1)S(1)} %bitcast_select_fusion.2), channel_id=1, source_target_pairs={{1,0},{0,1},{4,5},{5,12},{9,8},{8,9},{12,13},{13,20},{17,16},{16,1... | collective-permute-start | bytes 1572872 | tf_op jit(solution)/shard_map/ppermute | solution.py:484
  89.1 1.0 slice.47
  90.2 0.7 collective-permute-start.8
  90.9 1.1 pad_maximum_fusion.1
  92.0 1.9 collective-permute-start.9
  94.0 6.8 %collective-permute-start.6 = (bf16[256,1024]{1,0:T(8,128)(2,1)S(1)}, bf16[256,1024]{1,0:T(8,128)(2,1)S(1)}, u32[]{:S(2)}, u32[]{:S(2)}) collective-permute-start(bf16[256,1024]{1,0:T(8,128)(2,1)S(1)} %bitcast_select_fusion.3.refs_1_), channel_id=1, source_target_pairs={{0,4},{1,5},{2,6},{3,7},{4,0},{5,1},{6,2},{7,3},{8,12},{9,13},{10,... | collective-permute-start | bytes 1572872 | tf_op jit(solution)/shard_map/ppermute | solution.py:484
  101.1 1.3 collective-permute-done.6.refs_4_
  102.4 0.7 collective-permute-done.7.refs_5_
  103.2 0.8 copy-done.18
  104.1 8.8 %shard_map.41 = (bf16[1024,1024]{1,0:T(8,128)(2,1)}, bf16[1024,1024]{1,0:T(8,128)(2,1)}, bf16[1024,1024]{1,0:T(8,128)(2,1)}) custom-call(bf16[2,256,1024]{2,1,0:T(8,128)(2,1)} %copy-done.4, bf16[256,1024]{1,0:T(8,128)(2,1)} %copy-done.6, bf16[256,1024]{1,0:T(8,128)(2,1)} %copy-done.16, bf16[2,256,1024]{2,1,0:T(8,128)(2,1)} %copy-done.7, ...), custom_call_target="tpu_custom_call" | custom-call | flops 1 | bytes 1 | tf_op jit(solution)/shard_map/pallas_call | solution.py:81
  112.9 10.1 %collective-permute-done.9.refs_5_ = bf16[2,256,1024]{2,1,0:T(8,128)(2,1)} collective-permute-done((bf16[2,256,1024]{2,1,0:T(8,128)(2,1)}, bf16[2,256,1024]{2,1,0:T(8,128)(2,1)}, u32[]{:S(2)}, u32[]{:S(2)}) %collective-permute-start.9) | collective-permute-done | bytes 1048608 | tf_op jit(solution)/shard_map/ppermute | solution.py:484
  123.0 3.0 %shard_map.42.aq_ref = bf16[1024,1024]{1,0:T(8,128)(2,1)} custom-call(bf16[3,256,1024]{2,1,0:T(8,128)(2,1)} %bitcast.31, bf16[3,256,1024]{2,1,0:T(8,128)(2,1)} %collective-permute-done.refs_1_, bf16[3,256,1024]{2,1,0:T(8,128)(2,1)} %collective-permute-done.1.refs_2_, bf16[3,256,1024]{2,1,0:T(8,128)(2,1)} %copy-done, bf16[2,256,1024]{2,1,0:T(8,128)(2,1)} %copy-done.3, ...), custom_call_target="tpu_custom_call" | custom-call | flops 1 | bytes 1 | tf_op jit(solution)/shard_map/pallas_call | solution.py:81
  126.6 15.4 %shard_map.43 = (bf16[1024,1024]{1,0:T(8,128)(2,1)}, bf16[1024,1024]{1,0:T(8,128)(2,1)}) custom-call(bf16[1024,1024]{1,0:T(8,128)(2,1)} %get-tuple-element.36.cp_ref.jq_ref, bf16[1024,1024]{1,0:T(8,128)(2,1)} %get-tuple-element.39.x1_ref, bf16[1024,1024]{1,0:T(8,128)(2,1)} %get-tuple-element.40.r_ref, bf16[1024,1024]{1,0:T(8,128)(2,1)} %get-tuple-element.36.cp_ref.jq_ref, ...), custom_call_target="tpu_custom_call" | custom-call | flops 1 | bytes 1 | tf_op jit(solution)/shard_map/pallas_call | solution.py:81
  141.9 2.0 collective-permute-start.10
  144.2 1.3 copy-done.5
  145.5 23.5 %collective-permute-start.13 = (bf16[1024,1024]{1,0:T(8,128)(2,1)}, bf16[1024,1024]{1,0:T(8,128)(2,1)}, u32[]{:S(2)}, u32[]{:S(2)}) collective-permute-start(bf16[1024,1024]{1,0:T(8,128)(2,1)} %collective-permute-done.10.cp_q), channel_id=1, source_target_pairs={{0,4},{1,5},{2,6},{3,7},{4,0},{5,1},{6,2},{7,3},{8,12},{9,13},{10,... | collective-permute-start | bytes 6291464 | tf_op jit(solution)/shard_map/ppermute | solution.py:484
  169.1 2.0 collective-permute-start.17
  171.0 2.2 collective-permute-done.13.cp_p
  173.2 8.9 %shard_map.45 = (bf16[256,1024]{1,0:T(8,128)(2,1)}, bf16[256,1024]{1,0:T(8,128)(2,1)}, bf16[256,1024]{1,0:T(8,128)(2,1)}, bf16[256,1024]{1,0:T(8,128)(2,1)}, bf1...) custom-call(bf16[1024,1024]{1,0:T(8,128)(2,1)} %collective-permute-done.10.cp_q, ...), custom_call_target="tpu_custom_call" | custom-call | flops 1 | bytes 1 | tf_op jit(solution)/shard_map/pallas_call | solution.py:81
  182.1 1.3 collective-permute-start.14
  183.4 19.9 %collective-permute-done.14.refs_1_ = bf16[256,1024]{1,0:T(8,128)(2,1)S(1)} collective-permute-done((bf16[256,1024]{1,0:T(8,128)(2,1)}, bf16[256,1024]{1,0:T(8,128)(2,1)S(1)}, u32[]{:S(2)}, u32[]{:S(2)}) %collective-permute-start.14) | collective-permute-done | bytes 524320 | tf_op jit(solution)/shard_map/ppermute | solution.py:484
  203.3 4.0 %collective-permute-start.22 = (bf16[1024,1024]{1,0:T(8,128)(2,1)S(1)}, bf16[1024,1024]{1,0:T(8,128)(2,1)}, u32[]{:S(2)}, u32[]{:S(2)}) collective-permute-start(bf16[1024,1024]{1,0:T(8,128)(2,1)S(1)} %copy-done.1), channel_id=1, source_target_pairs={{4,12},{1,9},{12,20},{9,17},{20,28},{17,25},{27,19},{30,22},{19,11... | collective-permute-start | bytes 6291464 | tf_op jit(solution)/shard_map/ppermute | solution.py:484
  207.3 0.7 collective-permute-start.15
  208.0 1.3 collective-permute-start.16
  209.4 11.3 %shard_map.46 = (bf16[256,1024]{1,0:T(8,128)(2,1)}, bf16[256,1024]{1,0:T(8,128)(2,1)}, bf16[256,1024]{1,0:T(8,128)(2,1)}, bf16[256,1024]{1,0:T(8,128)(2,1)}, bf16[1024,1024]{1,0:T(8,128)(2,1)}) custom-call(bf16[1024,1024]{1,0:T(8,128)(2,1)} %collective-permute-done.17.ap_q, bf16[1024,1024]{1,0:T(8,128)(2,1)} %collective-permute-done.18.ap_p.ap_ref, ...), custom_call_target="tpu_custom_call" | custom-call | flops 1 | bytes 1 | tf_op jit(solution)/shard_map/pallas_call | solution.py:81
  220.7 1.3 collective-permute-start.19
  222.0 1.5 collective-permute-start.20
  223.5 1.3 collective-permute-start.21
  224.7 14.7 %collective-permute-done.16.refs_3_ = bf16[256,1024]{1,0:T(8,128)(2,1)S(1)} collective-permute-done((bf16[256,1024]{1,0:T(8,128)(2,1)}, bf16[256,1024]{1,0:T(8,128)(2,1)S(1)}, u32[]{:S(2)}, u32[]{:S(2)}) %collective-permute-start.16) | collective-permute-done | bytes 524320 | tf_op jit(solution)/shard_map/ppermute | solution.py:484
  239.5 7.1 %shard_map.47 = (bf16[256,1024]{1,0:T(8,128)(2,1)}, bf16[256,1024]{1,0:T(8,128)(2,1)}, bf16[256,1024]{1,0:T(8,128)(2,1)}, bf16[256,1024]{1,0:T(8,128)(2,1)}) custom-call(bf16[1024,1024]{1,0:T(8,128)(2,1)} %get-tuple-element.57.h_ref, bf16[1024,1024]{1,0:T(8,128)(2,1)} %collective-permute-done.18.ap_p.ap_ref, ...), custom_call_target="tpu_custom_call" | custom-call | flops 1 | bytes 1 | tf_op jit(solution)/shard_map/pallas_call | solution.py:81
  246.6 1.9 collective-permute-start.23
  248.6 1.3 collective-permute-start.24
  249.9 3.6 %collective-permute-start.25 = (bf16[256,1024]{1,0:T(8,128)(2,1)}, bf16[256,1024]{1,0:T(8,128)(2,1)S(1)}, u32[]{:S(2)}, u32[]{:S(2)}) collective-permute-start(bf16[256,1024]{1,0:T(8,128)(2,1)} %get-tuple-element.62), channel_id=1, source_target_pairs={{4,3},{27,30},{1,4},{30,25},{12,11},{19,22},{9,12},{22,17},{20,19}... | collective-permute-start | bytes 1572872 | tf_op jit(solution)/shard_map/ppermute | solution.py:484
  253.6 1.3 collective-permute-start.26
  254.9 12.0 %collective-permute-done.21.refs_7_ = bf16[256,1024]{1,0:T(8,128)(2,1)} collective-permute-done((bf16[256,1024]{1,0:T(8,128)(2,1)}, bf16[256,1024]{1,0:T(8,128)(2,1)}, u32[]{:S(2)}, u32[]{:S(2)}) %collective-permute-start.21) | collective-permute-done | bytes 524320 | tf_op jit(solution)/shard_map/ppermute | solution.py:484
  266.9 5.5 %collective-permute-done.24.refs_9_ = bf16[256,1024]{1,0:T(8,128)(2,1)S(1)} collective-permute-done((bf16[256,1024]{1,0:T(8,128)(2,1)}, bf16[256,1024]{1,0:T(8,128)(2,1)S(1)}, u32[]{:S(2)}, u32[]{:S(2)}) %collective-permute-start.24) | collective-permute-done | bytes 524320 | tf_op jit(solution)/shard_map/ppermute | solution.py:484
  272.4 0.8 collective-permute-done.25.refs_10_
  273.2 0.8 copy-done.14
  274.1 3.5 %shard_map.48 = (bf16[3,256,1024]{2,1,0:T(8,128)(2,1)}, bf16[3,256,1024]{2,1,0:T(8,128)(2,1)}) custom-call(bf16[256,1024]{1,0:T(8,128)(2,1)} %get-tuple-element.45.refs_0_, bf16[256,1024]{1,0:T(8,128)(2,1)} %copy-done.8, bf16[256,1024]{1,0:T(8,128)(2,1)} %copy-done.9, bf16[256,1024]{1,0:T(8,128)(2,1)} %copy-done.10, ...), custom_call_target="tpu_custom_call" | custom-call | flops 1 | bytes 1 | tf_op jit(solution)/shard_map/pallas_call | solution.py:81
  (62 shorter events, 1.8 us)
Async XLA Ops:
  3.9 76.1 %copy-start.2 = (bf16[3,1,256,1024]{3,2,0,1:T(8,128)(2,1)}, bf16[3,1,256,1024]{3,2,0,1:T(8,128)(2,1)S(1)}, u32[]{:S(2)}) copy-start(bf16[3,1,256,1024]{3,2,0,1:T(8,128)(2,1)S(1)} %get-tuple-element.69) | copy-start | bytes 4718596
  3.9 67.1 %collective-permute-start.1 = (bf16[3,256,1024]{2,1,0:T(8,128)(2,1)S(1)}, bf16[3,256,1024]{2,1,0:T(8,128)(2,1)}, u32[]{:S(2)}, u32[]{:S(2)}) collective-permute-start(bf16[3,256,1024]{2,1,0:T(8,128)(2,1)S(1)} %bitcast.29), channel_id=1, source_target_pairs={{1,0},{0,1},{4,5},{5,12},{9,8},{8,9},{12,13},{13,20},{17,16},{16,1... | collective-permute-start | bytes 4718600 | tf_op jit(solution)/shard_map/ppermute | solution.py:484
  6.2 64.7 %collective-permute-start = (bf16[3,256,1024]{2,1,0:T(8,128)(2,1)S(1)}, bf16[3,256,1024]{2,1,0:T(8,128)(2,1)}, u32[]{:S(2)}, u32[]{:S(2)}) collective-permute-start(bf16[3,256,1024]{2,1,0:T(8,128)(2,1)S(1)} %bitcast.30), channel_id=1, source_target_pairs={{4,12},{12,20},{20,28},{27,19},{19,11},{11,3}} | collective-permute-start | bytes 4718600 | tf_op jit(solution)/shard_map/ppermute | solution.py:484
  8.0 70.0 %collective-permute-start.2 = (bf16[3,256,1024]{2,1,0:T(8,128)(2,1)}, bf16[3,256,1024]{2,1,0:T(8,128)(2,1)S(1)}, u32[]{:S(2)}, u32[]{:S(2)}) collective-permute-start(bf16[3,256,1024]{2,1,0:T(8,128)(2,1)} %get-tuple-element.68), channel_id=1, source_target_pairs={{0,2},{1,3},{2,0},{3,1},{4,6},{5,7},{6,4},{7,5},{8,10},{9,11},{10,... | collective-permute-start | bytes 4718600 | tf_op jit(solution)/shard_map/ppermute | solution.py:484
  78.1 15.9 %copy-start = (bf16[3,256,1024]{2,1,0:T(8,128)(2,1)}, bf16[3,256,1024]{2,1,0:T(8,128)(2,1)S(1)}, u32[]{:S(2)}) copy-start(bf16[3,256,1024]{2,1,0:T(8,128)(2,1)S(1)} %collective-permute-done.2.refs_3_) | copy-start | bytes 4718596
  78.1 10.9 %collective-permute-start.3 = (bf16[256,1024]{1,0:T(8,128)(2,1)S(1)}, bf16[256,1024]{1,0:T(8,128)(2,1)S(1)}, u32[]{:S(2)}, u32[]{:S(2)}) collective-permute-start(bf16[256,1024]{1,0:T(8,128)(2,1)S(1)} %slice_bitcast_fusion), channel_id=1, source_target_pairs={{4,12},{12,20},{20,28},{27,19},{19,11},{11,3}} | collective-permute-start | bytes 1572872 | tf_op jit(solution)/shard_map/ppermute | solution.py:484
  81.3 7.8 %copy-start.4 = (bf16[2,256,1024]{2,1,0:T(8,128)(2,1)}, bf16[2,256,1024]{2,1,0:T(8,128)(2,1)S(1)}, u32[]{:S(2)}) copy-start(bf16[2,256,1024]{2,1,0:T(8,128)(2,1)S(1)} %pad_maximum_fusion.refs_0_) | copy-start | bytes 3145732
  81.3 19.8 %collective-permute-start.5 = (bf16[2,256,1024]{2,1,0:T(8,128)(2,1)S(1)}, bf16[2,256,1024]{2,1,0:T(8,128)(2,1)S(1)}, u32[]{:S(2)}, u32[]{:S(2)}) collective-permute-start(bf16[2,256,1024]{2,1,0:T(8,128)(2,1)S(1)} %pad_maximum_fusion.refs_0_), channel_id=1, source_target_pairs={{0,4},{1,5},{2,6},{3,7},{4,0},{5,1},{6,2},{7,3},{8,12},{9,13},{10,... | collective-permute-start | bytes 3145736 | tf_op jit(solution)/shard_map/ppermute | solution.py:484
  81.5 19.6 %collective-permute-start.4 = (bf16[256,1024]{1,0:T(8,128)(2,1)S(1)}, bf16[256,1024]{1,0:T(8,128)(2,1)S(1)}, u32[]{:S(2)}, u32[]{:S(2)}) collective-permute-start(bf16[256,1024]{1,0:T(8,128)(2,1)S(1)} %bitcast_select_fusion.2), channel_id=1, source_target_pairs={{1,0},{0,1},{4,5},{5,12},{9,8},{8,9},{12,13},{13,20},{17,16},{16,1... | collective-permute-start | bytes 1572872 | tf_op jit(solution)/shard_map/ppermute | solution.py:484
  90.2 22.7 %collective-permute-start.8 = (bf16[2,256,1024]{2,1,0:T(8,128)(2,1)}, bf16[2,256,1024]{2,1,0:T(8,128)(2,1)S(1)}, u32[]{:S(2)}, u32[]{:S(2)}) collective-permute-start(bf16[2,256,1024]{2,1,0:T(8,128)(2,1)} %slice.47), channel_id=1, source_target_pairs={{4,12},{12,20},{20,28},{27,19},{19,11},{11,3}} | collective-permute-start | bytes 3145736 | tf_op jit(solution)/shard_map/ppermute | solution.py:484
  92.0 31.0 %collective-permute-start.9 = (bf16[2,256,1024]{2,1,0:T(8,128)(2,1)}, bf16[2,256,1024]{2,1,0:T(8,128)(2,1)}, u32[]{:S(2)}, u32[]{:S(2)}) collective-permute-start(bf16[2,256,1024]{2,1,0:T(8,128)(2,1)} %pad_maximum_fusion.1), channel_id=1, source_target_pairs={{1,0},{0,1},{4,5},{5,12},{9,8},{8,9},{12,13},{13,20},{17,16},{16,1... | collective-permute-start | bytes 3145736 | tf_op jit(solution)/shard_map/ppermute | solution.py:484
  94.0 9.1 %copy-start.6 = (bf16[256,1024]{1,0:T(8,128)(2,1)}, bf16[256,1024]{1,0:T(8,128)(2,1)S(1)}, u32[]{:S(2)}) copy-start(bf16[256,1024]{1,0:T(8,128)(2,1)S(1)} %bitcast_select_fusion.3.refs_1_) | copy-start | bytes 1572868
  94.0 8.4 %collective-permute-start.6 = (bf16[256,1024]{1,0:T(8,128)(2,1)S(1)}, bf16[256,1024]{1,0:T(8,128)(2,1)S(1)}, u32[]{:S(2)}, u32[]{:S(2)}) collective-permute-start(bf16[256,1024]{1,0:T(8,128)(2,1)S(1)} %bitcast_select_fusion.3.refs_1_), channel_id=1, source_target_pairs={{0,4},{1,5},{2,6},{3,7},{4,0},{5,1},{6,2},{7,3},{8,12},{9,13},{10,... | collective-permute-start | bytes 1572872 | tf_op jit(solution)/shard_map/ppermute | solution.py:484
  101.1 2.0 copy-start.16
  101.1 2.0 collective-permute-start.7
  101.1 1.3 copy-start.7
  102.4 0.8 copy-start.17
  103.2 0.8 copy-start.18
  112.9 10.1 %copy-start.3 = (bf16[2,256,1024]{2,1,0:T(8,128)(2,1)}, bf16[2,256,1024]{2,1,0:T(8,128)(2,1)S(1)}, u32[]{:S(2)}) copy-start(bf16[2,256,1024]{2,1,0:T(8,128)(2,1)S(1)} %collective-permute-done.8.refs_4_) | copy-start | bytes 3145732
  126.0 18.2 %collective-permute-start.12 = (bf16[1024,1024]{1,0:T(8,128)(2,1)}, bf16[1024,1024]{1,0:T(8,128)(2,1)S(1)}, u32[]{:S(2)}, u32[]{:S(2)}) collective-permute-start(bf16[1024,1024]{1,0:T(8,128)(2,1)} %shard_map.42.aq_ref), channel_id=1, source_target_pairs={{0,4},{1,5},{2,6},{3,7},{4,0},{5,1},{6,2},{7,3},{8,12},{9,13},{10,... | collective-permute-start | bytes 6291464 | tf_op jit(solution)/shard_map/ppermute | solution.py:484
  141.9 3.6 %collective-permute-start.10 = (bf16[1024,1024]{1,0:T(8,128)(2,1)}, bf16[1024,1024]{1,0:T(8,128)(2,1)}, u32[]{:S(2)}, u32[]{:S(2)}) collective-permute-start(bf16[1024,1024]{1,0:T(8,128)(2,1)} %get-tuple-element.58.jq_p.cq_ref.jq_ref), channel_id=1, source_target_pairs={{0,8},{5,13},{8,16},{13,21},{16,24},{21,29},{31,23},{26,18},{23,15... | collective-permute-start | bytes 6291464 | tf_op jit(solution)/shard_map/ppermute | solution.py:484
  144.0 27.1 %collective-permute-start.11 = (bf16[1024,1024]{1,0:T(8,128)(2,1)}, bf16[1024,1024]{1,0:T(8,128)(2,1)}, u32[]{:S(2)}, u32[]{:S(2)}) collective-permute-start(bf16[1024,1024]{1,0:T(8,128)(2,1)} %get-tuple-element.58.jq_p.cq_ref.jq_ref), channel_id=1, source_target_pairs={{0,4},{1,5},{2,6},{3,7},{4,0},{5,1},{6,2},{7,3},{8,12},{9,13},{10,... | collective-permute-start | bytes 6291464 | tf_op jit(solution)/shard_map/ppermute | solution.py:484
  144.1 1.3 copy-start.5
  145.5 57.8 %copy-start.1 = (bf16[1024,1024]{1,0:T(8,128)(2,1)S(1)}, bf16[1024,1024]{1,0:T(8,128)(2,1)}, u32[]{:S(2)}) copy-start(bf16[1024,1024]{1,0:T(8,128)(2,1)} %get-tuple-element.58.jq_p.cq_ref.jq_ref) | copy-start | bytes 6291460
  145.5 27.7 %collective-permute-start.13 = (bf16[1024,1024]{1,0:T(8,128)(2,1)}, bf16[1024,1024]{1,0:T(8,128)(2,1)}, u32[]{:S(2)}, u32[]{:S(2)}) collective-permute-start(bf16[1024,1024]{1,0:T(8,128)(2,1)} %collective-permute-done.10.cp_q), channel_id=1, source_target_pairs={{0,4},{1,5},{2,6},{3,7},{4,0},{5,1},{6,2},{7,3},{8,12},{9,13},{10,... | collective-permute-start | bytes 6291464 | tf_op jit(solution)/shard_map/ppermute | solution.py:484
  169.1 14.3 %collective-permute-start.17 = (bf16[1024,1024]{1,0:T(8,128)(2,1)}, bf16[1024,1024]{1,0:T(8,128)(2,1)}, u32[]{:S(2)}, u32[]{:S(2)}) collective-permute-start(bf16[1024,1024]{1,0:T(8,128)(2,1)} %shard_map.44.aq_ref), channel_id=1, source_target_pairs={{0,8},{5,13},{8,16},{13,21},{16,24},{21,29},{31,23},{26,18},{23,15... | collective-permute-start | bytes 6291464 | tf_op jit(solution)/shard_map/ppermute | solution.py:484
  182.1 21.2 %collective-permute-start.14 = (bf16[256,1024]{1,0:T(8,128)(2,1)}, bf16[256,1024]{1,0:T(8,128)(2,1)S(1)}, u32[]{:S(2)}, u32[]{:S(2)}) collective-permute-start(bf16[256,1024]{1,0:T(8,128)(2,1)} %get-tuple-element.46), channel_id=1, source_target_pairs={{0,1},{31,28},{5,6},{26,27},{8,9},{23,20},{13,14},{18,19},{16,17},... | collective-permute-start | bytes 1572872 | tf_op jit(solution)/shard_map/ppermute | solution.py:484
  203.3 17.4 %copy-start.8 = (bf16[256,1024]{1,0:T(8,128)(2,1)}, bf16[256,1024]{1,0:T(8,128)(2,1)S(1)}, u32[]{:S(2)}) copy-start(bf16[256,1024]{1,0:T(8,128)(2,1)S(1)} %collective-permute-done.14.refs_1_) | copy-start | bytes 1572868
  203.3 6.1 %collective-permute-start.18 = (bf16[1024,1024]{1,0:T(8,128)(2,1)}, bf16[1024,1024]{1,0:T(8,128)(2,1)}, u32[]{:S(2)}, u32[]{:S(2)}) collective-permute-start(bf16[1024,1024]{1,0:T(8,128)(2,1)} %collective-permute-done.17.ap_q), channel_id=1, source_target_pairs={{0,4},{1,5},{2,6},{3,7},{4,0},{5,1},{6,2},{7,3},{8,12},{9,13},{10,... | collective-permute-start | bytes 6291464 | tf_op jit(solution)/shard_map/ppermute | solution.py:484
  203.3 36.2 %collective-permute-start.22 = (bf16[1024,1024]{1,0:T(8,128)(2,1)S(1)}, bf16[1024,1024]{1,0:T(8,128)(2,1)}, u32[]{:S(2)}, u32[]{:S(2)}) collective-permute-start(bf16[1024,1024]{1,0:T(8,128)(2,1)S(1)} %copy-done.1), channel_id=1, source_target_pairs={{4,12},{1,9},{12,20},{9,17},{20,28},{17,25},{27,19},{30,22},{19,11... | collective-permute-start | bytes 6291464 | tf_op jit(solution)/shard_map/ppermute | solution.py:484
  207.3 16.1 %collective-permute-start.15 = (bf16[256,1024]{1,0:T(8,128)(2,1)}, bf16[256,1024]{1,0:T(8,128)(2,1)S(1)}, u32[]{:S(2)}, u32[]{:S(2)}) collective-permute-start(bf16[256,1024]{1,0:T(8,128)(2,1)} %get-tuple-element.47), channel_id=1, source_target_pairs={{0,2},{31,29},{5,7},{26,24},{8,10},{23,21},{13,15},{18,16},{16,18}... | collective-permute-start | bytes 1572872 | tf_op jit(solution)/shard_map/ppermute | solution.py:484
  208.0 31.4 %collective-permute-start.16 = (bf16[256,1024]{1,0:T(8,128)(2,1)}, bf16[256,1024]{1,0:T(8,128)(2,1)S(1)}, u32[]{:S(2)}, u32[]{:S(2)}) collective-permute-start(bf16[256,1024]{1,0:T(8,128)(2,1)} %get-tuple-element.48), channel_id=1, source_target_pairs={{0,3},{31,30},{5,4},{26,25},{8,11},{23,22},{13,12},{18,17},{16,19}... | collective-permute-start | bytes 1572872 | tf_op jit(solution)/shard_map/ppermute | solution.py:484
  220.7 18.8 %collective-permute-start.19 = (bf16[256,1024]{1,0:T(8,128)(2,1)}, bf16[256,1024]{1,0:T(8,128)(2,1)S(1)}, u32[]{:S(2)}, u32[]{:S(2)}) collective-permute-start(bf16[256,1024]{1,0:T(8,128)(2,1)} %get-tuple-element.54), channel_id=1, source_target_pairs={{0,1},{31,28},{5,6},{26,27},{8,9},{23,20},{13,14},{18,19},{16,17},... | collective-permute-start | bytes 1572872 | tf_op jit(solution)/shard_map/ppermute | solution.py:484
  222.0 31.5 %collective-permute-start.20 = (bf16[256,1024]{1,0:T(8,128)(2,1)}, bf16[256,1024]{1,0:T(8,128)(2,1)}, u32[]{:S(2)}, u32[]{:S(2)}) collective-permute-start(bf16[256,1024]{1,0:T(8,128)(2,1)} %get-tuple-element.55), channel_id=1, source_target_pairs={{0,2},{31,29},{5,7},{26,24},{8,10},{23,21},{13,15},{18,16},{16,18}... | collective-permute-start | bytes 1572872 | tf_op jit(solution)/shard_map/ppermute | solution.py:484
  223.5 23.2 %copy-start.9 = (bf16[256,1024]{1,0:T(8,128)(2,1)}, bf16[256,1024]{1,0:T(8,128)(2,1)S(1)}, u32[]{:S(2)}) copy-start(bf16[256,1024]{1,0:T(8,128)(2,1)S(1)} %collective-permute-done.15.refs_2_) | copy-start | bytes 1572868
  223.5 43.5 %collective-permute-start.21 = (bf16[256,1024]{1,0:T(8,128)(2,1)}, bf16[256,1024]{1,0:T(8,128)(2,1)}, u32[]{:S(2)}, u32[]{:S(2)}) collective-permute-start(bf16[256,1024]{1,0:T(8,128)(2,1)} %get-tuple-element.56), channel_id=1, source_target_pairs={{0,3},{31,30},{5,4},{26,25},{8,11},{23,22},{13,12},{18,17},{16,19}... | collective-permute-start | bytes 1572872 | tf_op jit(solution)/shard_map/ppermute | solution.py:484
  239.5 7.2 %copy-start.10 = (bf16[256,1024]{1,0:T(8,128)(2,1)}, bf16[256,1024]{1,0:T(8,128)(2,1)S(1)}, u32[]{:S(2)}) copy-start(bf16[256,1024]{1,0:T(8,128)(2,1)S(1)} %collective-permute-done.16.refs_3_) | copy-start | bytes 1572868
  239.5 7.2 %copy-start.11 = (bf16[256,1024]{1,0:T(8,128)(2,1)}, bf16[256,1024]{1,0:T(8,128)(2,1)S(1)}, u32[]{:S(2)}) copy-start(bf16[256,1024]{1,0:T(8,128)(2,1)S(1)} %collective-permute-done.19.refs_5_) | copy-start | bytes 1572868
  246.6 20.3 %collective-permute-start.23 = (bf16[256,1024]{1,0:T(8,128)(2,1)}, bf16[256,1024]{1,0:T(8,128)(2,1)S(1)}, u32[]{:S(2)}, u32[]{:S(2)}) collective-permute-start(bf16[256,1024]{1,0:T(8,128)(2,1)} %get-tuple-element.60), channel_id=1, source_target_pairs={{4,1},{27,28},{1,6},{30,27},{12,9},{19,20},{9,14},{22,19},{20,17},... | collective-permute-start | bytes 1572872 | tf_op jit(solution)/shard_map/ppermute | solution.py:484
  248.6 23.8 %collective-permute-start.24 = (bf16[256,1024]{1,0:T(8,128)(2,1)}, bf16[256,1024]{1,0:T(8,128)(2,1)S(1)}, u32[]{:S(2)}, u32[]{:S(2)}) collective-permute-start(bf16[256,1024]{1,0:T(8,128)(2,1)} %get-tuple-element.61), channel_id=1, source_target_pairs={{4,2},{27,29},{1,7},{30,24},{12,10},{19,21},{9,15},{22,16},{20,18}... | collective-permute-start | bytes 1572872 | tf_op jit(solution)/shard_map/ppermute | solution.py:484
  249.9 23.3 %collective-permute-start.25 = (bf16[256,1024]{1,0:T(8,128)(2,1)}, bf16[256,1024]{1,0:T(8,128)(2,1)S(1)}, u32[]{:S(2)}, u32[]{:S(2)}) collective-permute-start(bf16[256,1024]{1,0:T(8,128)(2,1)} %get-tuple-element.62), channel_id=1, source_target_pairs={{4,3},{27,30},{1,4},{30,25},{12,11},{19,22},{9,12},{22,17},{20,19}... | collective-permute-start | bytes 1572872 | tf_op jit(solution)/shard_map/ppermute | solution.py:484
  253.6 19.6 %collective-permute-start.26 = (bf16[256,1024]{1,0:T(8,128)(2,1)}, bf16[256,1024]{1,0:T(8,128)(2,1)S(1)}, u32[]{:S(2)}, u32[]{:S(2)}) collective-permute-start(bf16[256,1024]{1,0:T(8,128)(2,1)} %get-tuple-element.63), channel_id=1, source_target_pairs={{4,0},{27,31},{1,5},{30,26},{12,8},{19,23},{9,13},{22,18},{20,16},... | collective-permute-start | bytes 1572872 | tf_op jit(solution)/shard_map/ppermute | solution.py:484
  266.9 6.2 %copy-start.12 = (bf16[256,1024]{1,0:T(8,128)(2,1)}, bf16[256,1024]{1,0:T(8,128)(2,1)S(1)}, u32[]{:S(2)}) copy-start(bf16[256,1024]{1,0:T(8,128)(2,1)S(1)} %collective-permute-done.23.refs_8_) | copy-start | bytes 1572868
  272.4 0.8 copy-start.13
  273.2 0.8 copy-start.14
  273.2 1.0 copy-start.15

commit v3 on v0

v3 whole, which is shorter than its diff:
```python
import functools

import jax
import jax.numpy as jnp
from jax import lax
from jax.experimental import pallas as pl
from jax.experimental.pallas import tpu as pltpu
from jax.sharding import PartitionSpec as P

AXES = ("tm", "panel")
VMEM_BYTES = 60 * 2**20
TILE = 512
HBM = pl.BlockSpec(memory_space=pltpu.HBM)


class Plan:
    def __init__(self, groups, panels):
        self.groups, self.panels, self.half = groups, panels, panels // 2
        assert groups % 2 == 0 and panels % 4 == 0
        columns = range(groups // 2)
        half = self.half

        def table(forward_routes):
            last = groups * panels - 1
            routes = [(a * panels + b, c * panels + d) for (a, b), (c, d) in forward_routes]
            return routes + [(last - source, last - target) for source, target in routes]

        def in_range(routes):
            return [route for route in routes if route[1][0] < groups]

        everyone = [(t, z) for t in range(groups) for z in range(panels)]
        self.core = [(t * panels + z, (t ^ 1) * panels + z) for t, z in everyone]
        q_of = {t: (t, t % 2) for t in range(groups)}
        p_of = {t: (t, 1) if t % 2 == 0 else (t + 2, 0) for t in range(groups)}
        self.cross = [table([((t, half + q), q_of[t]) for t in range(groups)]) for q in range(half)]
        self.forward = table(in_range([(q_of[t], p_of[t]) for t in range(groups)]))
        self.gather = {}
        for d in range(1, half):
            routes = [((t, (q_of[t][1] + d) % half), q_of[t]) for t in range(groups)]
            routes += [((t, (p_of[t][1] + d) % half), p_of[t]) for t in range(groups)]
            self.gather[d] = table(in_range(routes))
        self.onward = table(in_range([((t, 0), p_of[t]) for t in range(1, groups, 2)]))
        active = [(2 * c + core, layer) for c in columns for core in (0, 1) for layer in (0, 1)]
        self.next = table(in_range([((t, z), (t + 2, z)) for t, z in active]))
        self.home = {}
        for far in (True, False):
            for i in range(half // 2):
                routes = []
                for t, z in active:
                    d = i + (half // 2 if (t + z) % 2 == 0 else 0)
                    routes.append(((t, z), (t - t % 2 + z, half + d if far else (z + d) % half)))
                self.home[far, i] = table(routes)


class Place:
    def __init__(self, plan):
        t, z = lax.axis_index("tm"), lax.axis_index("panel")
        self.plan = plan
        self.forward = z < plan.half
        self.layer = jnp.where(self.forward, z, plan.panels - 1 - z)
        self.t = jnp.where(self.forward, t, plan.groups - 1 - t)
        core = lax.rem(self.t, 2)
        self.is_q = lax.rem(core + self.layer, 2) == 0
        self.is_p = jnp.logical_not(self.is_q)
        self.segment = self.t - core + self.layer

    def near(self, d):
        layer = lax.rem(self.layer + d, self.plan.half)
        return jnp.where(self.forward, layer, self.plan.panels - 1 - layer)

    def far(self, q):
        half = self.plan.half
        return jnp.where(self.forward, half + q, half - 1 - q)

    def part(self, mine):
        pairs = self.plan.half // 2
        first = jnp.where(self.is_q == mine, pairs, 0)
        return [block for i in range(pairs) for block in (self.near(first + i), self.far(first + i))]


def call(kernel, out_shapes, operands, scratch=(), out_space=pltpu.HBM, flops=1):
    return pl.pallas_call(
        kernel,
        out_shape=list(out_shapes),
        in_specs=[HBM] * len(operands),
        out_specs=[pl.BlockSpec(memory_space=out_space)] * len(out_shapes),
        scratch_shapes=list(scratch),
        compiler_params=pltpu.CompilerParams(vmem_limit_bytes=VMEM_BYTES),
        cost_estimate=pl.CostEstimate(flops=flops, bytes_accessed=1, transcendentals=0),
    )(*operands)


def bf16(*shape):
    return jax.ShapeDtypeStruct(shape, jnp.bfloat16)


def band(ref, block, rows):
    start = block * rows
    return ref.at[pl.ds(start if isinstance(block, int) else pl.multiple_of(start, rows), rows), :]


class Copies:
    def __init__(self, sems):
        self.sems, self.count = sems, 0

    def start(self, pairs, condition=None):
        copies = [pltpu.make_async_copy(a, b, self.sems.at[self.count + i]) for i, (a, b) in enumerate(pairs)]
        self.count += len(copies)
        self._start(copies, condition)
        return copies

    def start_either(self, condition, pairs, other_pairs):
        first = self.count
        copies = self.start(pairs, condition)
        self.count = first
        self.start(other_pairs, jnp.logical_not(condition))
        return copies

    @staticmethod
    def _start(copies, condition):
        def run():
            for copy in copies:
                copy.start()

        run() if condition is None else pl.when(condition)(run)


def wait(copies):
    for copy in copies:
        copy.wait()


def full_pairs(place, mine, theirs, target):
    rows = target.shape[0] // place.plan.panels
    return [
        (band(half, i, rows), band(target, block, rows))
        for half, is_mine in ((mine, True), (theirs, False))
        for i, block in enumerate(place.part(is_mine))
    ]


class Raw:
    def __init__(self, place, refs):
        half = place.plan.half
        self.place = place
        self.near = {True: refs[:half], False: refs[half : 2 * half]}
        self.far = {True: refs[2 * half : 3 * half], False: refs[3 * half : 4 * half]}

    @staticmethod
    def take(plan, refs):
        return refs[: 4 * plan.half], refs[4 * plan.half :]

    def start(self, copies, of_q, index, target, far_index=None, only_half=False):
        place, half = self.place, self.place.plan.half
        rows = self.near[True][0].shape[1]

        def pairs(mine):
            on_q = of_q == mine
            result = []
            ds = range(half // 2 if on_q else 0, half if on_q else half // 2) if only_half else range(half)
            for i, d in enumerate(ds):
                near, far = (2 * i, 2 * i + 1) if only_half else (place.near(d), place.far(d))
                result.append((self.near[mine][d].at[index], band(target, near, rows)))
                far_ref = self.far[mine][d] if far_index is None else self.far[mine][d].at[far_index]
                result.append((far_ref, band(target, far, rows)))
            return result

        return copies.start_either(place.is_q if of_q else place.is_p, pairs(True), pairs(False))


def product(out, a, b, finish=lambda acc, rows: acc, b_transposed=False, tile=TILE):
    n = out.shape[0]
    tile = min(tile, n)
    dims = (((1,), (1 if b_transposed else 0,)), ((), ()))

    @pl.loop(0, n // tile)
    def _(i):
        rows = pl.ds(pl.multiple_of(i * tile, tile), tile)
        acc = lax.dot_general(a[rows, :], b[...], dims, preferred_element_type=jnp.float32)
        out[rows, :] = finish(acc, rows).astype(jnp.bfloat16)


def upper_rows(place, out, a, b):
    rows = a.shape[0] // place.plan.panels
    for i, block in enumerate(place.part(True)):
        columns = pl.ds(pl.multiple_of(block * rows, rows), rows)
        acc = lax.dot_general(a[:, columns], b[...], (((0,), (0,)), ((), ())), preferred_element_type=jnp.float32)
        out[i * rows : (i + 1) * rows, :] = acc.astype(jnp.bfloat16)


def identity(rows, n):
    shape = (rows.size, n)
    row = lax.broadcasted_iota(jnp.int32, shape, 0) + rows.start
    return (row == lax.broadcasted_iota(jnp.int32, shape, 1)).astype(jnp.float32)


def iterates(n, cp, jq, u, x1, r):
    def first_iterate(acc, rows):
        x1[rows, :] = (identity(rows, n) - acc.astype(jnp.bfloat16)).astype(jnp.bfloat16)
        return acc

    product(u, cp, jq, first_iterate, tile=n)
    product(r, u, x1, lambda acc, rows: identity(rows, n) + u[rows, :] - acc, tile=n)


def plus(ref):
    return lambda acc, rows: acc + ref[rows, :]


def combine_front(place, copies, stride, loads, stored, cp, jq, aq, ah, ch, x1, r, full, u, f):
    load_cp, load_jq, load_ah, load_aq, load_ch = loads
    usable = place.segment >= stride
    wait(load_cp + load_jq)
    pl.when(usable)(lambda: iterates(cp.shape[0], cp, jq, full, x1, r))
    stores = copies.start(list(zip((x1, r), stored)))
    wait(load_ah)

    @pl.when(usable)
    def _():
        product(u, ah, x1)
        product(f, u, r)

    stores += copies.start([(f, stored[2])])
    pl.when(usable)(lambda: product(u, f, cp))
    wait(load_aq + load_ch)
    pl.when(usable)(lambda: product(ch, u, aq, plus(ch), b_transposed=True))
    return stores


def first_kernel(plan, stride, *refs):
    pairs = plan.half // 2
    raw, refs = Raw.take(plan, refs)
    kept, late, refs = refs[:pairs], refs[pairs : 2 * pairs], refs[2 * pairs :]
    c_ref, jq_ref, x1_ref, r_ref, f_ref, cp, jq, aq, ah, ch, x1, r, full, u, f, sems = refs
    place, copies = Place(plan), Copies(sems)
    raw_c = Raw(place, [*raw[: 2 * plan.half], *late, *late, *kept, *late])
    raw = Raw(place, raw)
    loads = [
        raw.start(copies, False, 0, cp, 0),
        raw.start(copies, True, 2, jq, 0),
        raw.start(copies, True, 1, ah, 1, only_half=True),
        raw.start(copies, True, 1, aq, 1),
        raw_c.start(copies, True, 0, ch, only_half=True),
    ]
    stored = (x1_ref, r_ref, f_ref)
    stores = combine_front(place, copies, stride, loads, stored, cp, jq, aq, ah, ch, x1, r, full, u, f)
    wait(stores + copies.start([(ch, c_ref), (jq, jq_ref)]))


def trans_info_kernel(plan, stride, f_ref, jq_ref, x1_ref, r_ref, *refs):
    raw_first, refs = Raw.take(plan, refs)
    raw_a, refs = Raw.take(plan, refs)
    raw_j, refs = Raw.take(plan, refs)
    a_ref, j_ref, f, ap, jq, x1, r, ah, u, w, jh, sems = refs
    place, copies = Place(plan), Copies(sems)
    raw_first, raw_a, raw_j = Raw(place, raw_first), Raw(place, raw_a), Raw(place, raw_j)
    usable = place.segment >= stride
    rows = ap.shape[0] // plan.panels
    load_ap = raw_a.start(copies, False, 1, ap)
    load_f = copies.start([(f_ref, f)])
    load_jq = copies.start([(jq_ref, jq)])
    load_x1 = copies.start([(x1_ref, x1)])
    load_r = copies.start([(r_ref, r)])
    load_jh = raw_j.start(copies, False, 2, jh, only_half=True)
    load_ah = raw_first.start(copies, True, 1, ah, 1, only_half=True)
    wait(load_ap + load_f + load_ah)
    pl.when(usable)(lambda: product(ah, f, ap))
    store_a = copies.start([(ah, a_ref)])
    wait(load_jq)
    pl.when(usable)(lambda: upper_rows(place, u, ap, jq))
    wait(load_x1)
    pl.when(usable)(lambda: product(w, u, x1))
    wait(load_r + load_jh)

    @pl.when(usable)
    def _():
        product(u, w, r)
        product(jh, u, ap, plus(jh))

    @pl.when(jnp.logical_not(usable))
    def _():
        for i, block in enumerate(place.part(True)):
            jh[i * rows : (i + 1) * rows, :] = jq[pl.ds(pl.multiple_of(block * rows, rows), rows), :]

    wait(copies.start([(jh, j_ref)]) + store_a)


def store_blocks(plan, copies, result, far, near):
    pairs = plan.half // 2
    rows = result.shape[0] // plan.half
    parts = len(far) // pairs
    stores = [
        (result.at[pl.ds((2 * (k % pairs) + 1) * rows + k // pairs * (rows // parts), rows // parts), :], piece)
        for k, piece in enumerate(far)
    ]
    stores += [(result.at[pl.ds(2 * i * rows, rows), :], piece) for i, piece in enumerate(near)]
    return copies.start(stores)


def front_kernel(plan, stride, c_mine, c_theirs, j_mine, j_theirs, a_mine, a_theirs, cq_mine, *refs):
    far, near = refs[: plan.half], refs[plan.half : plan.half + plan.half // 2]
    f_ref, x1_ref, r_ref, cp, jq, aq, ah, ch, x1, r, full, u, f, sems = refs[-14:]
    place, copies = Place(plan), Copies(sems)
    loads = [
        copies.start(full_pairs(place, c_mine, c_theirs, cp)),
        copies.start(full_pairs(place, j_mine, j_theirs, jq)),
        copies.start([(a_mine, ah)]),
        copies.start(full_pairs(place, a_mine, a_theirs, aq)),
        copies.start([(cq_mine, ch)]),
    ]
    stored = (x1_ref, r_ref, f_ref)
    stores = combine_front(place, copies, stride, loads, stored, cp, jq, aq, ah, ch, x1, r, full, u, f)
    wait(store_blocks(plan, copies, ch, far, near) + stores)


def trans_kernel(plan, stride, a_mine, a_theirs, f_ref, aq_mine, *refs):
    pairs = plan.half // 2
    c_near, far, near, refs = refs[:pairs], refs[pairs : 2 * pairs], refs[2 * pairs : 3 * pairs], refs[3 * pairs :]
    ap, f, ah, c, sems = refs
    place, copies = Place(plan), Copies(sems)
    rows = ah.shape[0] // plan.half
    usable = place.segment >= stride
    loads = copies.start([(f_ref, f), (aq_mine, ah)]) + copies.start(full_pairs(place, a_mine, a_theirs, ap))
    c_blocks = [c.at[pl.ds(i * rows, rows), :] for i in range(pairs)]
    load_c = copies.start(list(zip(c_near, c_blocks)))
    wait(loads)
    pl.when(usable)(lambda: product(ah, f, ap))
    stores = store_blocks(plan, copies, ah, far, [x.at[1] for x in near])
    wait(load_c)
    wait(copies.start([(block, x.at[0]) for block, x in zip(c_blocks, near)]) + stores)


def upper_kernel(plan, stride, a_mine, a_theirs, j_mine, j_theirs, x1_ref, r_ref, h_ref, ap, jq, x1, r, u, w, sems):
    place, copies = Place(plan), Copies(sems)

    @pl.when(place.segment >= stride)
    def _():
        load_ap = copies.start(full_pairs(place, a_mine, a_theirs, ap))
        load_jq = copies.start(full_pairs(place, j_mine, j_theirs, jq))
        load_x1 = copies.start([(x1_ref, x1)])
        load_r = copies.start([(r_ref, r)])
        wait(load_ap + load_jq)
        upper_rows(place, u, ap, jq)
        wait(load_x1)
        product(w, u, x1)
        wait(load_r)
        product(u, w, r)
        wait(copies.start([(u, h_ref)]))


def info_kernel(plan, stride, h_ref, a_mine, a_theirs, jp_mine, jq_mine, *refs):
    pairs = plan.half // 2
    far, near = refs[:pairs], refs[pairs : 2 * pairs]
    h, ap, jh, sems = refs[-4:]
    place, copies = Place(plan), Copies(sems)
    usable = place.segment >= stride
    load_jh = copies.start_either(usable, [(jp_mine, jh)], [(jq_mine, jh)])
    wait(load_jh + copies.start([(h_ref, h)]) + copies.start(full_pairs(place, a_mine, a_theirs, ap)))
    pl.when(usable)(lambda: product(jh, h, ap, plus(jh)))
    wait(store_blocks(plan, copies, jh, far, near))


def home_kernel(plan, *refs):
    half, pairs = plan.half, plan.half // 2
    c_far, a_far, ca_near = refs[:half], refs[half : half + pairs], refs[half + pairs : 2 * half]
    j_far, j_near = refs[2 * half : 2 * half + pairs], refs[2 * half + pairs : 3 * half]
    f_out, b_out, sems = refs[3 * half :]
    rows = f_out.shape[1]
    t, z = lax.axis_index("tm"), lax.axis_index("panel")
    waits = []
    places = [(f_out, t, z), (b_out, plan.groups - 1 - t, plan.panels - 1 - z)]
    for out, segment, panel in places:
        distance = lax.rem(panel + half - lax.rem(segment, 2), half)
        which = jnp.where(panel >= half, lax.rem(panel, pairs), pairs + lax.rem(distance, pairs))
        first = len(waits)
        for i in range(pairs):
            halves = [out.at[0, pl.ds(k * (rows // 2), rows // 2), :] for k in range(2)]
            far = [(c_far[i], halves[0]), (c_far[pairs + i], halves[1]), (a_far[i], out.at[1]), (j_far[i], out.at[2])]
            near = [(ca_near[i].at[k], out.at[k]) for k in range(2)] + [(j_near[i], out.at[2])]
            for owner, moves in ((i, far), (pairs + i, near)):
                @pl.when(which == owner)
                def _():
                    for k, (source_ref, target) in enumerate(moves):
                        at = k - 1 if len(moves) == 4 and k > 0 else k
                        pltpu.make_async_copy(source_ref, target, sems.at[first + at]).start()
        for matrix in range(3):
            waits.append(pltpu.make_async_copy(j_far[0], out.at[matrix], sems.at[first + matrix]))
    wait(waits)


def after(x, *others):
    return lax.optimization_barrier((x, *others))[0]


def shards(plan, forward_element, backward_element):
    forward, backward = forward_element[:, 0], backward_element[:, 0]
    rows, n = forward.shape[1:]
    half = plan.half
    full, part, block = bf16(n, n), bf16(n // 2, n), bf16(rows, n)
    square, slab = pltpu.VMEM((n, n), jnp.bfloat16), pltpu.VMEM((n // 2, n), jnp.bfloat16)
    sems = pltpu.SemaphoreType.DMA((12 * half,))

    def send(x, routes):
        return lax.ppermute(x, AXES, routes)

    def swap(x):
        return send(x, plan.core)

    def kernel(body, outs, operands, scratch, **options):
        return call(functools.partial(body, plan, *options.pop("static", ())), outs, operands, [*scratch, sems], **options)

    t, z = lax.axis_index("tm"), lax.axis_index("panel")
    layer = jnp.where(z < half, z, plan.panels - 1 - z)
    core = jnp.where(z < half, t, plan.groups - 1 - t) % 2
    is_q, special = (core + layer) % 2 == 0, (core == 1) & (layer == 0)
    other_c = jnp.where(z < half, backward[0], forward[0])
    other_ja = jnp.stack([jnp.where(z < half, backward[i], forward[i]) for i in (2, 1)])
    forward, backward, _ = lax.optimization_barrier((forward, backward, other_ja))
    own = jnp.where(z < half, forward, backward)

    far_c = [send(other_c, route) for route in plan.cross]
    far_ja = [send(other_ja, route) for route in plan.cross]
    local = [send(own, plan.gather[d]) for d in range(1, half)]
    onward_local = send(after(own, *far_c), plan.onward)
    far_c_of_p = [send(x, plan.forward) for x in far_c]
    far_first = [jnp.where(is_q, q, p[None]) for q, p in zip(far_ja, far_c_of_p)]
    first_swap = [swap(x) for x in far_first]
    near = [jnp.where(special, onward_local, own), *local]
    near_swap = [swap(x) for x in near]
    nears = [*near, *near_swap]
    raw_first = [*nears, *far_first, *first_swap]
    kept_c = [swap(x) for x in far_c[: half // 2]]

    rest = [send(after(x, *far_c_of_p), plan.forward) for x in far_ja]

    c_new, jq, x1, r, f = kernel(
        first_kernel,
        [part, full, full, full, part],
        [*raw_first, *kept_c, *far_c[half // 2 :]],
        [square] * 3 + [slab] * 2 + [square] * 3 + [slab] * 2,
        static=(1,),
    )
    rest = [after(x, c_new) for x in rest]
    j_rest, a_rest = [x[0] for x in rest], [x[1] for x in rest]
    raw_rest = [*nears, *a_rest, *[swap(x) for x in a_rest], *nears, *j_rest, *[swap(x) for x in j_rest]]
    a_new, j_new = kernel(
        trans_info_kernel,
        [part] * 2,
        [after(f, c_new), jq, x1, r, *raw_first, *raw_rest],
        [slab] + [square] * 4 + [slab] * 4,
        static=(1,),
    )
    j_swap, a_swap = swap(j_new), swap(a_new)
    c_next = send(c_new, plan.next)
    c_next, a_new = lax.optimization_barrier((c_next, a_new))
    c_next_swap = swap(c_next)
    a_next = send(a_new, plan.next)

    pairs = range(half // 2)
    blocks = [block for _ in pairs]
    far, near = [plan.home[True, i] for i in pairs], [plan.home[False, i] for i in pairs]

    def send_home(pieces, routes):
        return [send(x, route) for x, route in zip(pieces, routes)]

    *c_pieces, f, x1, r = kernel(
        front_kernel,
        [*[bf16(rows // 2, n)] * half, *blocks, part, full, full],
        [c_next, c_next_swap, j_new, j_swap, a_new, a_swap, c_new],
        [square] * 3 + [slab] * 2 + [square] * 3 + [slab] * 2,
        static=(2,),
    )
    c_far, c_near = send_home(c_pieces[:half], far * 2), c_pieces[half:]
    j_next = send(after(j_new, a_next), plan.next)
    a_next = after(a_next, f, *c_far[: half // 2])
    a_next_swap = swap(a_next)
    a_pieces = kernel(
        trans_kernel,
        [*blocks, *[bf16(2, rows, n) for _ in pairs]],
        [a_next, after(a_next_swap, *c_far), f, a_new, *c_near],
        [square] + [slab] * 3,
        static=(2,),
    )
    a_far = send_home(a_pieces[: half // 2], far)
    ca_near = send_home(a_pieces[half // 2 :], near)
    (h,) = kernel(
        upper_kernel,
        [part],
        [a_next, a_next_swap, j_new, j_swap, after(x1, *a_pieces), r],
        [square] * 4 + [slab] * 2,
        static=(2,),
    )
    j_pieces = kernel(
        info_kernel,
        [*blocks, *blocks],
        [h, a_next, a_next_swap, after(j_next, h), j_new],
        [slab, square, slab],
        static=(2,),
    )
    j_home = send_home([after(x, *a_far, *ca_near) for x in j_pieces], [*far, *near])

    f_out, b_out = kernel(
        home_kernel,
        [bf16(3, rows, n)] * 2,
        [*c_far, *a_far, *ca_near, *j_home],
        [],
        out_space=pltpu.VMEM,
    )
    return f_out[:, None], b_out[:, None]


def solution(mesh):
    plan = Plan(mesh.shape["tm"], mesh.shape["panel"])
    spec = P(None, "tm", "panel", None)
    return jax.shard_map(
        functools.partial(shards, plan),
        mesh=mesh,
        in_specs=(spec, spec),
        out_specs=(spec, spec),
        check_vma=False,
    )
```

time: 654 us -> 253 us (0.39); the launches traced: 642 us -> 249 us
  waiting for transfers between devices: 426 us -> 114 us
  matrix products: 116 us -> 0 us
  Pallas kernels: 0 us -> 58.3 us
  local copies, waits for them, and re-layouts: 52.7 us -> 9.05 us
  starting transfers between devices: 22.4 us -> 57.3 us
  between operations: 14.5 us -> 1.21 us
    all_gather x4 -> x0, waiting for transfers between devices: 275 us -> none  [advance(): gathered = lax.all_gather(element, 'panel', axis=1, tiled=True)]
    dot_general x28 -> x0, matrix products: 116 us -> none  [the longest x24 98.8 us: matmul(): return jnp.dot(left, right, preferred_element_type=jnp.float32)]
    pallas_call x0 -> x7, Pallas kernels: none -> 58.3 us  [call(): pl.pallas_call(kernel, out_shape=list(out_shapes), in_specs=[HBM] * len(o...]
    slice x12 -> x0, local copies, waits for them, and re-layouts: 44 us -> none  [the longest x4 18.4 us: advance(): shifted = passed_along(gathered[:2], 'tm', stride)]
    ppermute x8 -> x32, waiting for transfers between devices: 150 us -> 114 us  [send(): return lax.ppermute(x, AXES, routes)]
    ppermute x8 -> x32, starting transfers between devices: 22.2 us -> 57.3 us  [send(): return lax.ppermute(x, AXES, routes)]
  transfers between devices with their start and end apart: 12 -> 32, of which waited for: 7 -> 16; matrix products, arithmetic and copies ran while one was open for 26% -> 4% of each run, Pallas kernels for 0% -> 22%
where the time goes in v3:
time: 253 us; the launch traced here: 249 us
  waiting for transfers between devices  114 us (45%)
  Pallas kernels  58.3 us (23%)
  starting transfers between devices  57.3 us (23%)
  local copies, waits for them, and re-layouts  9.05 us (4%)
  other arithmetic  8.87 us (4%)
    ppermute x32, waiting for transfers between devices, send(): return lax.ppermute(x, AXES, routes)  114 us
    pallas_call x7, Pallas kernels, call(): pl.pallas_call(kernel, out_shape=list(out_shapes), in_specs=[HBM] * len(o...  58.3 us
    ppermute x32, starting transfers between devices, send(): return lax.ppermute(x, AXES, routes)  57.3 us
    unnamed x56, local copies, waits for them, and re-layouts  6.51 us
  transfers between devices with their start and end apart: 32, of which 16 were waited for; matrix products, arithmetic and copies ran while one was open for 4% of the time, Pallas kernels for 22%

profile of v3, /device:TPU:10, one launch (start us, length us, event | category | flops | bytes accessed | tf_op | source)
XLA Modules:
  0.0 249.2 jit_solution(9605791460025296272)
XLA Ops:
  0.6 2.1 select_bitcast_fusion
  3.6 4.9 %collective-permute-start = (bf16[256,1024]{1,0:T(8,128)(2,1)S(1)}, bf16[256,1024]{1,0:T(8,128)(2,1)}, u32[]{:S(2)}, u32[]{:S(2)}) collective-permute-start(bf16[256,1024]{1,0:T(8,128)(2,1)S(1)} %get-tuple-element.76), channel_id=1, source_target_pairs={{2,0},{6,5},{10,8},{14,13},{18,16},{22,21},{26,24},{30,29},{29,31}... | collective-permute-start | bytes 1572872 | tf_op jit(solution)/shard_map/ppermute | solution.py:404
  8.5 1.1 pad_maximum_fusion
  9.6 1.3 broadcast_select_fusion
  10.9 2.6 %collective-permute-start.3 = (bf16[3,256,1024]{2,1,0:T(8,128)(2,1)}, bf16[3,256,1024]{2,1,0:T(8,128)(2,1)S(1)}, u32[]{:S(2)}, u32[]{:S(2)}) collective-permute-start(bf16[3,256,1024]{2,1,0:T(8,128)(2,1)} %broadcast_select_fusion), channel_id=1, source_target_pairs={{1,0},{4,5},{9,8},{12,13},{17,16},{20,21},{25,24},{28,29},{0,1},{5... | collective-permute-start | bytes 4718600 | tf_op jit(solution)/shard_map/ppermute | solution.py:404
  13.5 17.2 %collective-permute-done = bf16[256,1024]{1,0:T(8,128)(2,1)} collective-permute-done((bf16[256,1024]{1,0:T(8,128)(2,1)S(1)}, bf16[256,1024]{1,0:T(8,128)(2,1)}, u32[]{:S(2)}, u32[]{:S(2)}) %collective-permute-start) | collective-permute-done | bytes 524320 | tf_op jit(solution)/shard_map/ppermute | solution.py:404
  30.7 1.8 collective-permute-start.2
  32.5 1.6 collective-permute-start.8
  34.1 1.3 collective-permute-start.9
  35.4 9.2 %collective-permute-start.6 = (bf16[2,256,1024]{2,1,0:T(8,128)(2,1)}, bf16[2,256,1024]{2,1,0:T(8,128)(2,1)}, u32[]{:S(2)}, u32[]{:S(2)}) collective-permute-start(bf16[2,256,1024]{2,1,0:T(8,128)(2,1)} %pad_maximum_fusion), channel_id=1, source_target_pairs={{2,0},{6,5},{10,8},{14,13},{18,16},{22,21},{26,24},{30,29},{29,31}... | collective-permute-start | bytes 3145736 | tf_op jit(solution)/shard_map/ppermute | solution.py:404
  44.6 37.8 %collective-permute-done.9 = bf16[256,1024]{1,0:T(8,128)(2,1)S(1)} collective-permute-done((bf16[256,1024]{1,0:T(8,128)(2,1)S(1)}, bf16[256,1024]{1,0:T(8,128)(2,1)S(1)}, u32[]{:S(2)}, u32[]{:S(2)}) %collective-permute-start.9) | collective-permute-done | bytes 524320 | tf_op jit(solution)/shard_map/ppermute | solution.py:404
  82.4 1.3 collective-permute-start.7
  83.7 1.1 broadcast_select_fusion.2.refs_5_
  84.8 5.8 %collective-permute-start.11 = (bf16[2,256,1024]{2,1,0:T(8,128)(2,1)}, bf16[2,256,1024]{2,1,0:T(8,128)(2,1)}, u32[]{:S(2)}, u32[]{:S(2)}) collective-permute-start(bf16[2,256,1024]{2,1,0:T(8,128)(2,1)} %broadcast_select_fusion.2.refs_5_), channel_id=1, source_target_pairs={{0,4},{1,5},{2,6},{3,7},{4,0},{5,1},{6,2},{7,3},{8,12},{9,13},{10,... | collective-permute-start | bytes 3145736 | tf_op jit(solution)/shard_map/ppermute | solution.py:404
  90.7 2.1 broadcast_select_fusion.1.refs_0_.refs_8_.refs_16_
  92.9 0.9 collective-permute-done.7
  93.9 1.2 broadcast_select_fusion.3.refs_4_
  95.8 1.1 collective-permute-done.12.refs_8_
  96.9 1.3 collective-permute-start.15
  98.2 1.3 collective-permute-start.14
  99.7 1.0 copy-done.10
  100.7 1.2 copy-done.2
  101.8 13.5 %shard_map.41 = (bf16[512,1024]{1,0:T(8,128)(2,1)}, bf16[1024,1024]{1,0:T(8,128)(2,1)}, bf16[1024,1024]{1,0:T(8,128)(2,1)}, bf16[1024,1024]{1,0:T(8,128)(2,1)}, bf16[512,1024]{1,0:T(8,128)(2,1)}) custom-call(bf16[3,256,1024]{2,1,0:T(8,128)(2,1)} %copy-done, bf16[3,256,1024]{2,1,0:T(8,128)(2,1)} %copy-done.1, ...), custom_call_target="tpu_custom_call" | custom-call | flops 1 | bytes 1 | tf_op jit(solution)/shard_map/pallas_call | solution.py:82
  115.4 2.3 collective-permute-start.13
  117.6 7.5 %collective-permute-done.14 = bf16[2,256,1024]{2,1,0:T(8,128)(2,1)} collective-permute-done((bf16[2,256,1024]{2,1,0:T(8,128)(2,1)}, bf16[2,256,1024]{2,1,0:T(8,128)(2,1)}, u32[]{:S(2)}, u32[]{:S(2)}) %collective-permute-start.14) | collective-permute-done | bytes 1048608 | tf_op jit(solution)/shard_map/ppermute | solution.py:404
  125.1 1.3 slice_bitcast_fusion.1
  127.0 1.3 slice_bitcast_fusion
  129.1 1.1 collective-permute-done.19.refs_23_
  131.8 11.9 %shard_map.42 = (bf16[512,1024]{1,0:T(8,128)(2,1)}, bf16[512,1024]{1,0:T(8,128)(2,1)}) custom-call(bf16[512,1024]{1,0:T(8,128)(2,1)} %get-tuple-element.43.f_ref, bf16[1024,1024]{1,0:T(8,128)(2,1)} %get-tuple-element.44.jq_ref, bf16[1024,1024]{1,0:T(8,128)(2,1)} %get-tuple-element.45.x1_ref, bf16[1024,1024]{1,0:T(8,128)(2,1)} %get-tuple-element.46.r_ref, ...), custom_call_target="tpu_custom_call" | custom-call | flops 1 | bytes 1 | tf_op jit(solution)/shard_map/pallas_call | solution.py:82
  144.4 2.6 %collective-permute-start.25 = (bf16[512,1024]{1,0:T(8,128)(2,1)}, bf16[512,1024]{1,0:T(8,128)(2,1)S(1)}, u32[]{:S(2)}, u32[]{:S(2)}) collective-permute-start(bf16[512,1024]{1,0:T(8,128)(2,1)} %get-tuple-element.54.a_mine.aq_mine), channel_id=1, source_target_pairs={{0,8},{1,9},{4,12},{5,13},{8,16},{9,17},{12,20},{13,21},{16,24},{1... | collective-permute-start | bytes 3145736 | tf_op jit(solution)/shard_map/ppermute | solution.py:404
  147.0 2.7 %collective-permute-done.21.j_theirs = bf16[512,1024]{1,0:T(8,128)(2,1)S(1)} collective-permute-done((bf16[512,1024]{1,0:T(8,128)(2,1)}, bf16[512,1024]{1,0:T(8,128)(2,1)S(1)}, u32[]{:S(2)}, u32[]{:S(2)}) %collective-permute-start.21) | collective-permute-done | bytes 1048608 | tf_op jit(solution)/shard_map/ppermute | solution.py:404
  149.8 0.8 copy-done.9
  150.6 12.8 %shard_map.43 = (bf16[128,1024]{1,0:T(8,128)(2,1)}, bf16[128,1024]{1,0:T(8,128)(2,1)}, bf16[256,1024]{1,0:T(8,128)(2,1)}, bf16[512,1024]{1,0:T(8,128)(2,1)}, bf1...) custom-call(bf16[512,1024]{1,0:T(8,128)(2,1)} %collective-permute-done.13.c_mine, ...), custom_call_target="tpu_custom_call" | custom-call | flops 1 | bytes 1 | tf_op jit(solution)/shard_map/pallas_call | solution.py:82
  163.5 8.5 %collective-permute-done.25.a_mine = bf16[512,1024]{1,0:T(8,128)(2,1)S(1)} collective-permute-done((bf16[512,1024]{1,0:T(8,128)(2,1)}, bf16[512,1024]{1,0:T(8,128)(2,1)S(1)}, u32[]{:S(2)}, u32[]{:S(2)}) %collective-permute-start.25) | collective-permute-done | bytes 1048608 | tf_op jit(solution)/shard_map/ppermute | solution.py:404
  172.0 5.7 %collective-permute-start.26 = (bf16[512,1024]{1,0:T(8,128)(2,1)S(1)}, bf16[512,1024]{1,0:T(8,128)(2,1)S(1)}, u32[]{:S(2)}, u32[]{:S(2)}) collective-permute-start(bf16[512,1024]{1,0:T(8,128)(2,1)S(1)} %collective-permute-done.25.a_mine), channel_id=1, source_target_pairs={{0,4},{1,5},{2,6},{3,7},{4,0},{5,1},{6,2},{7,3},{8,12},{9,13},{10,... | collective-permute-start | bytes 3145736 | tf_op jit(solution)/shard_map/ppermute | solution.py:404
  178.3 3.8 %collective-permute-start.29 = (bf16[512,1024]{1,0:T(8,128)(2,1)S(1)}, bf16[512,1024]{1,0:T(8,128)(2,1)}, u32[]{:S(2)}, u32[]{:S(2)}) collective-permute-start(bf16[512,1024]{1,0:T(8,128)(2,1)S(1)} %copy-done.3), channel_id=1, source_target_pairs={{0,8},{1,9},{4,12},{5,13},{8,16},{9,17},{12,20},{13,21},{16,24},{1... | collective-permute-start | bytes 3145736 | tf_op jit(solution)/shard_map/ppermute | solution.py:404
  182.1 8.0 %collective-permute-done.24.refs_1_ = bf16[128,1024]{1,0:T(8,128)(2,1)S(1)} collective-permute-done((bf16[128,1024]{1,0:T(8,128)(2,1)}, bf16[128,1024]{1,0:T(8,128)(2,1)S(1)}, u32[]{:S(2)}, u32[]{:S(2)}) %collective-permute-start.24) | collective-permute-done | bytes 262176 | tf_op jit(solution)/shard_map/ppermute | solution.py:404
  190.1 1.0 copy-done.5
  191.1 4.8 %shard_map.44 = (bf16[256,1024]{1,0:T(8,128)(2,1)}, bf16[2,256,1024]{2,1,0:T(8,128)(2,1)}) custom-call(bf16[512,1024]{1,0:T(8,128)(2,1)} %copy-done.4, bf16[512,1024]{1,0:T(8,128)(2,1)} %copy-done.5, bf16[512,1024]{1,0:T(8,128)(2,1)} %get-tuple-element.57.f_ref, bf16[512,1024]{1,0:T(8,128)(2,1)} %get-tuple-element.54.a_mine.aq_mine, ...), custom_call_target="tpu_custom_call" | custom-call | flops 1 | bytes 1 | tf_op jit(solution)/shard_map/pallas_call | solution.py:82
  195.9 1.1 collective-permute-start.28
  196.9 1.0 collective-permute-start.27
  198.0 7.2 %shard_map.45.h_ref = bf16[512,1024]{1,0:T(8,128)(2,1)} custom-call(bf16[512,1024]{1,0:T(8,128)(2,1)} %copy-done.4, bf16[512,1024]{1,0:T(8,128)(2,1)} %copy-done.5, bf16[512,1024]{1,0:T(8,128)(2,1)} %get-tuple-element.66.j_mine.jq_mine, bf16[512,1024]{1,0:T(8,128)(2,1)} %copy-done.9, bf16[1024,1024]{1,0:T(8,128)(2,1)} %get-tuple-element.64.x1_ref, ...), custom_call_target="tpu_custom_call" | custom-call | flops 1 | bytes 1 | tf_op jit(solution)/shard_map/pallas_call | solution.py:82
  205.2 4.6 %shard_map.46 = (bf16[256,1024]{1,0:T(8,128)(2,1)}, bf16[256,1024]{1,0:T(8,128)(2,1)}) custom-call(bf16[512,1024]{1,0:T(8,128)(2,1)} %shard_map.45.h_ref, bf16[512,1024]{1,0:T(8,128)(2,1)} %copy-done.4, bf16[512,1024]{1,0:T(8,128)(2,1)} %copy-done.5, bf16[512,1024]{1,0:T(8,128)(2,1)} %collective-permute-done.29.jp_mine, ...), custom_call_target="tpu_custom_call" | custom-call | flops 1 | bytes 1 | tf_op jit(solution)/shard_map/pallas_call | solution.py:82
  209.8 5.4 %collective-permute-done.27.refs_2_ = bf16[256,1024]{1,0:T(8,128)(2,1)S(1)} collective-permute-done((bf16[256,1024]{1,0:T(8,128)(2,1)}, bf16[256,1024]{1,0:T(8,128)(2,1)S(1)}, u32[]{:S(2)}, u32[]{:S(2)}) %collective-permute-start.27) | collective-permute-done | bytes 524320 | tf_op jit(solution)/shard_map/ppermute | solution.py:404
  215.1 2.7 %collective-permute-done.28.refs_3_ = bf16[2,256,1024]{2,1,0:T(8,128)(2,1)S(1)} collective-permute-done((bf16[2,256,1024]{2,1,0:T(8,128)(2,1)}, bf16[2,256,1024]{2,1,0:T(8,128)(2,1)S(1)}, u32[]{:S(2)}, u32[]{:S(2)}) %collective-permute-start.28) | collective-permute-done | bytes 1048608 | tf_op jit(solution)/shard_map/ppermute | solution.py:404
  218.2 5.2 %collective-permute-start.31 = (bf16[256,1024]{1,0:T(8,128)(2,1)}, bf16[256,1024]{1,0:T(8,128)(2,1)S(1)}, u32[]{:S(2)}, u32[]{:S(2)}) collective-permute-start(bf16[256,1024]{1,0:T(8,128)(2,1)} %get-tuple-element.71), channel_id=1, source_target_pairs={{0,1},{1,5},{4,0},{5,4},{8,9},{9,13},{12,8},{13,12},{16,17},{17,21... | collective-permute-start | bytes 1572872 | tf_op jit(solution)/shard_map/ppermute | solution.py:404
  223.4 20.3 %collective-permute-done.30.refs_4_ = bf16[256,1024]{1,0:T(8,128)(2,1)S(1)} collective-permute-done((bf16[256,1024]{1,0:T(8,128)(2,1)}, bf16[256,1024]{1,0:T(8,128)(2,1)S(1)}, u32[]{:S(2)}, u32[]{:S(2)}) %collective-permute-start.30) | collective-permute-done | bytes 524320 | tf_op jit(solution)/shard_map/ppermute | solution.py:404
  245.3 3.7 %shard_map.47 = (bf16[3,256,1024]{2,1,0:T(8,128)(2,1)}, bf16[3,256,1024]{2,1,0:T(8,128)(2,1)}) custom-call(bf16[128,1024]{1,0:T(8,128)(2,1)} %copy-done.26, bf16[128,1024]{1,0:T(8,128)(2,1)} %copy-done.27, bf16[256,1024]{1,0:T(8,128)(2,1)} %copy-done.23, bf16[2,256,1024]{2,1,0:T(8,128)(2,1)} %copy-done.15, bf16[256,1024]{1,0:T(8,128)(2,1)} %copy-done.24, ...), custom_call_target="tpu_custom_call" | custom-call | flops 1 | bytes 1 | tf_op jit(solution)/shard_map/pallas_call | solution.py:82
  (87 shorter events, 8.6 us)
Async XLA Ops:
  0.6 8.9 %copy-start.8 = (bf16[3,1,256,1024]{3,2,1,0:T(8,128)(2,1)S(1)}, bf16[3,1,256,1024]{3,2,1,0:T(8,128)(2,1)}, u32[]{:S(2)}) copy-start(bf16[3,1,256,1024]{3,2,1,0:T(8,128)(2,1)} %param.3) | copy-start | bytes 4718596
  2.8 6.8 %copy-start.7 = (bf16[3,1,256,1024]{3,2,1,0:T(8,128)(2,1)S(1)}, bf16[3,1,256,1024]{3,2,1,0:T(8,128)(2,1)}, u32[]{:S(2)}) copy-start(bf16[3,1,256,1024]{3,2,1,0:T(8,128)(2,1)} %param.2) | copy-start | bytes 4718596
  2.8 10.7 %collective-permute-start.1 = (bf16[256,1024]{1,0:T(8,128)(2,1)S(1)}, bf16[256,1024]{1,0:T(8,128)(2,1)S(1)}, u32[]{:S(2)}, u32[]{:S(2)}) collective-permute-start(bf16[256,1024]{1,0:T(8,128)(2,1)S(1)} %get-tuple-element.76), channel_id=1, source_target_pairs={{3,0},{7,5},{11,8},{15,13},{19,16},{23,21},{27,24},{31,29},{28,31}... | collective-permute-start | bytes 1572872 | tf_op jit(solution)/shard_map/ppermute | solution.py:404
  3.6 27.0 %collective-permute-start = (bf16[256,1024]{1,0:T(8,128)(2,1)S(1)}, bf16[256,1024]{1,0:T(8,128)(2,1)}, u32[]{:S(2)}, u32[]{:S(2)}) collective-permute-start(bf16[256,1024]{1,0:T(8,128)(2,1)S(1)} %get-tuple-element.76), channel_id=1, source_target_pairs={{2,0},{6,5},{10,8},{14,13},{18,16},{22,21},{26,24},{30,29},{29,31}... | collective-permute-start | bytes 1572872 | tf_op jit(solution)/shard_map/ppermute | solution.py:404
  10.9 79.7 %collective-permute-start.3 = (bf16[3,256,1024]{2,1,0:T(8,128)(2,1)}, bf16[3,256,1024]{2,1,0:T(8,128)(2,1)S(1)}, u32[]{:S(2)}, u32[]{:S(2)}) collective-permute-start(bf16[3,256,1024]{2,1,0:T(8,128)(2,1)} %broadcast_select_fusion), channel_id=1, source_target_pairs={{1,0},{4,5},{9,8},{12,13},{17,16},{20,21},{25,24},{28,29},{0,1},{5... | collective-permute-start | bytes 4718600 | tf_op jit(solution)/shard_map/ppermute | solution.py:404
  13.5 77.2 %copy-start.21 = (bf16[256,1024]{1,0:T(8,128)(2,1)}, bf16[256,1024]{1,0:T(8,128)(2,1)S(1)}, u32[]{:S(2)}) copy-start(bf16[256,1024]{1,0:T(8,128)(2,1)S(1)} %collective-permute-done.1.refs_9_) | copy-start | bytes 1572868
  30.7 60.0 %collective-permute-start.2 = (bf16[3,256,1024]{2,1,0:T(8,128)(2,1)}, bf16[3,256,1024]{2,1,0:T(8,128)(2,1)}, u32[]{:S(2)}, u32[]{:S(2)}) collective-permute-start(bf16[3,256,1024]{2,1,0:T(8,128)(2,1)} %broadcast_select_fusion), channel_id=1, source_target_pairs={{4,12},{12,20},{20,28},{27,19},{19,11},{11,3}} | collective-permute-start | bytes 4718600 | tf_op jit(solution)/shard_map/ppermute | solution.py:404
  32.5 51.2 %collective-permute-start.8 = (bf16[2,256,1024]{2,1,0:T(8,128)(2,1)}, bf16[2,256,1024]{2,1,0:T(8,128)(2,1)}, u32[]{:S(2)}, u32[]{:S(2)}) collective-permute-start(bf16[2,256,1024]{2,1,0:T(8,128)(2,1)} %pad_maximum_fusion), channel_id=1, source_target_pairs={{3,0},{7,5},{11,8},{15,13},{19,16},{23,21},{27,24},{31,29},{28,31}... | collective-permute-start | bytes 3145736 | tf_op jit(solution)/shard_map/ppermute | solution.py:404
  34.1 48.3 %collective-permute-start.9 = (bf16[256,1024]{1,0:T(8,128)(2,1)S(1)}, bf16[256,1024]{1,0:T(8,128)(2,1)S(1)}, u32[]{:S(2)}, u32[]{:S(2)}) collective-permute-start(bf16[256,1024]{1,0:T(8,128)(2,1)S(1)} %collective-permute-done.1.refs_9_), channel_id=1, source_target_pairs={{0,1},{5,12},{8,9},{13,20},{16,17},{21,28},{24,25},{31,30},{26,19}... | collective-permute-start | bytes 1572872 | tf_op jit(solution)/shard_map/ppermute | solution.py:404
  35.4 58.5 %collective-permute-start.6 = (bf16[2,256,1024]{2,1,0:T(8,128)(2,1)}, bf16[2,256,1024]{2,1,0:T(8,128)(2,1)}, u32[]{:S(2)}, u32[]{:S(2)}) collective-permute-start(bf16[2,256,1024]{2,1,0:T(8,128)(2,1)} %pad_maximum_fusion), channel_id=1, source_target_pairs={{2,0},{6,5},{10,8},{14,13},{18,16},{22,21},{26,24},{30,29},{29,31}... | collective-permute-start | bytes 3145736 | tf_op jit(solution)/shard_map/ppermute | solution.py:404
  82.4 11.4 %collective-permute-start.7 = (bf16[256,1024]{1,0:T(8,128)(2,1)}, bf16[256,1024]{1,0:T(8,128)(2,1)}, u32[]{:S(2)}, u32[]{:S(2)}) collective-permute-start(bf16[256,1024]{1,0:T(8,128)(2,1)} %collective-permute-done), channel_id=1, source_target_pairs={{0,1},{5,12},{8,9},{13,20},{16,17},{21,28},{24,25},{31,30},{26,19}... | collective-permute-start | bytes 1572872 | tf_op jit(solution)/shard_map/ppermute | solution.py:404
  84.8 13.4 %collective-permute-start.11 = (bf16[2,256,1024]{2,1,0:T(8,128)(2,1)}, bf16[2,256,1024]{2,1,0:T(8,128)(2,1)}, u32[]{:S(2)}, u32[]{:S(2)}) collective-permute-start(bf16[2,256,1024]{2,1,0:T(8,128)(2,1)} %broadcast_select_fusion.2.refs_5_), channel_id=1, source_target_pairs={{0,4},{1,5},{2,6},{3,7},{4,0},{5,1},{6,2},{7,3},{8,12},{9,13},{10,... | collective-permute-start | bytes 3145736 | tf_op jit(solution)/shard_map/ppermute | solution.py:404
  90.6 9.0 %collective-permute-start.5 = (bf16[3,256,1024]{2,1,0:T(8,128)(2,1)S(1)}, bf16[3,256,1024]{2,1,0:T(8,128)(2,1)S(1)}, u32[]{:S(2)}, u32[]{:S(2)}) collective-permute-start(bf16[3,256,1024]{2,1,0:T(8,128)(2,1)S(1)} %collective-permute-done.3.refs_1_.refs_9_.refs_17_), channel_id=1, source_target_pairs={{0,4},{1,5},{2,6},{3,7},{4,0},{5,1},{6,2},{7,3},{8,12},{9,13},{10,... | collective-permute-start | bytes 4718600 | tf_op jit(solution)/shard_map/ppermute | solution.py:404
  92.8 9.0 %copy-start = (bf16[3,256,1024]{2,1,0:T(8,128)(2,1)}, bf16[3,256,1024]{2,1,0:T(8,128)(2,1)S(1)}, u32[]{:S(2)}) copy-start(bf16[3,256,1024]{2,1,0:T(8,128)(2,1)S(1)} %broadcast_select_fusion.1.refs_0_.refs_8_.refs_16_) | copy-start | bytes 4718596
  92.8 9.0 %collective-permute-start.4 = (bf16[3,256,1024]{2,1,0:T(8,128)(2,1)S(1)}, bf16[3,256,1024]{2,1,0:T(8,128)(2,1)}, u32[]{:S(2)}, u32[]{:S(2)}) collective-permute-start(bf16[3,256,1024]{2,1,0:T(8,128)(2,1)S(1)} %broadcast_select_fusion.1.refs_0_.refs_8_.refs_16_), channel_id=1, source_target_pairs={{0,4},{1,5},{2,6},{3,7},{4,0},{5,1},{6,2},{7,3},{8,12},{9,13},{10,... | collective-permute-start | bytes 4718600 | tf_op jit(solution)/shard_map/ppermute | solution.py:404
  93.8 3.1 %collective-permute-start.12 = (bf16[256,1024]{1,0:T(8,128)(2,1)}, bf16[256,1024]{1,0:T(8,128)(2,1)S(1)}, u32[]{:S(2)}, u32[]{:S(2)}) collective-permute-start(bf16[256,1024]{1,0:T(8,128)(2,1)} %collective-permute-done), channel_id=1, source_target_pairs={{0,4},{1,5},{2,6},{3,7},{4,0},{5,1},{6,2},{7,3},{8,12},{9,13},{10,... | collective-permute-start | bytes 1572872 | tf_op jit(solution)/shard_map/ppermute | solution.py:404
  95.0 4.6 %copy-start.6 = (bf16[2,256,1024]{2,1,0:T(8,128)(2,1)}, bf16[2,256,1024]{2,1,0:T(8,128)(2,1)S(1)}, u32[]{:S(2)}) copy-start(bf16[2,256,1024]{2,1,0:T(8,128)(2,1)S(1)} %broadcast_select_fusion.3.refs_4_) | copy-start | bytes 3145732
  95.1 4.6 %collective-permute-start.10 = (bf16[2,256,1024]{2,1,0:T(8,128)(2,1)S(1)}, bf16[2,256,1024]{2,1,0:T(8,128)(2,1)S(1)}, u32[]{:S(2)}, u32[]{:S(2)}) collective-permute-start(bf16[2,256,1024]{2,1,0:T(8,128)(2,1)S(1)} %broadcast_select_fusion.3.refs_4_), channel_id=1, source_target_pairs={{0,4},{1,5},{2,6},{3,7},{4,0},{5,1},{6,2},{7,3},{8,12},{9,13},{10,... | collective-permute-start | bytes 3145736 | tf_op jit(solution)/shard_map/ppermute | solution.py:404
  96.9 5.0 %copy-start.22 = (bf16[256,1024]{1,0:T(8,128)(2,1)}, bf16[256,1024]{1,0:T(8,128)(2,1)S(1)}, u32[]{:S(2)}) copy-start(bf16[256,1024]{1,0:T(8,128)(2,1)S(1)} %collective-permute-done.12.refs_8_) | copy-start | bytes 1572868
  96.9 20.8 %collective-permute-start.15 = (bf16[2,256,1024]{2,1,0:T(8,128)(2,1)}, bf16[2,256,1024]{2,1,0:T(8,128)(2,1)}, u32[]{:S(2)}, u32[]{:S(2)}) collective-permute-start(bf16[2,256,1024]{2,1,0:T(8,128)(2,1)} %collective-permute-done.8), channel_id=1, source_target_pairs={{0,1},{5,12},{8,9},{13,20},{16,17},{21,28},{24,25},{31,30},{26,19}... | collective-permute-start | bytes 3145736 | tf_op jit(solution)/shard_map/ppermute | solution.py:404
  98.2 26.9 %collective-permute-start.14 = (bf16[2,256,1024]{2,1,0:T(8,128)(2,1)}, bf16[2,256,1024]{2,1,0:T(8,128)(2,1)}, u32[]{:S(2)}, u32[]{:S(2)}) collective-permute-start(bf16[2,256,1024]{2,1,0:T(8,128)(2,1)} %collective-permute-done.6), channel_id=1, source_target_pairs={{0,1},{5,12},{8,9},{13,20},{16,17},{21,28},{24,25},{31,30},{26,19}... | collective-permute-start | bytes 3145736 | tf_op jit(solution)/shard_map/ppermute | solution.py:404
  115.4 29.0 %collective-permute-start.13 = (bf16[512,1024]{1,0:T(8,128)(2,1)}, bf16[512,1024]{1,0:T(8,128)(2,1)}, u32[]{:S(2)}, u32[]{:S(2)}) collective-permute-start(bf16[512,1024]{1,0:T(8,128)(2,1)} %get-tuple-element.41.cq_mine), channel_id=1, source_target_pairs={{0,8},{1,9},{4,12},{5,13},{8,16},{9,17},{12,20},{13,21},{16,24},{1... | collective-permute-start | bytes 3145736 | tf_op jit(solution)/shard_map/ppermute | solution.py:404
  126.4 5.4 %copy-start.11 = (bf16[256,1024]{1,0:T(8,128)(2,1)}, bf16[256,1024]{1,0:T(8,128)(2,1)S(1)}, u32[]{:S(2)}) copy-start(bf16[256,1024]{1,0:T(8,128)(2,1)S(1)} %get-tuple-element.81.refs_20_) | copy-start | bytes 1572868
  126.4 5.4 %copy-start.12 = (bf16[256,1024]{1,0:T(8,128)(2,1)}, bf16[256,1024]{1,0:T(8,128)(2,1)S(1)}, u32[]{:S(2)}) copy-start(bf16[256,1024]{1,0:T(8,128)(2,1)S(1)} %get-tuple-element.82.refs_12_) | copy-start | bytes 1572868
  126.4 2.4 collective-permute-start.18
  126.5 2.6 %collective-permute-start.16 = (bf16[256,1024]{1,0:T(8,128)(2,1)S(1)}, bf16[256,1024]{1,0:T(8,128)(2,1)S(1)}, u32[]{:S(2)}, u32[]{:S(2)}) collective-permute-start(bf16[256,1024]{1,0:T(8,128)(2,1)S(1)} %get-tuple-element.82.refs_12_), channel_id=1, source_target_pairs={{0,4},{1,5},{2,6},{3,7},{4,0},{5,1},{6,2},{7,3},{8,12},{9,13},{10,... | collective-permute-start | bytes 1572872 | tf_op jit(solution)/shard_map/ppermute | solution.py:404
  128.2 3.6 %copy-start.13 = (bf16[256,1024]{1,0:T(8,128)(2,1)}, bf16[256,1024]{1,0:T(8,128)(2,1)S(1)}, u32[]{:S(2)}) copy-start(bf16[256,1024]{1,0:T(8,128)(2,1)S(1)} %get-tuple-element.79.refs_21_) | copy-start | bytes 1572868
  128.3 3.6 %copy-start.14 = (bf16[256,1024]{1,0:T(8,128)(2,1)}, bf16[256,1024]{1,0:T(8,128)(2,1)S(1)}, u32[]{:S(2)}) copy-start(bf16[256,1024]{1,0:T(8,128)(2,1)S(1)} %get-tuple-element.80.refs_13_) | copy-start | bytes 1572868
  128.3 2.0 collective-permute-start.19
  128.4 2.6 %collective-permute-start.17 = (bf16[256,1024]{1,0:T(8,128)(2,1)S(1)}, bf16[256,1024]{1,0:T(8,128)(2,1)S(1)}, u32[]{:S(2)}, u32[]{:S(2)}) collective-permute-start(bf16[256,1024]{1,0:T(8,128)(2,1)S(1)} %get-tuple-element.80.refs_13_), channel_id=1, source_target_pairs={{0,4},{1,5},{2,6},{3,7},{4,0},{5,1},{6,2},{7,3},{8,12},{9,13},{10,... | collective-permute-start | bytes 1572872 | tf_op jit(solution)/shard_map/ppermute | solution.py:404
  143.7 3.3 %collective-permute-start.22 = (bf16[512,1024]{1,0:T(8,128)(2,1)}, bf16[512,1024]{1,0:T(8,128)(2,1)S(1)}, u32[]{:S(2)}, u32[]{:S(2)}) collective-permute-start(bf16[512,1024]{1,0:T(8,128)(2,1)} %get-tuple-element.54.a_mine.aq_mine), channel_id=1, source_target_pairs={{0,4},{1,5},{2,6},{3,7},{4,0},{5,1},{6,2},{7,3},{8,12},{9,13},{10,... | collective-permute-start | bytes 3145736 | tf_op jit(solution)/shard_map/ppermute | solution.py:404
  143.9 34.4 %copy-start.3 = (bf16[512,1024]{1,0:T(8,128)(2,1)S(1)}, bf16[512,1024]{1,0:T(8,128)(2,1)}, u32[]{:S(2)}) copy-start(bf16[512,1024]{1,0:T(8,128)(2,1)} %get-tuple-element.66.j_mine.jq_mine) | copy-start | bytes 3145732
  143.9 5.8 %collective-permute-start.21 = (bf16[512,1024]{1,0:T(8,128)(2,1)}, bf16[512,1024]{1,0:T(8,128)(2,1)S(1)}, u32[]{:S(2)}, u32[]{:S(2)}) collective-permute-start(bf16[512,1024]{1,0:T(8,128)(2,1)} %get-tuple-element.66.j_mine.jq_mine), channel_id=1, source_target_pairs={{0,4},{1,5},{2,6},{3,7},{4,0},{5,1},{6,2},{7,3},{8,12},{9,13},{10,... | collective-permute-start | bytes 3145736 | tf_op jit(solution)/shard_map/ppermute | solution.py:404
  144.3 5.5 %collective-permute-start.20 = (bf16[512,1024]{1,0:T(8,128)(2,1)}, bf16[512,1024]{1,0:T(8,128)(2,1)}, u32[]{:S(2)}, u32[]{:S(2)}) collective-permute-start(bf16[512,1024]{1,0:T(8,128)(2,1)} %collective-permute-done.13.c_mine), channel_id=1, source_target_pairs={{0,4},{1,5},{2,6},{3,7},{4,0},{5,1},{6,2},{7,3},{8,12},{9,13},{10,... | collective-permute-start | bytes 3145736 | tf_op jit(solution)/shard_map/ppermute | solution.py:404
  144.4 27.6 %collective-permute-start.25 = (bf16[512,1024]{1,0:T(8,128)(2,1)}, bf16[512,1024]{1,0:T(8,128)(2,1)S(1)}, u32[]{:S(2)}, u32[]{:S(2)}) collective-permute-start(bf16[512,1024]{1,0:T(8,128)(2,1)} %get-tuple-element.54.a_mine.aq_mine), channel_id=1, source_target_pairs={{0,8},{1,9},{4,12},{5,13},{8,16},{9,17},{12,20},{13,21},{16,24},{1... | collective-permute-start | bytes 3145736 | tf_op jit(solution)/shard_map/ppermute | solution.py:404
  163.4 8.6 %collective-permute-start.23 = (bf16[128,1024]{1,0:T(8,128)(2,1)}, bf16[128,1024]{1,0:T(8,128)(2,1)S(1)}, u32[]{:S(2)}, u32[]{:S(2)}) collective-permute-start(bf16[128,1024]{1,0:T(8,128)(2,1)} %get-tuple-element.55), channel_id=1, source_target_pairs={{0,3},{1,6},{4,2},{5,7},{8,11},{9,14},{12,10},{13,15},{16,19},{17,... | collective-permute-start | bytes 786440 | tf_op jit(solution)/shard_map/ppermute | solution.py:404
  172.0 18.1 %copy-start.4 = (bf16[512,1024]{1,0:T(8,128)(2,1)}, bf16[512,1024]{1,0:T(8,128)(2,1)S(1)}, u32[]{:S(2)}) copy-start(bf16[512,1024]{1,0:T(8,128)(2,1)S(1)} %collective-permute-done.25.a_mine) | copy-start | bytes 3145732
  172.0 33.1 %copy-start.26 = (bf16[128,1024]{1,0:T(8,128)(2,1)}, bf16[128,1024]{1,0:T(8,128)(2,1)S(1)}, u32[]{:S(2)}) copy-start(bf16[128,1024]{1,0:T(8,128)(2,1)S(1)} %collective-permute-done.23.refs_0_) | copy-start | bytes 786436
  172.0 18.1 %collective-permute-start.26 = (bf16[512,1024]{1,0:T(8,128)(2,1)S(1)}, bf16[512,1024]{1,0:T(8,128)(2,1)S(1)}, u32[]{:S(2)}, u32[]{:S(2)}) collective-permute-start(bf16[512,1024]{1,0:T(8,128)(2,1)S(1)} %collective-permute-done.25.a_mine), channel_id=1, source_target_pairs={{0,4},{1,5},{2,6},{3,7},{4,0},{5,1},{6,2},{7,3},{8,12},{9,13},{10,... | collective-permute-start | bytes 3145736 | tf_op jit(solution)/shard_map/ppermute | solution.py:404
  177.7 12.4 %collective-permute-start.24 = (bf16[128,1024]{1,0:T(8,128)(2,1)}, bf16[128,1024]{1,0:T(8,128)(2,1)S(1)}, u32[]{:S(2)}, u32[]{:S(2)}) collective-permute-start(bf16[128,1024]{1,0:T(8,128)(2,1)} %get-tuple-element.56), channel_id=1, source_target_pairs={{0,3},{1,6},{4,2},{5,7},{8,11},{9,14},{12,10},{13,15},{16,19},{17,... | collective-permute-start | bytes 786440 | tf_op jit(solution)/shard_map/ppermute | solution.py:404
  178.3 26.8 %collective-permute-start.29 = (bf16[512,1024]{1,0:T(8,128)(2,1)S(1)}, bf16[512,1024]{1,0:T(8,128)(2,1)}, u32[]{:S(2)}, u32[]{:S(2)}) collective-permute-start(bf16[512,1024]{1,0:T(8,128)(2,1)S(1)} %copy-done.3), channel_id=1, source_target_pairs={{0,8},{1,9},{4,12},{5,13},{8,16},{9,17},{12,20},{13,21},{16,24},{1... | collective-permute-start | bytes 3145736 | tf_op jit(solution)/shard_map/ppermute | solution.py:404
  190.1 15.1 %copy-start.27 = (bf16[128,1024]{1,0:T(8,128)(2,1)}, bf16[128,1024]{1,0:T(8,128)(2,1)S(1)}, u32[]{:S(2)}) copy-start(bf16[128,1024]{1,0:T(8,128)(2,1)S(1)} %collective-permute-done.24.refs_1_) | copy-start | bytes 786436
  195.9 22.0 %collective-permute-start.28 = (bf16[2,256,1024]{2,1,0:T(8,128)(2,1)}, bf16[2,256,1024]{2,1,0:T(8,128)(2,1)S(1)}, u32[]{:S(2)}, u32[]{:S(2)}) collective-permute-start(bf16[2,256,1024]{2,1,0:T(8,128)(2,1)} %get-tuple-element.62), channel_id=1, source_target_pairs={{0,1},{1,5},{4,0},{5,4},{8,9},{9,13},{12,8},{13,12},{16,17},{17,21... | collective-permute-start | bytes 3145736 | tf_op jit(solution)/shard_map/ppermute | solution.py:404
  196.9 18.2 %collective-permute-start.27 = (bf16[256,1024]{1,0:T(8,128)(2,1)}, bf16[256,1024]{1,0:T(8,128)(2,1)S(1)}, u32[]{:S(2)}, u32[]{:S(2)}) collective-permute-start(bf16[256,1024]{1,0:T(8,128)(2,1)} %get-tuple-element.61), channel_id=1, source_target_pairs={{0,3},{1,6},{4,2},{5,7},{8,11},{9,14},{12,10},{13,15},{16,19},{17,... | collective-permute-start | bytes 1572872 | tf_op jit(solution)/shard_map/ppermute | solution.py:404
  215.1 28.5 %copy-start.23 = (bf16[256,1024]{1,0:T(8,128)(2,1)}, bf16[256,1024]{1,0:T(8,128)(2,1)S(1)}, u32[]{:S(2)}) copy-start(bf16[256,1024]{1,0:T(8,128)(2,1)S(1)} %collective-permute-done.27.refs_2_) | copy-start | bytes 1572868
  217.9 25.8 %copy-start.15 = (bf16[2,256,1024]{2,1,0:T(8,128)(2,1)}, bf16[2,256,1024]{2,1,0:T(8,128)(2,1)S(1)}, u32[]{:S(2)}) copy-start(bf16[2,256,1024]{2,1,0:T(8,128)(2,1)S(1)} %collective-permute-done.28.refs_3_) | copy-start | bytes 3145732
  217.9 25.8 %collective-permute-start.30 = (bf16[256,1024]{1,0:T(8,128)(2,1)}, bf16[256,1024]{1,0:T(8,128)(2,1)S(1)}, u32[]{:S(2)}, u32[]{:S(2)}) collective-permute-start(bf16[256,1024]{1,0:T(8,128)(2,1)} %get-tuple-element.69), channel_id=1, source_target_pairs={{0,3},{1,6},{4,2},{5,7},{8,11},{9,14},{12,10},{13,15},{16,19},{17,... | collective-permute-start | bytes 1572872 | tf_op jit(solution)/shard_map/ppermute | solution.py:404
  218.2 25.5 %collective-permute-start.31 = (bf16[256,1024]{1,0:T(8,128)(2,1)}, bf16[256,1024]{1,0:T(8,128)(2,1)S(1)}, u32[]{:S(2)}, u32[]{:S(2)}) collective-permute-start(bf16[256,1024]{1,0:T(8,128)(2,1)} %get-tuple-element.71), channel_id=1, source_target_pairs={{0,1},{1,5},{4,0},{5,4},{8,9},{9,13},{12,8},{13,12},{16,17},{17,21... | collective-permute-start | bytes 1572872 | tf_op jit(solution)/shard_map/ppermute | solution.py:404
  (12 other events, 18.7 us)

commit v4 on v3

--- a/solution.py
+++ b/solution.py
@@ -8,7 +8,7 @@
 from jax.sharding import PartitionSpec as P
 
 AXES = ("tm", "panel")
-VMEM_BYTES = 60 * 2**20
+VMEM_BYTES = 32 * 2**20
 TILE = 512
 HBM = pl.BlockSpec(memory_space=pltpu.HBM)
 
@@ -78,12 +78,13 @@
         return [block for i in range(pairs) for block in (self.near(first + i), self.far(first + i))]
 
 
-def call(kernel, out_shapes, operands, scratch=(), out_space=pltpu.HBM, flops=1):
+def call(kernel, out_shapes, operands, scratch=(), flops=1, aliases=None):
     return pl.pallas_call(
         kernel,
         out_shape=list(out_shapes),
         in_specs=[HBM] * len(operands),
-        out_specs=[pl.BlockSpec(memory_space=out_space)] * len(out_shapes),
+        out_specs=[HBM] * len(out_shapes),
+        input_output_aliases=aliases or {},
         scratch_shapes=list(scratch),
         compiler_params=pltpu.CompilerParams(vmem_limit_bytes=VMEM_BYTES),
         cost_estimate=pl.CostEstimate(flops=flops, bytes_accessed=1, transcendentals=0),
@@ -360,32 +361,54 @@
     wait(store_blocks(plan, copies, jh, far, near))
 
 
+def home_blocks(plan, rows):
+    half, pairs = plan.half, plan.half // 2
+    t, z = lax.axis_index("tm"), lax.axis_index("panel")
+    tests = []
+    for segment, panel in ((t, z), (plan.groups - 1 - t, plan.panels - 1 - z)):
+        distance = lax.rem(panel + half - lax.rem(segment, 2), half)
+        which = jnp.where(panel >= half, lax.rem(panel, pairs), pairs + lax.rem(distance, pairs))
+        tests.append(which)
+    return tests
+
+
 def home_kernel(plan, *refs):
     half, pairs = plan.half, plan.half // 2
     c_far, a_far, ca_near = refs[:half], refs[half : half + pairs], refs[half + pairs : 2 * half]
-    j_far, j_near = refs[2 * half : 2 * half + pairs], refs[2 * half + pairs : 3 * half]
-    f_out, b_out, sems = refs[3 * half :]
-    rows = f_out.shape[1]
-    t, z = lax.axis_index("tm"), lax.axis_index("panel")
+    outs, (held, sems) = refs[2 * half : 2 * half + 2], refs[2 * half + 2 :]
+    rows = held.shape[2]
+    part = rows // 2
     waits = []
-    places = [(f_out, t, z), (b_out, plan.groups - 1 - t, plan.panels - 1 - z)]
-    for out, segment, panel in places:
-        distance = lax.rem(panel + half - lax.rem(segment, 2), half)
-        which = jnp.where(panel >= half, lax.rem(panel, pairs), pairs + lax.rem(distance, pairs))
-        first = len(waits)
+    for k, which in enumerate(home_blocks(plan, rows)):
+        c, a = held.at[k, 0], held.at[k, 1]
         for i in range(pairs):
-            halves = [out.at[0, pl.ds(k * (rows // 2), rows // 2), :] for k in range(2)]
-            far = [(c_far[i], halves[0]), (c_far[pairs + i], halves[1]), (a_far[i], out.at[1]), (j_far[i], out.at[2])]
-            near = [(ca_near[i].at[k], out.at[k]) for k in range(2)] + [(j_near[i], out.at[2])]
+            far = [(c_far[i], c.at[pl.ds(0, part), :], 0), (c_far[pairs + i], c.at[pl.ds(part, part), :], 0), (a_far[i], a, 1)]
+            near = [(ca_near[i].at[0], c, 0), (ca_near[i].at[1], a, 1)]
             for owner, moves in ((i, far), (pairs + i, near)):
-                @pl.when(which == owner)
-                def _():
-                    for k, (source_ref, target) in enumerate(moves):
-                        at = k - 1 if len(moves) == 4 and k > 0 else k
-                        pltpu.make_async_copy(source_ref, target, sems.at[first + at]).start()
-        for matrix in range(3):
-            waits.append(pltpu.make_async_copy(j_far[0], out.at[matrix], sems.at[first + matrix]))
+                for source, target, matrix in moves:
+                    pl.when(which == owner)(pltpu.make_async_copy(source, target, sems.at[2 * k + matrix]).start)
+        for matrix in range(2):
+            waits.append(pltpu.make_async_copy(a_far[0], held.at[k, matrix], sems.at[2 * k + matrix]))
     wait(waits)
+    run = [pltpu.make_async_copy(held.at[k], outs[k].at[pl.ds(0, 2)], sems.at[k]) for k in range(2)]
+    for copy in run:
+        copy.start()
+    wait(run)
+
+
+def home_info_kernel(plan, f_in, b_in, *refs):
+    pairs = plan.half // 2
+    j_far, j_near, outs, (held, sems) = refs[:pairs], refs[pairs : 2 * pairs], refs[2 * pairs : 2 * pairs + 2], refs[-2:]
+    waits, run = [], []
+    for k, which in enumerate(home_blocks(plan, held.shape[1])):
+        for owner, source in enumerate([*j_far, *j_near]):
+            pl.when(which == owner)(pltpu.make_async_copy(source, held.at[k], sems.at[k]).start)
+        waits.append(pltpu.make_async_copy(j_far[0], held.at[k], sems.at[k]))
+        run.append(pltpu.make_async_copy(held.at[k], outs[k].at[2], sems.at[2 + k]))
+    for copy, store in zip(waits, run):
+        copy.wait()
+        store.start()
+    wait(run)
 
 
 def after(x, *others):
@@ -415,7 +438,6 @@
     is_q, special = (core + layer) % 2 == 0, (core == 1) & (layer == 0)
     other_c = jnp.where(z < half, backward[0], forward[0])
     other_ja = jnp.stack([jnp.where(z < half, backward[i], forward[i]) for i in (2, 1)])
-    forward, backward, _ = lax.optimization_barrier((forward, backward, other_ja))
     own = jnp.where(z < half, forward, backward)
 
     far_c = [send(other_c, route) for route in plan.cross]
@@ -431,7 +453,7 @@
     raw_first = [*nears, *far_first, *first_swap]
     kept_c = [swap(x) for x in far_c[: half // 2]]
 
-    rest = [send(after(x, *far_c_of_p), plan.forward) for x in far_ja]
+    rest = [send(x, plan.forward) for x in far_ja]
 
     c_new, jq, x1, r, f = kernel(
         first_kernel,
@@ -499,12 +521,20 @@
     )
     j_home = send_home([after(x, *a_far, *ca_near) for x in j_pieces], [*far, *near])
 
+    outs = [bf16(3, rows, n)] * 2
     f_out, b_out = kernel(
         home_kernel,
-        [bf16(3, rows, n)] * 2,
-        [*c_far, *a_far, *ca_near, *j_home],
-        [],
-        out_space=pltpu.VMEM,
+        outs,
+        [*c_far, *a_far, *ca_near],
+        [pltpu.VMEM((2, 2, rows, n), jnp.bfloat16)],
+        flops=n**3,
+    )
+    f_out, b_out = kernel(
+        home_info_kernel,
+        outs,
+        [f_out, b_out, *j_home],
+        [pltpu.VMEM((2, rows, n), jnp.bfloat16)],
+        aliases={0: 0, 1: 1},
     )
     return f_out[:, None], b_out[:, None]
 

time: 253 us -> 241 us (0.953)
  Pallas kernels: 58.3 us -> 41 us
  local copies, waits for them, and re-layouts: 9.05 us -> 0.15 us
  starting transfers between devices: 57.3 us -> 65.3 us
  waiting for transfers between devices: 114 us -> 121 us
    pallas_call x7 -> x8, Pallas kernels: 58.3 us -> 41 us  [call(): pl.pallas_call(kernel, out_shape=list(out_shapes), in_specs=[HBM] * len(o...]
    ppermute x32, starting transfers between devices: 57.3 us -> 65.3 us  [send(): return lax.ppermute(x, AXES, routes)]
    ppermute x32, waiting for transfers between devices: 114 us -> 121 us  [send(): return lax.ppermute(x, AXES, routes)]
    unnamed x56 -> x8, local copies, waits for them, and re-layouts: 6.51 us -> 0.02 us
  transfers between devices with their start and end apart: 32 -> 32, of which waited for: 16 -> 15; matrix products, arithmetic and copies ran while one was open for 4% -> 3% of each run, Pallas kernels for 22% -> 17%
where the time goes in v4:
time: 241 us; the launch traced here: 237 us
  waiting for transfers between devices  121 us (50%)
  starting transfers between devices  65.3 us (27%)
  Pallas kernels  41 us (17%)
  other arithmetic  8.45 us (4%)
    ppermute x32, waiting for transfers between devices, send(): return lax.ppermute(x, AXES, routes)  121 us
    ppermute x32, starting transfers between devices, send(): return lax.ppermute(x, AXES, routes)  65.3 us
    pallas_call x8, Pallas kernels, call(): pl.pallas_call(kernel, out_shape=list(out_shapes), in_specs=[HBM] * len(o...  41 us
  transfers between devices with their start and end apart: 32, of which 15 were waited for; matrix products, arithmetic and copies ran while one was open for 3% of the time, Pallas kernels for 17%

profile of v4, /device:TPU:10, one launch (start us, length us, event | category | flops | bytes accessed | tf_op | source)
XLA Modules:
  0.0 236.9 jit_solution(17686643809025432435)
XLA Ops:
  0.7 2.1 select_bitcast_fusion.1
  2.8 0.7 collective-permute-start.1
  3.5 4.9 %collective-permute-start = (bf16[256,1024]{1,0:T(8,128)(2,1)S(1)}, bf16[256,1024]{1,0:T(8,128)(2,1)}, u32[]{:S(2)}, u32[]{:S(2)}) collective-permute-start(bf16[256,1024]{1,0:T(8,128)(2,1)S(1)} %get-tuple-element.73), channel_id=1, source_target_pairs={{2,0},{6,5},{10,8},{14,13},{18,16},{22,21},{26,24},{30,29},{29,31}... | collective-permute-start | bytes 1572872 | tf_op jit(solution)/shard_map/ppermute | solution.py:427
  8.4 1.3 fusion
  9.7 2.6 %collective-permute-start.3 = (bf16[3,256,1024]{2,1,0:T(8,128)(2,1)}, bf16[3,256,1024]{2,1,0:T(8,128)(2,1)S(1)}, u32[]{:S(2)}, u32[]{:S(2)}) collective-permute-start(bf16[3,256,1024]{2,1,0:T(8,128)(2,1)} %fusion), channel_id=1, source_target_pairs={{1,0},{4,5},{9,8},{12,13},{17,16},{20,21},{25,24},{28,29},{0,1},{5... | collective-permute-start | bytes 4718600 | tf_op jit(solution)/shard_map/ppermute | solution.py:427
  12.3 18.2 %collective-permute-done = bf16[256,1024]{1,0:T(8,128)(2,1)} collective-permute-done((bf16[256,1024]{1,0:T(8,128)(2,1)S(1)}, bf16[256,1024]{1,0:T(8,128)(2,1)}, u32[]{:S(2)}, u32[]{:S(2)}) %collective-permute-start) | collective-permute-done | bytes 524320 | tf_op jit(solution)/shard_map/ppermute | solution.py:427
  30.6 1.8 collective-permute-start.2
  32.4 1.1 pad_maximum_fusion
  33.4 1.6 collective-permute-start.8
  35.1 1.3 collective-permute-start.9
  36.4 9.2 %collective-permute-start.6 = (bf16[2,256,1024]{2,1,0:T(8,128)(2,1)}, bf16[2,256,1024]{2,1,0:T(8,128)(2,1)}, u32[]{:S(2)}, u32[]{:S(2)}) collective-permute-start(bf16[2,256,1024]{2,1,0:T(8,128)(2,1)} %pad_maximum_fusion), channel_id=1, source_target_pairs={{2,0},{6,5},{10,8},{14,13},{18,16},{22,21},{26,24},{30,29},{29,31}... | collective-permute-start | bytes 3145736 | tf_op jit(solution)/shard_map/ppermute | solution.py:427
  45.6 36.7 %collective-permute-done.9 = bf16[256,1024]{1,0:T(8,128)(2,1)S(1)} collective-permute-done((bf16[256,1024]{1,0:T(8,128)(2,1)S(1)}, bf16[256,1024]{1,0:T(8,128)(2,1)S(1)}, u32[]{:S(2)}, u32[]{:S(2)}) %collective-permute-start.9) | collective-permute-done | bytes 524320 | tf_op jit(solution)/shard_map/ppermute | solution.py:427
  82.3 1.3 collective-permute-start.7
  83.6 1.2 broadcast_select_fusion.1.refs_5_
  84.7 2.9 %collective-permute-start.11 = (bf16[2,256,1024]{2,1,0:T(8,128)(2,1)S(1)}, bf16[2,256,1024]{2,1,0:T(8,128)(2,1)}, u32[]{:S(2)}, u32[]{:S(2)}) collective-permute-start(bf16[2,256,1024]{2,1,0:T(8,128)(2,1)S(1)} %broadcast_select_fusion.1.refs_5_), channel_id=1, source_target_pairs={{0,4},{1,5},{2,6},{3,7},{4,0},{5,1},{6,2},{7,3},{8,12},{9,13},{10,... | collective-permute-start | bytes 3145736 | tf_op jit(solution)/shard_map/ppermute | solution.py:427
  87.7 1.6 broadcast_select_fusion.refs_0_.refs_8_.refs_16_
  89.8 3.9 %collective-permute-done.7 = bf16[256,1024]{1,0:T(8,128)(2,1)} collective-permute-done((bf16[256,1024]{1,0:T(8,128)(2,1)}, bf16[256,1024]{1,0:T(8,128)(2,1)}, u32[]{:S(2)}, u32[]{:S(2)}) %collective-permute-start.7) | collective-permute-done | bytes 524320 | tf_op jit(solution)/shard_map/ppermute | solution.py:427
  93.7 1.2 broadcast_select_fusion.2.refs_4_
  94.8 0.9 collective-permute-start.10
  95.8 1.3 collective-permute-start.15
  97.1 1.3 collective-permute-start.14
  98.4 11.5 %shard_map.41 = (bf16[512,1024]{1,0:T(8,128)(2,1)S(1)}, bf16[1024,1024]{1,0:T(8,128)(2,1)S(1)}, bf16[1024,1024]{1,0:T(8,128)(2,1)S(1)}, bf16[1024,1024]{1,0:T(8,128)(2,1)S(1)}, bf16[512,1024]{1,0:T(8,128)(2,1)S(1)}) custom-call(bf16[3,256,1024]{2,1,0:T(8,128)(2,1)S(1)} %broadcast_select_fusion.refs_0_.refs_8_.refs_16_, ...), custom_call_target="tpu_custom_call" | custom-call | flops 1 | bytes 1 | tf_op jit(solution)/shard_map/pallas_call | solution.py:82
  110.0 3.4 %collective-permute-start.13 = (bf16[512,1024]{1,0:T(8,128)(2,1)S(1)}, bf16[512,1024]{1,0:T(8,128)(2,1)S(1)}, u32[]{:S(2)}, u32[]{:S(2)}) collective-permute-start(bf16[512,1024]{1,0:T(8,128)(2,1)S(1)} %get-tuple-element.37.cq_mine), channel_id=1, source_target_pairs={{0,8},{1,9},{4,12},{5,13},{8,16},{9,17},{12,20},{13,21},{16,24},{1... | collective-permute-start | bytes 3145736 | tf_op jit(solution)/shard_map/ppermute | solution.py:427
  113.4 10.5 %collective-permute-done.14 = bf16[2,256,1024]{2,1,0:T(8,128)(2,1)S(1)} collective-permute-done((bf16[2,256,1024]{2,1,0:T(8,128)(2,1)}, bf16[2,256,1024]{2,1,0:T(8,128)(2,1)S(1)}, u32[]{:S(2)}, u32[]{:S(2)}) %collective-permute-start.14) | collective-permute-done | bytes 1048608 | tf_op jit(solution)/shard_map/ppermute | solution.py:427
  125.2 0.7 collective-permute-done.18.refs_22_
  126.0 0.7 collective-permute-done.16.refs_14_
  126.7 0.7 collective-permute-done.19.refs_23_
  127.5 0.7 collective-permute-done.17.refs_15_
  128.2 7.4 %shard_map.42 = (bf16[512,1024]{1,0:T(8,128)(2,1)S(1)}, bf16[512,1024]{1,0:T(8,128)(2,1)S(1)}) custom-call(bf16[512,1024]{1,0:T(8,128)(2,1)S(1)} %get-tuple-element.39.f_ref, bf16[1024,1024]{1,0:T(8,128)(2,1)S(1)} %get-tuple-element.40.jq_ref, bf16[1024,1024]{1,0:T(8,128)(2,1)S(1)} %get-tuple-element.41.x1_ref, bf16[1024,1024]{1,0:T(8,128)(2,1)} %copy-done, ...), custom_call_target="tpu_custom_call" | custom-call | flops 1 | bytes 1 | tf_op jit(solution)/shard_map/pallas_call | solution.py:82
  136.2 1.5 collective-permute-start.20
  137.7 4.3 %collective-permute-start.25 = (bf16[512,1024]{1,0:T(8,128)(2,1)S(1)}, bf16[512,1024]{1,0:T(8,128)(2,1)S(1)}, u32[]{:S(2)}, u32[]{:S(2)}) collective-permute-start(bf16[512,1024]{1,0:T(8,128)(2,1)S(1)} %get-tuple-element.48.a_mine.aq_mine), channel_id=1, source_target_pairs={{0,8},{1,9},{4,12},{5,13},{8,16},{9,17},{12,20},{13,21},{16,24},{1... | collective-permute-start | bytes 3145736 | tf_op jit(solution)/shard_map/ppermute | solution.py:427
  142.0 10.7 %shard_map.43 = (bf16[128,1024]{1,0:T(8,128)(2,1)S(1)}, bf16[128,1024]{1,0:T(8,128)(2,1)S(1)}, bf16[256,1024]{1,0:T(8,128)(2,1)S(1)}, bf16[512,1024]{1,0:T(8,128...) custom-call(bf16[512,1024]{1,0:T(8,128)(2,1)S(1)} %collective-permute-done.13.c_mine, ...), custom_call_target="tpu_custom_call" | custom-call | flops 1 | bytes 1 | tf_op jit(solution)/shard_map/pallas_call | solution.py:82
  152.8 11.9 %collective-permute-done.25.a_mine = bf16[512,1024]{1,0:T(8,128)(2,1)S(1)} collective-permute-done((bf16[512,1024]{1,0:T(8,128)(2,1)S(1)}, bf16[512,1024]{1,0:T(8,128)(2,1)S(1)}, u32[]{:S(2)}, u32[]{:S(2)}) %collective-permute-start.25) | collective-permute-done | bytes 1048608 | tf_op jit(solution)/shard_map/ppermute | solution.py:427
  164.7 7.6 %collective-permute-start.26 = (bf16[512,1024]{1,0:T(8,128)(2,1)S(1)}, bf16[512,1024]{1,0:T(8,128)(2,1)S(1)}, u32[]{:S(2)}, u32[]{:S(2)}) collective-permute-start(bf16[512,1024]{1,0:T(8,128)(2,1)S(1)} %collective-permute-done.25.a_mine), channel_id=1, source_target_pairs={{0,4},{1,5},{2,6},{3,7},{4,0},{5,1},{6,2},{7,3},{8,12},{9,13},{10,... | collective-permute-start | bytes 3145736 | tf_op jit(solution)/shard_map/ppermute | solution.py:427
  172.3 1.7 collective-permute-start.24
  174.0 3.3 %collective-permute-start.29 = (bf16[512,1024]{1,0:T(8,128)(2,1)S(1)}, bf16[512,1024]{1,0:T(8,128)(2,1)S(1)}, u32[]{:S(2)}, u32[]{:S(2)}) collective-permute-start(bf16[512,1024]{1,0:T(8,128)(2,1)S(1)} %get-tuple-element.62.j_mine.jq_mine), channel_id=1, source_target_pairs={{0,8},{1,9},{4,12},{5,13},{8,16},{9,17},{12,20},{13,21},{16,24},{1... | collective-permute-start | bytes 3145736 | tf_op jit(solution)/shard_map/ppermute | solution.py:427
  177.3 4.0 %collective-permute-done.24.refs_1_ = bf16[128,1024]{1,0:T(8,128)(2,1)S(1)} collective-permute-done((bf16[128,1024]{1,0:T(8,128)(2,1)S(1)}, bf16[128,1024]{1,0:T(8,128)(2,1)S(1)}, u32[]{:S(2)}, u32[]{:S(2)}) %collective-permute-start.24) | collective-permute-done | bytes 262176 | tf_op jit(solution)/shard_map/ppermute | solution.py:427
  181.4 1.9 shard_map.44
  183.3 5.4 %collective-permute-start.28 = (bf16[2,256,1024]{2,1,0:T(8,128)(2,1)S(1)}, bf16[2,256,1024]{2,1,0:T(8,128)(2,1)S(1)}, u32[]{:S(2)}, u32[]{:S(2)}) collective-permute-start(bf16[2,256,1024]{2,1,0:T(8,128)(2,1)S(1)} %get-tuple-element.56), channel_id=1, source_target_pairs={{0,1},{1,5},{4,0},{5,4},{8,9},{9,13},{12,8},{13,12},{16,17},{17,21... | collective-permute-start | bytes 3145736 | tf_op jit(solution)/shard_map/ppermute | solution.py:427
  189.3 4.7 %shard_map.46.h_ref = bf16[512,1024]{1,0:T(8,128)(2,1)S(1)} custom-call(bf16[512,1024]{1,0:T(8,128)(2,1)S(1)} %collective-permute-done.25.a_mine, bf16[512,1024]{1,0:T(8,128)(2,1)S(1)} %collective-permute-done.26.a_theirs, bf16[512,1024]{1,0:T(8,128)(2,1)S(1)} %get-tuple-element.62.j_mine.jq_mine, bf16[512,1024]{1,0:T(8,128)(2,1)S(1)} %collective-permute-done.21.j_theirs, ...), custom_call_target="tpu_custom_call" | custom-call | flops 1 | bytes 1 | tf_op jit(solution)/shard_map/pallas_call | solution.py:82
  194.0 3.3 %collective-permute-done.29.jp_mine = bf16[512,1024]{1,0:T(8,128)(2,1)S(1)} collective-permute-done((bf16[512,1024]{1,0:T(8,128)(2,1)S(1)}, bf16[512,1024]{1,0:T(8,128)(2,1)S(1)}, u32[]{:S(2)}, u32[]{:S(2)}) %collective-permute-start.29) | collective-permute-done | bytes 1048608 | tf_op jit(solution)/shard_map/ppermute | solution.py:427
  197.2 1.9 shard_map.47
  199.1 7.1 %collective-permute-done.27.refs_2_ = bf16[256,1024]{1,0:T(8,128)(2,1)S(1)} collective-permute-done((bf16[256,1024]{1,0:T(8,128)(2,1)S(1)}, bf16[256,1024]{1,0:T(8,128)(2,1)S(1)}, u32[]{:S(2)}, u32[]{:S(2)}) %collective-permute-start.27) | collective-permute-done | bytes 524320 | tf_op jit(solution)/shard_map/ppermute | solution.py:427
  206.2 3.3 %collective-permute-done.28.refs_3_ = bf16[2,256,1024]{2,1,0:T(8,128)(2,1)S(1)} collective-permute-done((bf16[2,256,1024]{2,1,0:T(8,128)(2,1)S(1)}, bf16[2,256,1024]{2,1,0:T(8,128)(2,1)S(1)}, u32[]{:S(2)}, u32[]{:S(2)}) %collective-permute-start.28) | collective-permute-done | bytes 1048608 | tf_op jit(solution)/shard_map/ppermute | solution.py:427
  209.7 5.1 %collective-permute-start.31 = (bf16[256,1024]{1,0:T(8,128)(2,1)S(1)}, bf16[256,1024]{1,0:T(8,128)(2,1)S(1)}, u32[]{:S(2)}, u32[]{:S(2)}) collective-permute-start(bf16[256,1024]{1,0:T(8,128)(2,1)S(1)} %get-tuple-element.67), channel_id=1, source_target_pairs={{0,1},{1,5},{4,0},{5,4},{8,9},{9,13},{12,8},{13,12},{16,17},{17,21... | collective-permute-start | bytes 1572872 | tf_op jit(solution)/shard_map/ppermute | solution.py:427
  214.8 1.7 shard_map.45
  216.5 19.0 %collective-permute-done.30.refs_0_ = bf16[256,1024]{1,0:T(8,128)(2,1)S(1)} collective-permute-done((bf16[256,1024]{1,0:T(8,128)(2,1)S(1)}, bf16[256,1024]{1,0:T(8,128)(2,1)S(1)}, u32[]{:S(2)}, u32[]{:S(2)}) %collective-permute-start.30) | collective-permute-done | bytes 524320 | tf_op jit(solution)/shard_map/ppermute | solution.py:427
  235.4 1.3 shard_map.48
  (40 shorter events, 3.5 us)
Async XLA Ops:
  0.6 7.8 %copy-start.1 = (bf16[3,1,256,1024]{3,2,1,0:T(8,128)(2,1)S(1)}, bf16[3,1,256,1024]{3,2,1,0:T(8,128)(2,1)}, u32[]{:S(2)}) copy-start(bf16[3,1,256,1024]{3,2,1,0:T(8,128)(2,1)} %param.3) | copy-start | bytes 4718596
  0.6 7.8 %copy-start.2 = (bf16[3,1,256,1024]{3,2,1,0:T(8,128)(2,1)S(1)}, bf16[3,1,256,1024]{3,2,1,0:T(8,128)(2,1)}, u32[]{:S(2)}) copy-start(bf16[3,1,256,1024]{3,2,1,0:T(8,128)(2,1)} %param.2) | copy-start | bytes 4718596
  2.8 9.5 %collective-permute-start.1 = (bf16[256,1024]{1,0:T(8,128)(2,1)S(1)}, bf16[256,1024]{1,0:T(8,128)(2,1)S(1)}, u32[]{:S(2)}, u32[]{:S(2)}) collective-permute-start(bf16[256,1024]{1,0:T(8,128)(2,1)S(1)} %get-tuple-element.73), channel_id=1, source_target_pairs={{3,0},{7,5},{11,8},{15,13},{19,16},{23,21},{27,24},{31,29},{28,31}... | collective-permute-start | bytes 1572872 | tf_op jit(solution)/shard_map/ppermute | solution.py:427
  3.5 27.0 %collective-permute-start = (bf16[256,1024]{1,0:T(8,128)(2,1)S(1)}, bf16[256,1024]{1,0:T(8,128)(2,1)}, u32[]{:S(2)}, u32[]{:S(2)}) collective-permute-start(bf16[256,1024]{1,0:T(8,128)(2,1)S(1)} %get-tuple-element.73), channel_id=1, source_target_pairs={{2,0},{6,5},{10,8},{14,13},{18,16},{22,21},{26,24},{30,29},{29,31}... | collective-permute-start | bytes 1572872 | tf_op jit(solution)/shard_map/ppermute | solution.py:427
  9.7 77.9 %collective-permute-start.3 = (bf16[3,256,1024]{2,1,0:T(8,128)(2,1)}, bf16[3,256,1024]{2,1,0:T(8,128)(2,1)S(1)}, u32[]{:S(2)}, u32[]{:S(2)}) collective-permute-start(bf16[3,256,1024]{2,1,0:T(8,128)(2,1)} %fusion), channel_id=1, source_target_pairs={{1,0},{4,5},{9,8},{12,13},{17,16},{20,21},{25,24},{28,29},{0,1},{5... | collective-permute-start | bytes 4718600 | tf_op jit(solution)/shard_map/ppermute | solution.py:427
  30.6 57.1 %collective-permute-start.2 = (bf16[3,256,1024]{2,1,0:T(8,128)(2,1)}, bf16[3,256,1024]{2,1,0:T(8,128)(2,1)}, u32[]{:S(2)}, u32[]{:S(2)}) collective-permute-start(bf16[3,256,1024]{2,1,0:T(8,128)(2,1)} %fusion), channel_id=1, source_target_pairs={{4,12},{12,20},{20,28},{27,19},{19,11},{11,3}} | collective-permute-start | bytes 4718600 | tf_op jit(solution)/shard_map/ppermute | solution.py:427
  33.4 50.1 %collective-permute-start.8 = (bf16[2,256,1024]{2,1,0:T(8,128)(2,1)}, bf16[2,256,1024]{2,1,0:T(8,128)(2,1)}, u32[]{:S(2)}, u32[]{:S(2)}) collective-permute-start(bf16[2,256,1024]{2,1,0:T(8,128)(2,1)} %pad_maximum_fusion), channel_id=1, source_target_pairs={{3,0},{7,5},{11,8},{15,13},{19,16},{23,21},{27,24},{31,29},{28,31}... | collective-permute-start | bytes 3145736 | tf_op jit(solution)/shard_map/ppermute | solution.py:427
  35.1 47.2 %collective-permute-start.9 = (bf16[256,1024]{1,0:T(8,128)(2,1)S(1)}, bf16[256,1024]{1,0:T(8,128)(2,1)S(1)}, u32[]{:S(2)}, u32[]{:S(2)}) collective-permute-start(bf16[256,1024]{1,0:T(8,128)(2,1)S(1)} %collective-permute-done.1.refs_9_), channel_id=1, source_target_pairs={{0,1},{5,12},{8,9},{13,20},{16,17},{21,28},{24,25},{31,30},{26,19}... | collective-permute-start | bytes 1572872 | tf_op jit(solution)/shard_map/ppermute | solution.py:427
  36.4 57.3 %collective-permute-start.6 = (bf16[2,256,1024]{2,1,0:T(8,128)(2,1)}, bf16[2,256,1024]{2,1,0:T(8,128)(2,1)}, u32[]{:S(2)}, u32[]{:S(2)}) collective-permute-start(bf16[2,256,1024]{2,1,0:T(8,128)(2,1)} %pad_maximum_fusion), channel_id=1, source_target_pairs={{2,0},{6,5},{10,8},{14,13},{18,16},{22,21},{26,24},{30,29},{29,31}... | collective-permute-start | bytes 3145736 | tf_op jit(solution)/shard_map/ppermute | solution.py:427
  82.3 1.3 copy-start.3
  82.3 11.4 %collective-permute-start.7 = (bf16[256,1024]{1,0:T(8,128)(2,1)}, bf16[256,1024]{1,0:T(8,128)(2,1)}, u32[]{:S(2)}, u32[]{:S(2)}) collective-permute-start(bf16[256,1024]{1,0:T(8,128)(2,1)} %collective-permute-done), channel_id=1, source_target_pairs={{0,1},{5,12},{8,9},{13,20},{16,17},{21,28},{24,25},{31,30},{26,19}... | collective-permute-start | bytes 1572872 | tf_op jit(solution)/shard_map/ppermute | solution.py:427
  84.7 12.3 %collective-permute-start.11 = (bf16[2,256,1024]{2,1,0:T(8,128)(2,1)S(1)}, bf16[2,256,1024]{2,1,0:T(8,128)(2,1)}, u32[]{:S(2)}, u32[]{:S(2)}) collective-permute-start(bf16[2,256,1024]{2,1,0:T(8,128)(2,1)S(1)} %broadcast_select_fusion.1.refs_5_), channel_id=1, source_target_pairs={{0,4},{1,5},{2,6},{3,7},{4,0},{5,1},{6,2},{7,3},{8,12},{9,13},{10,... | collective-permute-start | bytes 3145736 | tf_op jit(solution)/shard_map/ppermute | solution.py:427
  87.6 10.8 %collective-permute-start.5 = (bf16[3,256,1024]{2,1,0:T(8,128)(2,1)S(1)}, bf16[3,256,1024]{2,1,0:T(8,128)(2,1)S(1)}, u32[]{:S(2)}, u32[]{:S(2)}) collective-permute-start(bf16[3,256,1024]{2,1,0:T(8,128)(2,1)S(1)} %collective-permute-done.3.refs_1_.refs_9_.refs_17_), channel_id=1, source_target_pairs={{0,4},{1,5},{2,6},{3,7},{4,0},{5,1},{6,2},{7,3},{8,12},{9,13},{10,... | collective-permute-start | bytes 4718600 | tf_op jit(solution)/shard_map/ppermute | solution.py:427
  89.3 9.1 %collective-permute-start.4 = (bf16[3,256,1024]{2,1,0:T(8,128)(2,1)S(1)}, bf16[3,256,1024]{2,1,0:T(8,128)(2,1)S(1)}, u32[]{:S(2)}, u32[]{:S(2)}) collective-permute-start(bf16[3,256,1024]{2,1,0:T(8,128)(2,1)S(1)} %broadcast_select_fusion.refs_0_.refs_8_.refs_16_), channel_id=1, source_target_pairs={{0,4},{1,5},{2,6},{3,7},{4,0},{5,1},{6,2},{7,3},{8,12},{9,13},{10,... | collective-permute-start | bytes 4718600 | tf_op jit(solution)/shard_map/ppermute | solution.py:427
  93.7 2.1 collective-permute-start.12
  94.8 3.6 %collective-permute-start.10 = (bf16[2,256,1024]{2,1,0:T(8,128)(2,1)S(1)}, bf16[2,256,1024]{2,1,0:T(8,128)(2,1)S(1)}, u32[]{:S(2)}, u32[]{:S(2)}) collective-permute-start(bf16[2,256,1024]{2,1,0:T(8,128)(2,1)S(1)} %broadcast_select_fusion.2.refs_4_), channel_id=1, source_target_pairs={{0,4},{1,5},{2,6},{3,7},{4,0},{5,1},{6,2},{7,3},{8,12},{9,13},{10,... | collective-permute-start | bytes 3145736 | tf_op jit(solution)/shard_map/ppermute | solution.py:427
  95.8 17.6 %collective-permute-start.15 = (bf16[2,256,1024]{2,1,0:T(8,128)(2,1)}, bf16[2,256,1024]{2,1,0:T(8,128)(2,1)S(1)}, u32[]{:S(2)}, u32[]{:S(2)}) collective-permute-start(bf16[2,256,1024]{2,1,0:T(8,128)(2,1)} %collective-permute-done.8), channel_id=1, source_target_pairs={{0,1},{5,12},{8,9},{13,20},{16,17},{21,28},{24,25},{31,30},{26,19}... | collective-permute-start | bytes 3145736 | tf_op jit(solution)/shard_map/ppermute | solution.py:427
  97.1 26.8 %collective-permute-start.14 = (bf16[2,256,1024]{2,1,0:T(8,128)(2,1)}, bf16[2,256,1024]{2,1,0:T(8,128)(2,1)S(1)}, u32[]{:S(2)}, u32[]{:S(2)}) collective-permute-start(bf16[2,256,1024]{2,1,0:T(8,128)(2,1)} %collective-permute-done.6), channel_id=1, source_target_pairs={{0,1},{5,12},{8,9},{13,20},{16,17},{21,28},{24,25},{31,30},{26,19}... | collective-permute-start | bytes 3145736 | tf_op jit(solution)/shard_map/ppermute | solution.py:427
  109.9 14.7 %copy-start = (bf16[1024,1024]{1,0:T(8,128)(2,1)}, bf16[1024,1024]{1,0:T(8,128)(2,1)S(1)}, u32[]{:S(2)}) copy-start(bf16[1024,1024]{1,0:T(8,128)(2,1)S(1)} %get-tuple-element.42.r_ref) | copy-start | bytes 6291460
  110.0 26.2 %collective-permute-start.13 = (bf16[512,1024]{1,0:T(8,128)(2,1)S(1)}, bf16[512,1024]{1,0:T(8,128)(2,1)S(1)}, u32[]{:S(2)}, u32[]{:S(2)}) collective-permute-start(bf16[512,1024]{1,0:T(8,128)(2,1)S(1)} %get-tuple-element.37.cq_mine), channel_id=1, source_target_pairs={{0,8},{1,9},{4,12},{5,13},{8,16},{9,17},{12,20},{13,21},{16,24},{1... | collective-permute-start | bytes 3145736 | tf_op jit(solution)/shard_map/ppermute | solution.py:427
  124.0 2.0 collective-permute-start.18
  124.1 2.6 %collective-permute-start.16 = (bf16[256,1024]{1,0:T(8,128)(2,1)S(1)}, bf16[256,1024]{1,0:T(8,128)(2,1)S(1)}, u32[]{:S(2)}, u32[]{:S(2)}) collective-permute-start(bf16[256,1024]{1,0:T(8,128)(2,1)S(1)} %get-tuple-element.78.refs_12_), channel_id=1, source_target_pairs={{0,4},{1,5},{2,6},{3,7},{4,0},{5,1},{6,2},{7,3},{8,12},{9,13},{10,... | collective-permute-start | bytes 1572872 | tf_op jit(solution)/shard_map/ppermute | solution.py:427
  124.6 2.8 %collective-permute-start.19 = (bf16[256,1024]{1,0:T(8,128)(2,1)S(1)}, bf16[256,1024]{1,0:T(8,128)(2,1)S(1)}, u32[]{:S(2)}, u32[]{:S(2)}) collective-permute-start(bf16[256,1024]{1,0:T(8,128)(2,1)S(1)} %get-tuple-element.75.refs_21_), channel_id=1, source_target_pairs={{0,4},{1,5},{2,6},{3,7},{4,0},{5,1},{6,2},{7,3},{8,12},{9,13},{10,... | collective-permute-start | bytes 1572872 | tf_op jit(solution)/shard_map/ppermute | solution.py:427
  124.8 3.4 %collective-permute-start.17 = (bf16[256,1024]{1,0:T(8,128)(2,1)S(1)}, bf16[256,1024]{1,0:T(8,128)(2,1)S(1)}, u32[]{:S(2)}, u32[]{:S(2)}) collective-permute-start(bf16[256,1024]{1,0:T(8,128)(2,1)S(1)} %get-tuple-element.76.refs_13_), channel_id=1, source_target_pairs={{0,4},{1,5},{2,6},{3,7},{4,0},{5,1},{6,2},{7,3},{8,12},{9,13},{10,... | collective-permute-start | bytes 1572872 | tf_op jit(solution)/shard_map/ppermute | solution.py:427
  135.6 6.4 %collective-permute-start.22 = (bf16[512,1024]{1,0:T(8,128)(2,1)S(1)}, bf16[512,1024]{1,0:T(8,128)(2,1)S(1)}, u32[]{:S(2)}, u32[]{:S(2)}) collective-permute-start(bf16[512,1024]{1,0:T(8,128)(2,1)S(1)} %get-tuple-element.48.a_mine.aq_mine), channel_id=1, source_target_pairs={{0,4},{1,5},{2,6},{3,7},{4,0},{5,1},{6,2},{7,3},{8,12},{9,13},{10,... | collective-permute-start | bytes 3145736 | tf_op jit(solution)/shard_map/ppermute | solution.py:427
  135.8 6.2 %collective-permute-start.21 = (bf16[512,1024]{1,0:T(8,128)(2,1)S(1)}, bf16[512,1024]{1,0:T(8,128)(2,1)S(1)}, u32[]{:S(2)}, u32[]{:S(2)}) collective-permute-start(bf16[512,1024]{1,0:T(8,128)(2,1)S(1)} %get-tuple-element.62.j_mine.jq_mine), channel_id=1, source_target_pairs={{0,4},{1,5},{2,6},{3,7},{4,0},{5,1},{6,2},{7,3},{8,12},{9,13},{10,... | collective-permute-start | bytes 3145736 | tf_op jit(solution)/shard_map/ppermute | solution.py:427
  136.2 5.8 %collective-permute-start.20 = (bf16[512,1024]{1,0:T(8,128)(2,1)S(1)}, bf16[512,1024]{1,0:T(8,128)(2,1)S(1)}, u32[]{:S(2)}, u32[]{:S(2)}) collective-permute-start(bf16[512,1024]{1,0:T(8,128)(2,1)S(1)} %collective-permute-done.13.c_mine), channel_id=1, source_target_pairs={{0,4},{1,5},{2,6},{3,7},{4,0},{5,1},{6,2},{7,3},{8,12},{9,13},{10,... | collective-permute-start | bytes 3145736 | tf_op jit(solution)/shard_map/ppermute | solution.py:427
  137.7 26.9 %collective-permute-start.25 = (bf16[512,1024]{1,0:T(8,128)(2,1)S(1)}, bf16[512,1024]{1,0:T(8,128)(2,1)S(1)}, u32[]{:S(2)}, u32[]{:S(2)}) collective-permute-start(bf16[512,1024]{1,0:T(8,128)(2,1)S(1)} %get-tuple-element.48.a_mine.aq_mine), channel_id=1, source_target_pairs={{0,8},{1,9},{4,12},{5,13},{8,16},{9,17},{12,20},{13,21},{16,24},{1... | collective-permute-start | bytes 3145736 | tf_op jit(solution)/shard_map/ppermute | solution.py:427
  152.7 11.9 %collective-permute-start.23 = (bf16[128,1024]{1,0:T(8,128)(2,1)S(1)}, bf16[128,1024]{1,0:T(8,128)(2,1)S(1)}, u32[]{:S(2)}, u32[]{:S(2)}) collective-permute-start(bf16[128,1024]{1,0:T(8,128)(2,1)S(1)} %get-tuple-element.49), channel_id=1, source_target_pairs={{0,3},{1,6},{4,2},{5,7},{8,11},{9,14},{12,10},{13,15},{16,19},{17,... | collective-permute-start | bytes 786440 | tf_op jit(solution)/shard_map/ppermute | solution.py:427
  164.7 16.7 %collective-permute-start.26 = (bf16[512,1024]{1,0:T(8,128)(2,1)S(1)}, bf16[512,1024]{1,0:T(8,128)(2,1)S(1)}, u32[]{:S(2)}, u32[]{:S(2)}) collective-permute-start(bf16[512,1024]{1,0:T(8,128)(2,1)S(1)} %collective-permute-done.25.a_mine), channel_id=1, source_target_pairs={{0,4},{1,5},{2,6},{3,7},{4,0},{5,1},{6,2},{7,3},{8,12},{9,13},{10,... | collective-permute-start | bytes 3145736 | tf_op jit(solution)/shard_map/ppermute | solution.py:427
  172.3 9.1 %collective-permute-start.24 = (bf16[128,1024]{1,0:T(8,128)(2,1)S(1)}, bf16[128,1024]{1,0:T(8,128)(2,1)S(1)}, u32[]{:S(2)}, u32[]{:S(2)}) collective-permute-start(bf16[128,1024]{1,0:T(8,128)(2,1)S(1)} %get-tuple-element.50), channel_id=1, source_target_pairs={{0,3},{1,6},{4,2},{5,7},{8,11},{9,14},{12,10},{13,15},{16,19},{17,... | collective-permute-start | bytes 786440 | tf_op jit(solution)/shard_map/ppermute | solution.py:427
  174.0 23.2 %collective-permute-start.29 = (bf16[512,1024]{1,0:T(8,128)(2,1)S(1)}, bf16[512,1024]{1,0:T(8,128)(2,1)S(1)}, u32[]{:S(2)}, u32[]{:S(2)}) collective-permute-start(bf16[512,1024]{1,0:T(8,128)(2,1)S(1)} %get-tuple-element.62.j_mine.jq_mine), channel_id=1, source_target_pairs={{0,8},{1,9},{4,12},{5,13},{8,16},{9,17},{12,20},{13,21},{16,24},{1... | collective-permute-start | bytes 3145736 | tf_op jit(solution)/shard_map/ppermute | solution.py:427
  183.3 26.2 %collective-permute-start.28 = (bf16[2,256,1024]{2,1,0:T(8,128)(2,1)S(1)}, bf16[2,256,1024]{2,1,0:T(8,128)(2,1)S(1)}, u32[]{:S(2)}, u32[]{:S(2)}) collective-permute-start(bf16[2,256,1024]{2,1,0:T(8,128)(2,1)S(1)} %get-tuple-element.56), channel_id=1, source_target_pairs={{0,1},{1,5},{4,0},{5,4},{8,9},{9,13},{12,8},{13,12},{16,17},{17,21... | collective-permute-start | bytes 3145736 | tf_op jit(solution)/shard_map/ppermute | solution.py:427
  188.6 17.6 %collective-permute-start.27 = (bf16[256,1024]{1,0:T(8,128)(2,1)S(1)}, bf16[256,1024]{1,0:T(8,128)(2,1)S(1)}, u32[]{:S(2)}, u32[]{:S(2)}) collective-permute-start(bf16[256,1024]{1,0:T(8,128)(2,1)S(1)} %get-tuple-element.55), channel_id=1, source_target_pairs={{0,3},{1,6},{4,2},{5,7},{8,11},{9,14},{12,10},{13,15},{16,19},{17,... | collective-permute-start | bytes 1572872 | tf_op jit(solution)/shard_map/ppermute | solution.py:427
  209.5 26.0 %collective-permute-start.30 = (bf16[256,1024]{1,0:T(8,128)(2,1)S(1)}, bf16[256,1024]{1,0:T(8,128)(2,1)S(1)}, u32[]{:S(2)}, u32[]{:S(2)}) collective-permute-start(bf16[256,1024]{1,0:T(8,128)(2,1)S(1)} %get-tuple-element.65), channel_id=1, source_target_pairs={{0,3},{1,6},{4,2},{5,7},{8,11},{9,14},{12,10},{13,15},{16,19},{17,... | collective-permute-start | bytes 1572872 | tf_op jit(solution)/shard_map/ppermute | solution.py:427
  209.7 25.7 %collective-permute-start.31 = (bf16[256,1024]{1,0:T(8,128)(2,1)S(1)}, bf16[256,1024]{1,0:T(8,128)(2,1)S(1)}, u32[]{:S(2)}, u32[]{:S(2)}) collective-permute-start(bf16[256,1024]{1,0:T(8,128)(2,1)S(1)} %get-tuple-element.67), channel_id=1, source_target_pairs={{0,1},{1,5},{4,0},{5,4},{8,9},{9,13},{12,8},{13,12},{16,17},{17,21... | collective-permute-start | bytes 1572872 | tf_op jit(solution)/shard_map/ppermute | solution.py:427

commit v5 on v4

--- a/solution.py
+++ b/solution.py
@@ -299,7 +299,8 @@
 
 
 def front_kernel(plan, stride, c_mine, c_theirs, j_mine, j_theirs, a_mine, a_theirs, cq_mine, *refs):
-    far, near = refs[: plan.half], refs[plan.half : plan.half + plan.half // 2]
+    pairs = plan.half // 2
+    far, near = refs[:pairs], refs[pairs : 2 * pairs]
     f_ref, x1_ref, r_ref, cp, jq, aq, ah, ch, x1, r, full, u, f, sems = refs[-14:]
     place, copies = Place(plan), Copies(sems)
     loads = [
@@ -374,15 +375,14 @@
 
 def home_kernel(plan, *refs):
     half, pairs = plan.half, plan.half // 2
-    c_far, a_far, ca_near = refs[:half], refs[half : half + pairs], refs[half + pairs : 2 * half]
-    outs, (held, sems) = refs[2 * half : 2 * half + 2], refs[2 * half + 2 :]
+    c_far, a_far, ca_near = [refs[i * pairs : (i + 1) * pairs] for i in range(3)]
+    outs, (held, sems) = refs[3 * pairs : 3 * pairs + 2], refs[3 * pairs + 2 :]
     rows = held.shape[2]
-    part = rows // 2
     waits = []
     for k, which in enumerate(home_blocks(plan, rows)):
         c, a = held.at[k, 0], held.at[k, 1]
         for i in range(pairs):
-            far = [(c_far[i], c.at[pl.ds(0, part), :], 0), (c_far[pairs + i], c.at[pl.ds(part, part), :], 0), (a_far[i], a, 1)]
+            far = [(c_far[i], c, 0), (a_far[i], a, 1)]
             near = [(ca_near[i].at[0], c, 0), (ca_near[i].at[1], a, 1)]
             for owner, moves in ((i, far), (pairs + i, near)):
                 for source, target, matrix in moves:
@@ -487,19 +487,19 @@
 
     *c_pieces, f, x1, r = kernel(
         front_kernel,
-        [*[bf16(rows // 2, n)] * half, *blocks, part, full, full],
+        [*blocks, *blocks, part, full, full],
         [c_next, c_next_swap, j_new, j_swap, a_new, a_swap, c_new],
         [square] * 3 + [slab] * 2 + [square] * 3 + [slab] * 2,
         static=(2,),
     )
-    c_far, c_near = send_home(c_pieces[:half], far * 2), c_pieces[half:]
+    c_far, c_near = send_home(c_pieces[: half // 2], far), c_pieces[half // 2 :]
     j_next = send(after(j_new, a_next), plan.next)
-    a_next = after(a_next, f, *c_far[: half // 2])
+    a_next = after(a_next, f, *c_far)
     a_next_swap = swap(a_next)
     a_pieces = kernel(
         trans_kernel,
         [*blocks, *[bf16(2, rows, n) for _ in pairs]],
-        [a_next, after(a_next_swap, *c_far), f, a_new, *c_near],
+        [a_next, a_next_swap, f, a_new, *c_near],
         [square] + [slab] * 3,
         static=(2,),
     )

time: 241 us -> 239 us (level)
    ppermute x32 -> x31, starting transfers between devices: 65.3 us -> 64.7 us  [send(): return lax.ppermute(x, AXES, routes)]
    ppermute x32 -> x31, waiting for transfers between devices: 121 us -> 121 us  [send(): return lax.ppermute(x, AXES, routes)]
  transfers between devices with their start and end apart: 32 -> 31, of which waited for: 15 -> 12; matrix products, arithmetic and copies ran while one was open for 3% -> 3% of each run, Pallas kernels for 17% -> 17%
where the time goes in v5:
time: 239 us; the launch traced here: 237 us
  waiting for transfers between devices  121 us (51%)
  starting transfers between devices  64.7 us (27%)
  Pallas kernels  41 us (17%)
  other arithmetic  8.45 us (4%)
    ppermute x31, waiting for transfers between devices, send(): return lax.ppermute(x, AXES, routes)  121 us
    ppermute x31, starting transfers between devices, send(): return lax.ppermute(x, AXES, routes)  64.7 us
    pallas_call x8, Pallas kernels, call(): pl.pallas_call(kernel, out_shape=list(out_shapes), in_specs=[HBM] * len(o...  41 us
  transfers between devices with their start and end apart: 31, of which 12 were waited for; matrix products, arithmetic and copies ran while one was open for 3% of the time, Pallas kernels for 17%

profile of v5, /device:TPU:10, one launch (start us, length us, event | category | flops | bytes accessed | tf_op | source)
XLA Modules:
  0.0 236.9 jit_solution(4511434670111677471)
XLA Ops:
  0.7 2.1 select_bitcast_fusion.1
  2.8 0.7 collective-permute-start.1
  3.5 4.9 %collective-permute-start = (bf16[256,1024]{1,0:T(8,128)(2,1)S(1)}, bf16[256,1024]{1,0:T(8,128)(2,1)}, u32[]{:S(2)}, u32[]{:S(2)}) collective-permute-start(bf16[256,1024]{1,0:T(8,128)(2,1)S(1)} %get-tuple-element.69), channel_id=1, source_target_pairs={{2,0},{6,5},{10,8},{14,13},{18,16},{22,21},{26,24},{30,29},{29,31}... | collective-permute-start | bytes 1572872 | tf_op jit(solution)/shard_map/ppermute | solution.py:427
  8.4 1.3 fusion
  9.8 2.6 %collective-permute-start.3 = (bf16[3,256,1024]{2,1,0:T(8,128)(2,1)}, bf16[3,256,1024]{2,1,0:T(8,128)(2,1)S(1)}, u32[]{:S(2)}, u32[]{:S(2)}) collective-permute-start(bf16[3,256,1024]{2,1,0:T(8,128)(2,1)} %fusion), channel_id=1, source_target_pairs={{1,0},{4,5},{9,8},{12,13},{17,16},{20,21},{25,24},{28,29},{0,1},{5... | collective-permute-start | bytes 4718600 | tf_op jit(solution)/shard_map/ppermute | solution.py:427
  12.3 18.2 %collective-permute-done = bf16[256,1024]{1,0:T(8,128)(2,1)} collective-permute-done((bf16[256,1024]{1,0:T(8,128)(2,1)S(1)}, bf16[256,1024]{1,0:T(8,128)(2,1)}, u32[]{:S(2)}, u32[]{:S(2)}) %collective-permute-start) | collective-permute-done | bytes 524320 | tf_op jit(solution)/shard_map/ppermute | solution.py:427
  30.6 1.8 collective-permute-start.2
  32.4 1.1 pad_maximum_fusion
  33.5 1.6 collective-permute-start.8
  35.1 1.3 collective-permute-start.9
  36.4 9.2 %collective-permute-start.6 = (bf16[2,256,1024]{2,1,0:T(8,128)(2,1)}, bf16[2,256,1024]{2,1,0:T(8,128)(2,1)}, u32[]{:S(2)}, u32[]{:S(2)}) collective-permute-start(bf16[2,256,1024]{2,1,0:T(8,128)(2,1)} %pad_maximum_fusion), channel_id=1, source_target_pairs={{2,0},{6,5},{10,8},{14,13},{18,16},{22,21},{26,24},{30,29},{29,31}... | collective-permute-start | bytes 3145736 | tf_op jit(solution)/shard_map/ppermute | solution.py:427
  45.6 36.7 %collective-permute-done.9 = bf16[256,1024]{1,0:T(8,128)(2,1)S(1)} collective-permute-done((bf16[256,1024]{1,0:T(8,128)(2,1)S(1)}, bf16[256,1024]{1,0:T(8,128)(2,1)S(1)}, u32[]{:S(2)}, u32[]{:S(2)}) %collective-permute-start.9) | collective-permute-done | bytes 524320 | tf_op jit(solution)/shard_map/ppermute | solution.py:427
  82.3 1.3 collective-permute-start.7
  83.6 1.2 broadcast_select_fusion.1.refs_5_
  84.8 2.8 %collective-permute-start.11 = (bf16[2,256,1024]{2,1,0:T(8,128)(2,1)S(1)}, bf16[2,256,1024]{2,1,0:T(8,128)(2,1)}, u32[]{:S(2)}, u32[]{:S(2)}) collective-permute-start(bf16[2,256,1024]{2,1,0:T(8,128)(2,1)S(1)} %broadcast_select_fusion.1.refs_5_), channel_id=1, source_target_pairs={{0,4},{1,5},{2,6},{3,7},{4,0},{5,1},{6,2},{7,3},{8,12},{9,13},{10,... | collective-permute-start | bytes 3145736 | tf_op jit(solution)/shard_map/ppermute | solution.py:427
  87.7 1.6 broadcast_select_fusion.refs_0_.refs_8_.refs_16_
  89.3 0.5 collective-permute-start.4
  89.8 3.9 %collective-permute-done.7 = bf16[256,1024]{1,0:T(8,128)(2,1)} collective-permute-done((bf16[256,1024]{1,0:T(8,128)(2,1)}, bf16[256,1024]{1,0:T(8,128)(2,1)}, u32[]{:S(2)}, u32[]{:S(2)}) %collective-permute-start.7) | collective-permute-done | bytes 524320 | tf_op jit(solution)/shard_map/ppermute | solution.py:427
  93.7 1.2 broadcast_select_fusion.2.refs_4_
  94.8 0.9 collective-permute-start.10
  95.8 1.3 collective-permute-start.15
  97.1 1.3 collective-permute-start.14
  98.4 11.5 %shard_map.41 = (bf16[512,1024]{1,0:T(8,128)(2,1)S(1)}, bf16[1024,1024]{1,0:T(8,128)(2,1)S(1)}, bf16[1024,1024]{1,0:T(8,128)(2,1)S(1)}, bf16[1024,1024]{1,0:T(8,128)(2,1)S(1)}, bf16[512,1024]{1,0:T(8,128)(2,1)S(1)}) custom-call(bf16[3,256,1024]{2,1,0:T(8,128)(2,1)S(1)} %broadcast_select_fusion.refs_0_.refs_8_.refs_16_, ...), custom_call_target="tpu_custom_call" | custom-call | flops 1 | bytes 1 | tf_op jit(solution)/shard_map/pallas_call | solution.py:82
  110.0 3.4 %collective-permute-start.13 = (bf16[512,1024]{1,0:T(8,128)(2,1)S(1)}, bf16[512,1024]{1,0:T(8,128)(2,1)S(1)}, u32[]{:S(2)}, u32[]{:S(2)}) collective-permute-start(bf16[512,1024]{1,0:T(8,128)(2,1)S(1)} %get-tuple-element.35.cq_mine), channel_id=1, source_target_pairs={{0,8},{1,9},{4,12},{5,13},{8,16},{9,17},{12,20},{13,21},{16,24},{1... | collective-permute-start | bytes 3145736 | tf_op jit(solution)/shard_map/ppermute | solution.py:427
  113.4 10.5 %collective-permute-done.14 = bf16[2,256,1024]{2,1,0:T(8,128)(2,1)S(1)} collective-permute-done((bf16[2,256,1024]{2,1,0:T(8,128)(2,1)}, bf16[2,256,1024]{2,1,0:T(8,128)(2,1)S(1)}, u32[]{:S(2)}, u32[]{:S(2)}) %collective-permute-start.14) | collective-permute-done | bytes 1048608 | tf_op jit(solution)/shard_map/ppermute | solution.py:427
  124.1 0.5 collective-permute-start.16
  124.8 0.4 collective-permute-start.17
  125.2 0.7 collective-permute-done.18.refs_22_
  126.0 0.7 collective-permute-done.16.refs_14_
  126.7 0.7 collective-permute-done.19.refs_23_
  127.5 0.7 collective-permute-done.17.refs_15_
  128.2 7.4 %shard_map.42 = (bf16[512,1024]{1,0:T(8,128)(2,1)S(1)}, bf16[512,1024]{1,0:T(8,128)(2,1)S(1)}) custom-call(bf16[512,1024]{1,0:T(8,128)(2,1)S(1)} %get-tuple-element.37.f_ref, bf16[1024,1024]{1,0:T(8,128)(2,1)S(1)} %get-tuple-element.38.jq_ref, bf16[1024,1024]{1,0:T(8,128)(2,1)S(1)} %get-tuple-element.39.x1_ref, bf16[1024,1024]{1,0:T(8,128)(2,1)} %copy-done, ...), custom_call_target="tpu_custom_call" | custom-call | flops 1 | bytes 1 | tf_op jit(solution)/shard_map/pallas_call | solution.py:82
  136.2 1.5 collective-permute-start.20
  137.7 4.3 %collective-permute-start.24 = (bf16[512,1024]{1,0:T(8,128)(2,1)S(1)}, bf16[512,1024]{1,0:T(8,128)(2,1)S(1)}, u32[]{:S(2)}, u32[]{:S(2)}) collective-permute-start(bf16[512,1024]{1,0:T(8,128)(2,1)S(1)} %get-tuple-element.46.a_mine.aq_mine), channel_id=1, source_target_pairs={{0,8},{1,9},{4,12},{5,13},{8,16},{9,17},{12,20},{13,21},{16,24},{1... | collective-permute-start | bytes 3145736 | tf_op jit(solution)/shard_map/ppermute | solution.py:427
  142.0 10.7 %shard_map.43 = (bf16[256,1024]{1,0:T(8,128)(2,1)S(1)}, bf16[256,1024]{1,0:T(8,128)(2,1)S(1)}, bf16[512,1024]{1,0:T(8,128)(2,1)S(1)}, bf16[1024,1024]{1,0:T(8,128)(2,1)S(1)}, bf16[1024,1024]{1,0:T(8,128)(2,1)S(1)}) custom-call(bf16[512,1024]{1,0:T(8,128)(2,1)S(1)} %collective-permute-done.13.c_mine, bf16[512,1024]{1,0:T(8,128)(2,1)S(1)} %collective-permute-done.20.c_theirs, ...), custom_call_target="tpu_custom_call" | custom-call | flops 1 | bytes 1 | tf_op jit(solution)/shard_map/pallas_call | solution.py:82
  152.8 11.9 %collective-permute-done.24.a_mine = bf16[512,1024]{1,0:T(8,128)(2,1)S(1)} collective-permute-done((bf16[512,1024]{1,0:T(8,128)(2,1)S(1)}, bf16[512,1024]{1,0:T(8,128)(2,1)S(1)}, u32[]{:S(2)}, u32[]{:S(2)}) %collective-permute-start.24) | collective-permute-done | bytes 1048608 | tf_op jit(solution)/shard_map/ppermute | solution.py:427
  164.7 16.0 %collective-permute-start.25 = (bf16[512,1024]{1,0:T(8,128)(2,1)S(1)}, bf16[512,1024]{1,0:T(8,128)(2,1)S(1)}, u32[]{:S(2)}, u32[]{:S(2)}) collective-permute-start(bf16[512,1024]{1,0:T(8,128)(2,1)S(1)} %collective-permute-done.24.a_mine), channel_id=1, source_target_pairs={{0,4},{1,5},{2,6},{3,7},{4,0},{5,1},{6,2},{7,3},{8,12},{9,13},{10,... | collective-permute-start | bytes 3145736 | tf_op jit(solution)/shard_map/ppermute | solution.py:427
  180.7 2.5 %collective-permute-start.28 = (bf16[512,1024]{1,0:T(8,128)(2,1)S(1)}, bf16[512,1024]{1,0:T(8,128)(2,1)S(1)}, u32[]{:S(2)}, u32[]{:S(2)}) collective-permute-start(bf16[512,1024]{1,0:T(8,128)(2,1)S(1)} %get-tuple-element.58.j_mine.jq_mine), channel_id=1, source_target_pairs={{0,8},{1,9},{4,12},{5,13},{8,16},{9,17},{12,20},{13,21},{16,24},{1... | collective-permute-start | bytes 3145736 | tf_op jit(solution)/shard_map/ppermute | solution.py:427
  183.2 1.9 shard_map.44
  185.4 1.7 collective-permute-start.26
  187.1 4.7 %shard_map.46.h_ref = bf16[512,1024]{1,0:T(8,128)(2,1)S(1)} custom-call(bf16[512,1024]{1,0:T(8,128)(2,1)S(1)} %collective-permute-done.24.a_mine, bf16[512,1024]{1,0:T(8,128)(2,1)S(1)} %collective-permute-done.25.a_theirs, bf16[512,1024]{1,0:T(8,128)(2,1)S(1)} %get-tuple-element.58.j_mine.jq_mine, bf16[512,1024]{1,0:T(8,128)(2,1)S(1)} %collective-permute-done.21.j_theirs, ...), custom_call_target="tpu_custom_call" | custom-call | flops 1 | bytes 1 | tf_op jit(solution)/shard_map/pallas_call | solution.py:82
  191.8 15.9 %collective-permute-done.28.jp_mine = bf16[512,1024]{1,0:T(8,128)(2,1)S(1)} collective-permute-done((bf16[512,1024]{1,0:T(8,128)(2,1)S(1)}, bf16[512,1024]{1,0:T(8,128)(2,1)S(1)}, u32[]{:S(2)}, u32[]{:S(2)}) %collective-permute-start.28) | collective-permute-done | bytes 1048608 | tf_op jit(solution)/shard_map/ppermute | solution.py:427
  207.7 1.9 shard_map.47
  209.5 2.4 %collective-permute-start.29 = (bf16[256,1024]{1,0:T(8,128)(2,1)S(1)}, bf16[256,1024]{1,0:T(8,128)(2,1)S(1)}, u32[]{:S(2)}, u32[]{:S(2)}) collective-permute-start(bf16[256,1024]{1,0:T(8,128)(2,1)S(1)} %get-tuple-element.61), channel_id=1, source_target_pairs={{0,3},{1,6},{4,2},{5,7},{8,11},{9,14},{12,10},{13,15},{16,19},{17,... | collective-permute-start | bytes 1572872 | tf_op jit(solution)/shard_map/ppermute | solution.py:427
  211.9 0.6 collective-permute-start.30
  212.5 1.7 shard_map.45
  214.2 21.2 %collective-permute-done.29.refs_0_ = bf16[256,1024]{1,0:T(8,128)(2,1)S(1)} collective-permute-done((bf16[256,1024]{1,0:T(8,128)(2,1)S(1)}, bf16[256,1024]{1,0:T(8,128)(2,1)S(1)}, u32[]{:S(2)}, u32[]{:S(2)}) %collective-permute-start.29) | collective-permute-done | bytes 524320 | tf_op jit(solution)/shard_map/ppermute | solution.py:427
  235.4 1.3 shard_map.48
  (38 shorter events, 1.5 us)
Async XLA Ops:
  0.6 7.8 %copy-start.1 = (bf16[3,1,256,1024]{3,2,1,0:T(8,128)(2,1)S(1)}, bf16[3,1,256,1024]{3,2,1,0:T(8,128)(2,1)}, u32[]{:S(2)}) copy-start(bf16[3,1,256,1024]{3,2,1,0:T(8,128)(2,1)} %param.3) | copy-start | bytes 4718596
  0.6 7.8 %copy-start.2 = (bf16[3,1,256,1024]{3,2,1,0:T(8,128)(2,1)S(1)}, bf16[3,1,256,1024]{3,2,1,0:T(8,128)(2,1)}, u32[]{:S(2)}) copy-start(bf16[3,1,256,1024]{3,2,1,0:T(8,128)(2,1)} %param.2) | copy-start | bytes 4718596
  2.8 9.5 %collective-permute-start.1 = (bf16[256,1024]{1,0:T(8,128)(2,1)S(1)}, bf16[256,1024]{1,0:T(8,128)(2,1)S(1)}, u32[]{:S(2)}, u32[]{:S(2)}) collective-permute-start(bf16[256,1024]{1,0:T(8,128)(2,1)S(1)} %get-tuple-element.69), channel_id=1, source_target_pairs={{3,0},{7,5},{11,8},{15,13},{19,16},{23,21},{27,24},{31,29},{28,31}... | collective-permute-start | bytes 1572872 | tf_op jit(solution)/shard_map/ppermute | solution.py:427
  3.5 27.0 %collective-permute-start = (bf16[256,1024]{1,0:T(8,128)(2,1)S(1)}, bf16[256,1024]{1,0:T(8,128)(2,1)}, u32[]{:S(2)}, u32[]{:S(2)}) collective-permute-start(bf16[256,1024]{1,0:T(8,128)(2,1)S(1)} %get-tuple-element.69), channel_id=1, source_target_pairs={{2,0},{6,5},{10,8},{14,13},{18,16},{22,21},{26,24},{30,29},{29,31}... | collective-permute-start | bytes 1572872 | tf_op jit(solution)/shard_map/ppermute | solution.py:427
  9.8 77.8 %collective-permute-start.3 = (bf16[3,256,1024]{2,1,0:T(8,128)(2,1)}, bf16[3,256,1024]{2,1,0:T(8,128)(2,1)S(1)}, u32[]{:S(2)}, u32[]{:S(2)}) collective-permute-start(bf16[3,256,1024]{2,1,0:T(8,128)(2,1)} %fusion), channel_id=1, source_target_pairs={{1,0},{4,5},{9,8},{12,13},{17,16},{20,21},{25,24},{28,29},{0,1},{5... | collective-permute-start | bytes 4718600 | tf_op jit(solution)/shard_map/ppermute | solution.py:427
  30.6 57.1 %collective-permute-start.2 = (bf16[3,256,1024]{2,1,0:T(8,128)(2,1)}, bf16[3,256,1024]{2,1,0:T(8,128)(2,1)}, u32[]{:S(2)}, u32[]{:S(2)}) collective-permute-start(bf16[3,256,1024]{2,1,0:T(8,128)(2,1)} %fusion), channel_id=1, source_target_pairs={{4,12},{12,20},{20,28},{27,19},{19,11},{11,3}} | collective-permute-start | bytes 4718600 | tf_op jit(solution)/shard_map/ppermute | solution.py:427
  33.5 50.1 %collective-permute-start.8 = (bf16[2,256,1024]{2,1,0:T(8,128)(2,1)}, bf16[2,256,1024]{2,1,0:T(8,128)(2,1)}, u32[]{:S(2)}, u32[]{:S(2)}) collective-permute-start(bf16[2,256,1024]{2,1,0:T(8,128)(2,1)} %pad_maximum_fusion), channel_id=1, source_target_pairs={{3,0},{7,5},{11,8},{15,13},{19,16},{23,21},{27,24},{31,29},{28,31}... | collective-permute-start | bytes 3145736 | tf_op jit(solution)/shard_map/ppermute | solution.py:427
  35.1 47.2 %collective-permute-start.9 = (bf16[256,1024]{1,0:T(8,128)(2,1)S(1)}, bf16[256,1024]{1,0:T(8,128)(2,1)S(1)}, u32[]{:S(2)}, u32[]{:S(2)}) collective-permute-start(bf16[256,1024]{1,0:T(8,128)(2,1)S(1)} %collective-permute-done.1.refs_9_), channel_id=1, source_target_pairs={{0,1},{5,12},{8,9},{13,20},{16,17},{21,28},{24,25},{31,30},{26,19}... | collective-permute-start | bytes 1572872 | tf_op jit(solution)/shard_map/ppermute | solution.py:427
  36.4 57.3 %collective-permute-start.6 = (bf16[2,256,1024]{2,1,0:T(8,128)(2,1)}, bf16[2,256,1024]{2,1,0:T(8,128)(2,1)}, u32[]{:S(2)}, u32[]{:S(2)}) collective-permute-start(bf16[2,256,1024]{2,1,0:T(8,128)(2,1)} %pad_maximum_fusion), channel_id=1, source_target_pairs={{2,0},{6,5},{10,8},{14,13},{18,16},{22,21},{26,24},{30,29},{29,31}... | collective-permute-start | bytes 3145736 | tf_op jit(solution)/shard_map/ppermute | solution.py:427
  82.3 1.3 copy-start.3
  82.3 11.4 %collective-permute-start.7 = (bf16[256,1024]{1,0:T(8,128)(2,1)}, bf16[256,1024]{1,0:T(8,128)(2,1)}, u32[]{:S(2)}, u32[]{:S(2)}) collective-permute-start(bf16[256,1024]{1,0:T(8,128)(2,1)} %collective-permute-done), channel_id=1, source_target_pairs={{0,1},{5,12},{8,9},{13,20},{16,17},{21,28},{24,25},{31,30},{26,19}... | collective-permute-start | bytes 1572872 | tf_op jit(solution)/shard_map/ppermute | solution.py:427
  84.8 12.3 %collective-permute-start.11 = (bf16[2,256,1024]{2,1,0:T(8,128)(2,1)S(1)}, bf16[2,256,1024]{2,1,0:T(8,128)(2,1)}, u32[]{:S(2)}, u32[]{:S(2)}) collective-permute-start(bf16[2,256,1024]{2,1,0:T(8,128)(2,1)S(1)} %broadcast_select_fusion.1.refs_5_), channel_id=1, source_target_pairs={{0,4},{1,5},{2,6},{3,7},{4,0},{5,1},{6,2},{7,3},{8,12},{9,13},{10,... | collective-permute-start | bytes 3145736 | tf_op jit(solution)/shard_map/ppermute | solution.py:427
  87.6 10.8 %collective-permute-start.5 = (bf16[3,256,1024]{2,1,0:T(8,128)(2,1)S(1)}, bf16[3,256,1024]{2,1,0:T(8,128)(2,1)S(1)}, u32[]{:S(2)}, u32[]{:S(2)}) collective-permute-start(bf16[3,256,1024]{2,1,0:T(8,128)(2,1)S(1)} %collective-permute-done.3.refs_1_.refs_9_.refs_17_), channel_id=1, source_target_pairs={{0,4},{1,5},{2,6},{3,7},{4,0},{5,1},{6,2},{7,3},{8,12},{9,13},{10,... | collective-permute-start | bytes 4718600 | tf_op jit(solution)/shard_map/ppermute | solution.py:427
  89.3 9.1 %collective-permute-start.4 = (bf16[3,256,1024]{2,1,0:T(8,128)(2,1)S(1)}, bf16[3,256,1024]{2,1,0:T(8,128)(2,1)S(1)}, u32[]{:S(2)}, u32[]{:S(2)}) collective-permute-start(bf16[3,256,1024]{2,1,0:T(8,128)(2,1)S(1)} %broadcast_select_fusion.refs_0_.refs_8_.refs_16_), channel_id=1, source_target_pairs={{0,4},{1,5},{2,6},{3,7},{4,0},{5,1},{6,2},{7,3},{8,12},{9,13},{10,... | collective-permute-start | bytes 4718600 | tf_op jit(solution)/shard_map/ppermute | solution.py:427
  93.7 2.1 collective-permute-start.12
  94.8 3.6 %collective-permute-start.10 = (bf16[2,256,1024]{2,1,0:T(8,128)(2,1)S(1)}, bf16[2,256,1024]{2,1,0:T(8,128)(2,1)S(1)}, u32[]{:S(2)}, u32[]{:S(2)}) collective-permute-start(bf16[2,256,1024]{2,1,0:T(8,128)(2,1)S(1)} %broadcast_select_fusion.2.refs_4_), channel_id=1, source_target_pairs={{0,4},{1,5},{2,6},{3,7},{4,0},{5,1},{6,2},{7,3},{8,12},{9,13},{10,... | collective-permute-start | bytes 3145736 | tf_op jit(solution)/shard_map/ppermute | solution.py:427
  95.8 17.6 %collective-permute-start.15 = (bf16[2,256,1024]{2,1,0:T(8,128)(2,1)}, bf16[2,256,1024]{2,1,0:T(8,128)(2,1)S(1)}, u32[]{:S(2)}, u32[]{:S(2)}) collective-permute-start(bf16[2,256,1024]{2,1,0:T(8,128)(2,1)} %collective-permute-done.8), channel_id=1, source_target_pairs={{0,1},{5,12},{8,9},{13,20},{16,17},{21,28},{24,25},{31,30},{26,19}... | collective-permute-start | bytes 3145736 | tf_op jit(solution)/shard_map/ppermute | solution.py:427
  97.1 26.8 %collective-permute-start.14 = (bf16[2,256,1024]{2,1,0:T(8,128)(2,1)}, bf16[2,256,1024]{2,1,0:T(8,128)(2,1)S(1)}, u32[]{:S(2)}, u32[]{:S(2)}) collective-permute-start(bf16[2,256,1024]{2,1,0:T(8,128)(2,1)} %collective-permute-done.6), channel_id=1, source_target_pairs={{0,1},{5,12},{8,9},{13,20},{16,17},{21,28},{24,25},{31,30},{26,19}... | collective-permute-start | bytes 3145736 | tf_op jit(solution)/shard_map/ppermute | solution.py:427
  110.0 14.7 %copy-start = (bf16[1024,1024]{1,0:T(8,128)(2,1)}, bf16[1024,1024]{1,0:T(8,128)(2,1)S(1)}, u32[]{:S(2)}) copy-start(bf16[1024,1024]{1,0:T(8,128)(2,1)S(1)} %get-tuple-element.40.r_ref) | copy-start | bytes 6291460
  110.0 26.2 %collective-permute-start.13 = (bf16[512,1024]{1,0:T(8,128)(2,1)S(1)}, bf16[512,1024]{1,0:T(8,128)(2,1)S(1)}, u32[]{:S(2)}, u32[]{:S(2)}) collective-permute-start(bf16[512,1024]{1,0:T(8,128)(2,1)S(1)} %get-tuple-element.35.cq_mine), channel_id=1, source_target_pairs={{0,8},{1,9},{4,12},{5,13},{8,16},{9,17},{12,20},{13,21},{16,24},{1... | collective-permute-start | bytes 3145736 | tf_op jit(solution)/shard_map/ppermute | solution.py:427
  124.0 2.0 collective-permute-start.18
  124.1 2.6 %collective-permute-start.16 = (bf16[256,1024]{1,0:T(8,128)(2,1)S(1)}, bf16[256,1024]{1,0:T(8,128)(2,1)S(1)}, u32[]{:S(2)}, u32[]{:S(2)}) collective-permute-start(bf16[256,1024]{1,0:T(8,128)(2,1)S(1)} %get-tuple-element.74.refs_12_), channel_id=1, source_target_pairs={{0,4},{1,5},{2,6},{3,7},{4,0},{5,1},{6,2},{7,3},{8,12},{9,13},{10,... | collective-permute-start | bytes 1572872 | tf_op jit(solution)/shard_map/ppermute | solution.py:427
  124.6 2.8 %collective-permute-start.19 = (bf16[256,1024]{1,0:T(8,128)(2,1)S(1)}, bf16[256,1024]{1,0:T(8,128)(2,1)S(1)}, u32[]{:S(2)}, u32[]{:S(2)}) collective-permute-start(bf16[256,1024]{1,0:T(8,128)(2,1)S(1)} %get-tuple-element.71.refs_21_), channel_id=1, source_target_pairs={{0,4},{1,5},{2,6},{3,7},{4,0},{5,1},{6,2},{7,3},{8,12},{9,13},{10,... | collective-permute-start | bytes 1572872 | tf_op jit(solution)/shard_map/ppermute | solution.py:427
  124.8 3.4 %collective-permute-start.17 = (bf16[256,1024]{1,0:T(8,128)(2,1)S(1)}, bf16[256,1024]{1,0:T(8,128)(2,1)S(1)}, u32[]{:S(2)}, u32[]{:S(2)}) collective-permute-start(bf16[256,1024]{1,0:T(8,128)(2,1)S(1)} %get-tuple-element.72.refs_13_), channel_id=1, source_target_pairs={{0,4},{1,5},{2,6},{3,7},{4,0},{5,1},{6,2},{7,3},{8,12},{9,13},{10,... | collective-permute-start | bytes 1572872 | tf_op jit(solution)/shard_map/ppermute | solution.py:427
  135.6 6.4 %collective-permute-start.22 = (bf16[512,1024]{1,0:T(8,128)(2,1)S(1)}, bf16[512,1024]{1,0:T(8,128)(2,1)S(1)}, u32[]{:S(2)}, u32[]{:S(2)}) collective-permute-start(bf16[512,1024]{1,0:T(8,128)(2,1)S(1)} %get-tuple-element.46.a_mine.aq_mine), channel_id=1, source_target_pairs={{0,4},{1,5},{2,6},{3,7},{4,0},{5,1},{6,2},{7,3},{8,12},{9,13},{10,... | collective-permute-start | bytes 3145736 | tf_op jit(solution)/shard_map/ppermute | solution.py:427
  135.8 6.2 %collective-permute-start.21 = (bf16[512,1024]{1,0:T(8,128)(2,1)S(1)}, bf16[512,1024]{1,0:T(8,128)(2,1)S(1)}, u32[]{:S(2)}, u32[]{:S(2)}) collective-permute-start(bf16[512,1024]{1,0:T(8,128)(2,1)S(1)} %get-tuple-element.58.j_mine.jq_mine), channel_id=1, source_target_pairs={{0,4},{1,5},{2,6},{3,7},{4,0},{5,1},{6,2},{7,3},{8,12},{9,13},{10,... | collective-permute-start | bytes 3145736 | tf_op jit(solution)/shard_map/ppermute | solution.py:427
  136.2 5.8 %collective-permute-start.20 = (bf16[512,1024]{1,0:T(8,128)(2,1)S(1)}, bf16[512,1024]{1,0:T(8,128)(2,1)S(1)}, u32[]{:S(2)}, u32[]{:S(2)}) collective-permute-start(bf16[512,1024]{1,0:T(8,128)(2,1)S(1)} %collective-permute-done.13.c_mine), channel_id=1, source_target_pairs={{0,4},{1,5},{2,6},{3,7},{4,0},{5,1},{6,2},{7,3},{8,12},{9,13},{10,... | collective-permute-start | bytes 3145736 | tf_op jit(solution)/shard_map/ppermute | solution.py:427
  137.7 26.9 %collective-permute-start.24 = (bf16[512,1024]{1,0:T(8,128)(2,1)S(1)}, bf16[512,1024]{1,0:T(8,128)(2,1)S(1)}, u32[]{:S(2)}, u32[]{:S(2)}) collective-permute-start(bf16[512,1024]{1,0:T(8,128)(2,1)S(1)} %get-tuple-element.46.a_mine.aq_mine), channel_id=1, source_target_pairs={{0,8},{1,9},{4,12},{5,13},{8,16},{9,17},{12,20},{13,21},{16,24},{1... | collective-permute-start | bytes 3145736 | tf_op jit(solution)/shard_map/ppermute | solution.py:427
  152.7 11.9 %collective-permute-start.23 = (bf16[256,1024]{1,0:T(8,128)(2,1)S(1)}, bf16[256,1024]{1,0:T(8,128)(2,1)S(1)}, u32[]{:S(2)}, u32[]{:S(2)}) collective-permute-start(bf16[256,1024]{1,0:T(8,128)(2,1)S(1)} %get-tuple-element.47), channel_id=1, source_target_pairs={{0,3},{1,6},{4,2},{5,7},{8,11},{9,14},{12,10},{13,15},{16,19},{17,... | collective-permute-start | bytes 1572872 | tf_op jit(solution)/shard_map/ppermute | solution.py:427
  164.7 18.5 %collective-permute-start.25 = (bf16[512,1024]{1,0:T(8,128)(2,1)S(1)}, bf16[512,1024]{1,0:T(8,128)(2,1)S(1)}, u32[]{:S(2)}, u32[]{:S(2)}) collective-permute-start(bf16[512,1024]{1,0:T(8,128)(2,1)S(1)} %collective-permute-done.24.a_mine), channel_id=1, source_target_pairs={{0,4},{1,5},{2,6},{3,7},{4,0},{5,1},{6,2},{7,3},{8,12},{9,13},{10,... | collective-permute-start | bytes 3145736 | tf_op jit(solution)/shard_map/ppermute | solution.py:427
  180.7 26.9 %collective-permute-start.28 = (bf16[512,1024]{1,0:T(8,128)(2,1)S(1)}, bf16[512,1024]{1,0:T(8,128)(2,1)S(1)}, u32[]{:S(2)}, u32[]{:S(2)}) collective-permute-start(bf16[512,1024]{1,0:T(8,128)(2,1)S(1)} %get-tuple-element.58.j_mine.jq_mine), channel_id=1, source_target_pairs={{0,8},{1,9},{4,12},{5,13},{8,16},{9,17},{12,20},{13,21},{16,24},{1... | collective-permute-start | bytes 3145736 | tf_op jit(solution)/shard_map/ppermute | solution.py:427
  185.2 24.4 %collective-permute-start.27 = (bf16[2,256,1024]{2,1,0:T(8,128)(2,1)S(1)}, bf16[2,256,1024]{2,1,0:T(8,128)(2,1)S(1)}, u32[]{:S(2)}, u32[]{:S(2)}) collective-permute-start(bf16[2,256,1024]{2,1,0:T(8,128)(2,1)S(1)} %get-tuple-element.52), channel_id=1, source_target_pairs={{0,1},{1,5},{4,0},{5,4},{8,9},{9,13},{12,8},{13,12},{16,17},{17,21... | collective-permute-start | bytes 3145736 | tf_op jit(solution)/shard_map/ppermute | solution.py:427
  185.4 24.2 %collective-permute-start.26 = (bf16[256,1024]{1,0:T(8,128)(2,1)S(1)}, bf16[256,1024]{1,0:T(8,128)(2,1)S(1)}, u32[]{:S(2)}, u32[]{:S(2)}) collective-permute-start(bf16[256,1024]{1,0:T(8,128)(2,1)S(1)} %get-tuple-element.51), channel_id=1, source_target_pairs={{0,3},{1,6},{4,2},{5,7},{8,11},{9,14},{12,10},{13,15},{16,19},{17,... | collective-permute-start | bytes 1572872 | tf_op jit(solution)/shard_map/ppermute | solution.py:427
  209.5 25.9 %collective-permute-start.29 = (bf16[256,1024]{1,0:T(8,128)(2,1)S(1)}, bf16[256,1024]{1,0:T(8,128)(2,1)S(1)}, u32[]{:S(2)}, u32[]{:S(2)}) collective-permute-start(bf16[256,1024]{1,0:T(8,128)(2,1)S(1)} %get-tuple-element.61), channel_id=1, source_target_pairs={{0,3},{1,6},{4,2},{5,7},{8,11},{9,14},{12,10},{13,15},{16,19},{17,... | collective-permute-start | bytes 1572872 | tf_op jit(solution)/shard_map/ppermute | solution.py:427
  211.9 23.5 %collective-permute-start.30 = (bf16[256,1024]{1,0:T(8,128)(2,1)S(1)}, bf16[256,1024]{1,0:T(8,128)(2,1)S(1)}, u32[]{:S(2)}, u32[]{:S(2)}) collective-permute-start(bf16[256,1024]{1,0:T(8,128)(2,1)S(1)} %get-tuple-element.63), channel_id=1, source_target_pairs={{0,1},{1,5},{4,0},{5,4},{8,9},{9,13},{12,8},{13,12},{16,17},{17,21... | collective-permute-start | bytes 1572872 | tf_op jit(solution)/shard_map/ppermute | solution.py:427

commit v6 on v5

--- a/solution.py
+++ b/solution.py
@@ -493,7 +493,7 @@
         static=(2,),
     )
     c_far, c_near = send_home(c_pieces[: half // 2], far), c_pieces[half // 2 :]
-    j_next = send(after(j_new, a_next), plan.next)
+    j_next = send(after(j_new, f), plan.next)
     a_next = after(a_next, f, *c_far)
     a_next_swap = swap(a_next)
     a_pieces = kernel(

time: 239 us -> 241 us (level)
  transfers between devices with their start and end apart: 31 -> 31, of which waited for: 12 -> 13; matrix products, arithmetic and copies ran while one was open for 3% -> 3% of each run, Pallas kernels for 17% -> 17%
where the time goes in v6:
time: 241 us; the launch traced here: 237 us
  waiting for transfers between devices  121 us (50%)
  starting transfers between devices  64.9 us (27%)
  Pallas kernels  41 us (17%)
  other arithmetic  8.45 us (4%)
    ppermute x31, waiting for transfers between devices, send(): return lax.ppermute(x, AXES, routes)  121 us
    ppermute x31, starting transfers between devices, send(): return lax.ppermute(x, AXES, routes)  64.9 us
    pallas_call x8, Pallas kernels, call(): pl.pallas_call(kernel, out_shape=list(out_shapes), in_specs=[HBM] * len(o...  41 us
  transfers between devices with their start and end apart: 31, of which 13 were waited for; matrix products, arithmetic and copies ran while one was open for 3% of the time, Pallas kernels for 17%

profile of v6, /device:TPU:10, one launch (start us, length us, event | category | flops | bytes accessed | tf_op | source)
XLA Modules:
  0.0 236.9 jit_solution(9479149436344914158)
XLA Ops:
  0.7 2.1 select_bitcast_fusion.1
  2.8 0.7 collective-permute-start.1
  3.5 4.9 %collective-permute-start = (bf16[256,1024]{1,0:T(8,128)(2,1)S(1)}, bf16[256,1024]{1,0:T(8,128)(2,1)}, u32[]{:S(2)}, u32[]{:S(2)}) collective-permute-start(bf16[256,1024]{1,0:T(8,128)(2,1)S(1)} %get-tuple-element.69), channel_id=1, source_target_pairs={{2,0},{6,5},{10,8},{14,13},{18,16},{22,21},{26,24},{30,29},{29,31}... | collective-permute-start | bytes 1572872 | tf_op jit(solution)/shard_map/ppermute | solution.py:427
  8.4 1.3 fusion
  9.8 2.6 %collective-permute-start.3 = (bf16[3,256,1024]{2,1,0:T(8,128)(2,1)}, bf16[3,256,1024]{2,1,0:T(8,128)(2,1)S(1)}, u32[]{:S(2)}, u32[]{:S(2)}) collective-permute-start(bf16[3,256,1024]{2,1,0:T(8,128)(2,1)} %fusion), channel_id=1, source_target_pairs={{1,0},{4,5},{9,8},{12,13},{17,16},{20,21},{25,24},{28,29},{0,1},{5... | collective-permute-start | bytes 4718600 | tf_op jit(solution)/shard_map/ppermute | solution.py:427
  12.3 18.2 %collective-permute-done = bf16[256,1024]{1,0:T(8,128)(2,1)} collective-permute-done((bf16[256,1024]{1,0:T(8,128)(2,1)S(1)}, bf16[256,1024]{1,0:T(8,128)(2,1)}, u32[]{:S(2)}, u32[]{:S(2)}) %collective-permute-start) | collective-permute-done | bytes 524320 | tf_op jit(solution)/shard_map/ppermute | solution.py:427
  30.6 1.8 collective-permute-start.2
  32.4 1.1 pad_maximum_fusion
  33.5 1.6 collective-permute-start.8
  35.1 1.3 collective-permute-start.9
  36.4 9.2 %collective-permute-start.6 = (bf16[2,256,1024]{2,1,0:T(8,128)(2,1)}, bf16[2,256,1024]{2,1,0:T(8,128)(2,1)}, u32[]{:S(2)}, u32[]{:S(2)}) collective-permute-start(bf16[2,256,1024]{2,1,0:T(8,128)(2,1)} %pad_maximum_fusion), channel_id=1, source_target_pairs={{2,0},{6,5},{10,8},{14,13},{18,16},{22,21},{26,24},{30,29},{29,31}... | collective-permute-start | bytes 3145736 | tf_op jit(solution)/shard_map/ppermute | solution.py:427
  45.6 36.7 %collective-permute-done.9 = bf16[256,1024]{1,0:T(8,128)(2,1)S(1)} collective-permute-done((bf16[256,1024]{1,0:T(8,128)(2,1)S(1)}, bf16[256,1024]{1,0:T(8,128)(2,1)S(1)}, u32[]{:S(2)}, u32[]{:S(2)}) %collective-permute-start.9) | collective-permute-done | bytes 524320 | tf_op jit(solution)/shard_map/ppermute | solution.py:427
  82.3 1.3 collective-permute-start.7
  83.6 1.2 broadcast_select_fusion.1.refs_5_
  84.8 2.8 %collective-permute-start.11 = (bf16[2,256,1024]{2,1,0:T(8,128)(2,1)S(1)}, bf16[2,256,1024]{2,1,0:T(8,128)(2,1)}, u32[]{:S(2)}, u32[]{:S(2)}) collective-permute-start(bf16[2,256,1024]{2,1,0:T(8,128)(2,1)S(1)} %broadcast_select_fusion.1.refs_5_), channel_id=1, source_target_pairs={{0,4},{1,5},{2,6},{3,7},{4,0},{5,1},{6,2},{7,3},{8,12},{9,13},{10,... | collective-permute-start | bytes 3145736 | tf_op jit(solution)/shard_map/ppermute | solution.py:427
  87.7 1.6 broadcast_select_fusion.refs_0_.refs_8_.refs_16_
  89.3 0.5 collective-permute-start.4
  89.8 3.9 %collective-permute-done.7 = bf16[256,1024]{1,0:T(8,128)(2,1)} collective-permute-done((bf16[256,1024]{1,0:T(8,128)(2,1)}, bf16[256,1024]{1,0:T(8,128)(2,1)}, u32[]{:S(2)}, u32[]{:S(2)}) %collective-permute-start.7) | collective-permute-done | bytes 524320 | tf_op jit(solution)/shard_map/ppermute | solution.py:427
  93.7 1.2 broadcast_select_fusion.2.refs_4_
  94.8 0.9 collective-permute-start.10
  95.8 1.3 collective-permute-start.15
  97.1 1.3 collective-permute-start.14
  98.4 11.5 %shard_map.41 = (bf16[512,1024]{1,0:T(8,128)(2,1)S(1)}, bf16[1024,1024]{1,0:T(8,128)(2,1)S(1)}, bf16[1024,1024]{1,0:T(8,128)(2,1)S(1)}, bf16[1024,1024]{1,0:T(8,128)(2,1)S(1)}, bf16[512,1024]{1,0:T(8,128)(2,1)S(1)}) custom-call(bf16[3,256,1024]{2,1,0:T(8,128)(2,1)S(1)} %broadcast_select_fusion.refs_0_.refs_8_.refs_16_, ...), custom_call_target="tpu_custom_call" | custom-call | flops 1 | bytes 1 | tf_op jit(solution)/shard_map/pallas_call | solution.py:82
  110.0 3.4 %collective-permute-start.13 = (bf16[512,1024]{1,0:T(8,128)(2,1)S(1)}, bf16[512,1024]{1,0:T(8,128)(2,1)S(1)}, u32[]{:S(2)}, u32[]{:S(2)}) collective-permute-start(bf16[512,1024]{1,0:T(8,128)(2,1)S(1)} %get-tuple-element.35.cq_mine), channel_id=1, source_target_pairs={{0,8},{1,9},{4,12},{5,13},{8,16},{9,17},{12,20},{13,21},{16,24},{1... | collective-permute-start | bytes 3145736 | tf_op jit(solution)/shard_map/ppermute | solution.py:427
  113.4 10.5 %collective-permute-done.14 = bf16[2,256,1024]{2,1,0:T(8,128)(2,1)S(1)} collective-permute-done((bf16[2,256,1024]{2,1,0:T(8,128)(2,1)}, bf16[2,256,1024]{2,1,0:T(8,128)(2,1)S(1)}, u32[]{:S(2)}, u32[]{:S(2)}) %collective-permute-start.14) | collective-permute-done | bytes 1048608 | tf_op jit(solution)/shard_map/ppermute | solution.py:427
  124.1 0.5 collective-permute-start.16
  124.8 0.4 collective-permute-start.17
  125.2 0.7 collective-permute-done.18.refs_22_
  126.0 0.7 collective-permute-done.16.refs_14_
  126.7 0.7 collective-permute-done.19.refs_23_
  127.5 0.7 collective-permute-done.17.refs_15_
  128.2 7.4 %shard_map.42 = (bf16[512,1024]{1,0:T(8,128)(2,1)S(1)}, bf16[512,1024]{1,0:T(8,128)(2,1)S(1)}) custom-call(bf16[512,1024]{1,0:T(8,128)(2,1)S(1)} %get-tuple-element.37.f_ref, bf16[1024,1024]{1,0:T(8,128)(2,1)S(1)} %get-tuple-element.38.jq_ref, bf16[1024,1024]{1,0:T(8,128)(2,1)S(1)} %get-tuple-element.39.x1_ref, bf16[1024,1024]{1,0:T(8,128)(2,1)} %copy-done, ...), custom_call_target="tpu_custom_call" | custom-call | flops 1 | bytes 1 | tf_op jit(solution)/shard_map/pallas_call | solution.py:82
  136.2 1.5 collective-permute-start.20
  137.7 4.3 %collective-permute-start.24 = (bf16[512,1024]{1,0:T(8,128)(2,1)S(1)}, bf16[512,1024]{1,0:T(8,128)(2,1)S(1)}, u32[]{:S(2)}, u32[]{:S(2)}) collective-permute-start(bf16[512,1024]{1,0:T(8,128)(2,1)S(1)} %get-tuple-element.46.a_mine.aq_mine), channel_id=1, source_target_pairs={{0,8},{1,9},{4,12},{5,13},{8,16},{9,17},{12,20},{13,21},{16,24},{1... | collective-permute-start | bytes 3145736 | tf_op jit(solution)/shard_map/ppermute | solution.py:427
  142.0 10.7 %shard_map.43 = (bf16[256,1024]{1,0:T(8,128)(2,1)S(1)}, bf16[256,1024]{1,0:T(8,128)(2,1)S(1)}, bf16[512,1024]{1,0:T(8,128)(2,1)S(1)}, bf16[1024,1024]{1,0:T(8,128)(2,1)S(1)}, bf16[1024,1024]{1,0:T(8,128)(2,1)S(1)}) custom-call(bf16[512,1024]{1,0:T(8,128)(2,1)S(1)} %collective-permute-done.13.c_mine, bf16[512,1024]{1,0:T(8,128)(2,1)S(1)} %collective-permute-done.20.c_theirs, ...), custom_call_target="tpu_custom_call" | custom-call | flops 1 | bytes 1 | tf_op jit(solution)/shard_map/pallas_call | solution.py:82
  152.8 11.9 %collective-permute-done.24.a_mine = bf16[512,1024]{1,0:T(8,128)(2,1)S(1)} collective-permute-done((bf16[512,1024]{1,0:T(8,128)(2,1)S(1)}, bf16[512,1024]{1,0:T(8,128)(2,1)S(1)}, u32[]{:S(2)}, u32[]{:S(2)}) %collective-permute-start.24) | collective-permute-done | bytes 1048608 | tf_op jit(solution)/shard_map/ppermute | solution.py:427
  164.7 16.0 %collective-permute-start.25 = (bf16[512,1024]{1,0:T(8,128)(2,1)S(1)}, bf16[512,1024]{1,0:T(8,128)(2,1)S(1)}, u32[]{:S(2)}, u32[]{:S(2)}) collective-permute-start(bf16[512,1024]{1,0:T(8,128)(2,1)S(1)} %collective-permute-done.24.a_mine), channel_id=1, source_target_pairs={{0,4},{1,5},{2,6},{3,7},{4,0},{5,1},{6,2},{7,3},{8,12},{9,13},{10,... | collective-permute-start | bytes 3145736 | tf_op jit(solution)/shard_map/ppermute | solution.py:427
  180.7 2.5 %collective-permute-start.28 = (bf16[512,1024]{1,0:T(8,128)(2,1)S(1)}, bf16[512,1024]{1,0:T(8,128)(2,1)S(1)}, u32[]{:S(2)}, u32[]{:S(2)}) collective-permute-start(bf16[512,1024]{1,0:T(8,128)(2,1)S(1)} %get-tuple-element.58.j_mine.jq_mine), channel_id=1, source_target_pairs={{0,8},{1,9},{4,12},{5,13},{8,16},{9,17},{12,20},{13,21},{16,24},{1... | collective-permute-start | bytes 3145736 | tf_op jit(solution)/shard_map/ppermute | solution.py:427
  183.2 1.9 shard_map.44
  185.4 1.7 collective-permute-start.26
  187.1 4.7 %shard_map.46.h_ref = bf16[512,1024]{1,0:T(8,128)(2,1)S(1)} custom-call(bf16[512,1024]{1,0:T(8,128)(2,1)S(1)} %collective-permute-done.24.a_mine, bf16[512,1024]{1,0:T(8,128)(2,1)S(1)} %collective-permute-done.25.a_theirs, bf16[512,1024]{1,0:T(8,128)(2,1)S(1)} %get-tuple-element.58.j_mine.jq_mine, bf16[512,1024]{1,0:T(8,128)(2,1)S(1)} %collective-permute-done.21.j_theirs, ...), custom_call_target="tpu_custom_call" | custom-call | flops 1 | bytes 1 | tf_op jit(solution)/shard_map/pallas_call | solution.py:82
  191.8 15.9 %collective-permute-done.28.jp_mine = bf16[512,1024]{1,0:T(8,128)(2,1)S(1)} collective-permute-done((bf16[512,1024]{1,0:T(8,128)(2,1)S(1)}, bf16[512,1024]{1,0:T(8,128)(2,1)S(1)}, u32[]{:S(2)}, u32[]{:S(2)}) %collective-permute-start.28) | collective-permute-done | bytes 1048608 | tf_op jit(solution)/shard_map/ppermute | solution.py:427
  207.7 1.9 shard_map.47
  209.5 3.0 %collective-permute-start.30 = (bf16[256,1024]{1,0:T(8,128)(2,1)S(1)}, bf16[256,1024]{1,0:T(8,128)(2,1)S(1)}, u32[]{:S(2)}, u32[]{:S(2)}) collective-permute-start(bf16[256,1024]{1,0:T(8,128)(2,1)S(1)} %get-tuple-element.63), channel_id=1, source_target_pairs={{0,1},{1,5},{4,0},{5,4},{8,9},{9,13},{12,8},{13,12},{16,17},{17,21... | collective-permute-start | bytes 1572872 | tf_op jit(solution)/shard_map/ppermute | solution.py:427
  212.7 1.7 shard_map.45
  214.4 8.2 %collective-permute-done.30.refs_1_ = bf16[256,1024]{1,0:T(8,128)(2,1)S(1)} collective-permute-done((bf16[256,1024]{1,0:T(8,128)(2,1)S(1)}, bf16[256,1024]{1,0:T(8,128)(2,1)S(1)}, u32[]{:S(2)}, u32[]{:S(2)}) %collective-permute-start.30) | collective-permute-done | bytes 524320 | tf_op jit(solution)/shard_map/ppermute | solution.py:427
  222.6 12.8 %collective-permute-done.29.refs_0_ = bf16[256,1024]{1,0:T(8,128)(2,1)S(1)} collective-permute-done((bf16[256,1024]{1,0:T(8,128)(2,1)S(1)}, bf16[256,1024]{1,0:T(8,128)(2,1)S(1)}, u32[]{:S(2)}, u32[]{:S(2)}) %collective-permute-start.29) | collective-permute-done | bytes 524320 | tf_op jit(solution)/shard_map/ppermute | solution.py:427
  235.4 1.3 shard_map.48
  (38 shorter events, 1.6 us)
Async XLA Ops:
  0.6 7.8 %copy-start.1 = (bf16[3,1,256,1024]{3,2,1,0:T(8,128)(2,1)S(1)}, bf16[3,1,256,1024]{3,2,1,0:T(8,128)(2,1)}, u32[]{:S(2)}) copy-start(bf16[3,1,256,1024]{3,2,1,0:T(8,128)(2,1)} %param.3) | copy-start | bytes 4718596
  0.6 7.8 %copy-start.2 = (bf16[3,1,256,1024]{3,2,1,0:T(8,128)(2,1)S(1)}, bf16[3,1,256,1024]{3,2,1,0:T(8,128)(2,1)}, u32[]{:S(2)}) copy-start(bf16[3,1,256,1024]{3,2,1,0:T(8,128)(2,1)} %param.2) | copy-start | bytes 4718596
  2.8 9.5 %collective-permute-start.1 = (bf16[256,1024]{1,0:T(8,128)(2,1)S(1)}, bf16[256,1024]{1,0:T(8,128)(2,1)S(1)}, u32[]{:S(2)}, u32[]{:S(2)}) collective-permute-start(bf16[256,1024]{1,0:T(8,128)(2,1)S(1)} %get-tuple-element.69), channel_id=1, source_target_pairs={{3,0},{7,5},{11,8},{15,13},{19,16},{23,21},{27,24},{31,29},{28,31}... | collective-permute-start | bytes 1572872 | tf_op jit(solution)/shard_map/ppermute | solution.py:427
  3.5 27.0 %collective-permute-start = (bf16[256,1024]{1,0:T(8,128)(2,1)S(1)}, bf16[256,1024]{1,0:T(8,128)(2,1)}, u32[]{:S(2)}, u32[]{:S(2)}) collective-permute-start(bf16[256,1024]{1,0:T(8,128)(2,1)S(1)} %get-tuple-element.69), channel_id=1, source_target_pairs={{2,0},{6,5},{10,8},{14,13},{18,16},{22,21},{26,24},{30,29},{29,31}... | collective-permute-start | bytes 1572872 | tf_op jit(solution)/shard_map/ppermute | solution.py:427
  9.8 77.8 %collective-permute-start.3 = (bf16[3,256,1024]{2,1,0:T(8,128)(2,1)}, bf16[3,256,1024]{2,1,0:T(8,128)(2,1)S(1)}, u32[]{:S(2)}, u32[]{:S(2)}) collective-permute-start(bf16[3,256,1024]{2,1,0:T(8,128)(2,1)} %fusion), channel_id=1, source_target_pairs={{1,0},{4,5},{9,8},{12,13},{17,16},{20,21},{25,24},{28,29},{0,1},{5... | collective-permute-start | bytes 4718600 | tf_op jit(solution)/shard_map/ppermute | solution.py:427
  30.6 57.1 %collective-permute-start.2 = (bf16[3,256,1024]{2,1,0:T(8,128)(2,1)}, bf16[3,256,1024]{2,1,0:T(8,128)(2,1)}, u32[]{:S(2)}, u32[]{:S(2)}) collective-permute-start(bf16[3,256,1024]{2,1,0:T(8,128)(2,1)} %fusion), channel_id=1, source_target_pairs={{4,12},{12,20},{20,28},{27,19},{19,11},{11,3}} | collective-permute-start | bytes 4718600 | tf_op jit(solution)/shard_map/ppermute | solution.py:427
  33.5 50.1 %collective-permute-start.8 = (bf16[2,256,1024]{2,1,0:T(8,128)(2,1)}, bf16[2,256,1024]{2,1,0:T(8,128)(2,1)}, u32[]{:S(2)}, u32[]{:S(2)}) collective-permute-start(bf16[2,256,1024]{2,1,0:T(8,128)(2,1)} %pad_maximum_fusion), channel_id=1, source_target_pairs={{3,0},{7,5},{11,8},{15,13},{19,16},{23,21},{27,24},{31,29},{28,31}... | collective-permute-start | bytes 3145736 | tf_op jit(solution)/shard_map/ppermute | solution.py:427
  35.1 47.2 %collective-permute-start.9 = (bf16[256,1024]{1,0:T(8,128)(2,1)S(1)}, bf16[256,1024]{1,0:T(8,128)(2,1)S(1)}, u32[]{:S(2)}, u32[]{:S(2)}) collective-permute-start(bf16[256,1024]{1,0:T(8,128)(2,1)S(1)} %collective-permute-done.1.refs_9_), channel_id=1, source_target_pairs={{0,1},{5,12},{8,9},{13,20},{16,17},{21,28},{24,25},{31,30},{26,19}... | collective-permute-start | bytes 1572872 | tf_op jit(solution)/shard_map/ppermute | solution.py:427
  36.4 57.3 %collective-permute-start.6 = (bf16[2,256,1024]{2,1,0:T(8,128)(2,1)}, bf16[2,256,1024]{2,1,0:T(8,128)(2,1)}, u32[]{:S(2)}, u32[]{:S(2)}) collective-permute-start(bf16[2,256,1024]{2,1,0:T(8,128)(2,1)} %pad_maximum_fusion), channel_id=1, source_target_pairs={{2,0},{6,5},{10,8},{14,13},{18,16},{22,21},{26,24},{30,29},{29,31}... | collective-permute-start | bytes 3145736 | tf_op jit(solution)/shard_map/ppermute | solution.py:427
  82.3 1.3 copy-start.3
  82.3 11.4 %collective-permute-start.7 = (bf16[256,1024]{1,0:T(8,128)(2,1)}, bf16[256,1024]{1,0:T(8,128)(2,1)}, u32[]{:S(2)}, u32[]{:S(2)}) collective-permute-start(bf16[256,1024]{1,0:T(8,128)(2,1)} %collective-permute-done), channel_id=1, source_target_pairs={{0,1},{5,12},{8,9},{13,20},{16,17},{21,28},{24,25},{31,30},{26,19}... | collective-permute-start | bytes 1572872 | tf_op jit(solution)/shard_map/ppermute | solution.py:427
  84.8 12.3 %collective-permute-start.11 = (bf16[2,256,1024]{2,1,0:T(8,128)(2,1)S(1)}, bf16[2,256,1024]{2,1,0:T(8,128)(2,1)}, u32[]{:S(2)}, u32[]{:S(2)}) collective-permute-start(bf16[2,256,1024]{2,1,0:T(8,128)(2,1)S(1)} %broadcast_select_fusion.1.refs_5_), channel_id=1, source_target_pairs={{0,4},{1,5},{2,6},{3,7},{4,0},{5,1},{6,2},{7,3},{8,12},{9,13},{10,... | collective-permute-start | bytes 3145736 | tf_op jit(solution)/shard_map/ppermute | solution.py:427
  87.6 10.8 %collective-permute-start.5 = (bf16[3,256,1024]{2,1,0:T(8,128)(2,1)S(1)}, bf16[3,256,1024]{2,1,0:T(8,128)(2,1)S(1)}, u32[]{:S(2)}, u32[]{:S(2)}) collective-permute-start(bf16[3,256,1024]{2,1,0:T(8,128)(2,1)S(1)} %collective-permute-done.3.refs_1_.refs_9_.refs_17_), channel_id=1, source_target_pairs={{0,4},{1,5},{2,6},{3,7},{4,0},{5,1},{6,2},{7,3},{8,12},{9,13},{10,... | collective-permute-start | bytes 4718600 | tf_op jit(solution)/shard_map/ppermute | solution.py:427
  89.3 9.1 %collective-permute-start.4 = (bf16[3,256,1024]{2,1,0:T(8,128)(2,1)S(1)}, bf16[3,256,1024]{2,1,0:T(8,128)(2,1)S(1)}, u32[]{:S(2)}, u32[]{:S(2)}) collective-permute-start(bf16[3,256,1024]{2,1,0:T(8,128)(2,1)S(1)} %broadcast_select_fusion.refs_0_.refs_8_.refs_16_), channel_id=1, source_target_pairs={{0,4},{1,5},{2,6},{3,7},{4,0},{5,1},{6,2},{7,3},{8,12},{9,13},{10,... | collective-permute-start | bytes 4718600 | tf_op jit(solution)/shard_map/ppermute | solution.py:427
  93.7 2.1 collective-permute-start.12
  94.8 3.6 %collective-permute-start.10 = (bf16[2,256,1024]{2,1,0:T(8,128)(2,1)S(1)}, bf16[2,256,1024]{2,1,0:T(8,128)(2,1)S(1)}, u32[]{:S(2)}, u32[]{:S(2)}) collective-permute-start(bf16[2,256,1024]{2,1,0:T(8,128)(2,1)S(1)} %broadcast_select_fusion.2.refs_4_), channel_id=1, source_target_pairs={{0,4},{1,5},{2,6},{3,7},{4,0},{5,1},{6,2},{7,3},{8,12},{9,13},{10,... | collective-permute-start | bytes 3145736 | tf_op jit(solution)/shard_map/ppermute | solution.py:427
  95.8 17.6 %collective-permute-start.15 = (bf16[2,256,1024]{2,1,0:T(8,128)(2,1)}, bf16[2,256,1024]{2,1,0:T(8,128)(2,1)S(1)}, u32[]{:S(2)}, u32[]{:S(2)}) collective-permute-start(bf16[2,256,1024]{2,1,0:T(8,128)(2,1)} %collective-permute-done.8), channel_id=1, source_target_pairs={{0,1},{5,12},{8,9},{13,20},{16,17},{21,28},{24,25},{31,30},{26,19}... | collective-permute-start | bytes 3145736 | tf_op jit(solution)/shard_map/ppermute | solution.py:427
  97.1 26.8 %collective-permute-start.14 = (bf16[2,256,1024]{2,1,0:T(8,128)(2,1)}, bf16[2,256,1024]{2,1,0:T(8,128)(2,1)S(1)}, u32[]{:S(2)}, u32[]{:S(2)}) collective-permute-start(bf16[2,256,1024]{2,1,0:T(8,128)(2,1)} %collective-permute-done.6), channel_id=1, source_target_pairs={{0,1},{5,12},{8,9},{13,20},{16,17},{21,28},{24,25},{31,30},{26,19}... | collective-permute-start | bytes 3145736 | tf_op jit(solution)/shard_map/ppermute | solution.py:427
  110.0 14.7 %copy-start = (bf16[1024,1024]{1,0:T(8,128)(2,1)}, bf16[1024,1024]{1,0:T(8,128)(2,1)S(1)}, u32[]{:S(2)}) copy-start(bf16[1024,1024]{1,0:T(8,128)(2,1)S(1)} %get-tuple-element.40.r_ref) | copy-start | bytes 6291460
  110.0 26.2 %collective-permute-start.13 = (bf16[512,1024]{1,0:T(8,128)(2,1)S(1)}, bf16[512,1024]{1,0:T(8,128)(2,1)S(1)}, u32[]{:S(2)}, u32[]{:S(2)}) collective-permute-start(bf16[512,1024]{1,0:T(8,128)(2,1)S(1)} %get-tuple-element.35.cq_mine), channel_id=1, source_target_pairs={{0,8},{1,9},{4,12},{5,13},{8,16},{9,17},{12,20},{13,21},{16,24},{1... | collective-permute-start | bytes 3145736 | tf_op jit(solution)/shard_map/ppermute | solution.py:427
  124.0 2.0 collective-permute-start.18
  124.1 2.6 %collective-permute-start.16 = (bf16[256,1024]{1,0:T(8,128)(2,1)S(1)}, bf16[256,1024]{1,0:T(8,128)(2,1)S(1)}, u32[]{:S(2)}, u32[]{:S(2)}) collective-permute-start(bf16[256,1024]{1,0:T(8,128)(2,1)S(1)} %get-tuple-element.74.refs_12_), channel_id=1, source_target_pairs={{0,4},{1,5},{2,6},{3,7},{4,0},{5,1},{6,2},{7,3},{8,12},{9,13},{10,... | collective-permute-start | bytes 1572872 | tf_op jit(solution)/shard_map/ppermute | solution.py:427
  124.6 2.8 %collective-permute-start.19 = (bf16[256,1024]{1,0:T(8,128)(2,1)S(1)}, bf16[256,1024]{1,0:T(8,128)(2,1)S(1)}, u32[]{:S(2)}, u32[]{:S(2)}) collective-permute-start(bf16[256,1024]{1,0:T(8,128)(2,1)S(1)} %get-tuple-element.71.refs_21_), channel_id=1, source_target_pairs={{0,4},{1,5},{2,6},{3,7},{4,0},{5,1},{6,2},{7,3},{8,12},{9,13},{10,... | collective-permute-start | bytes 1572872 | tf_op jit(solution)/shard_map/ppermute | solution.py:427
  124.8 3.4 %collective-permute-start.17 = (bf16[256,1024]{1,0:T(8,128)(2,1)S(1)}, bf16[256,1024]{1,0:T(8,128)(2,1)S(1)}, u32[]{:S(2)}, u32[]{:S(2)}) collective-permute-start(bf16[256,1024]{1,0:T(8,128)(2,1)S(1)} %get-tuple-element.72.refs_13_), channel_id=1, source_target_pairs={{0,4},{1,5},{2,6},{3,7},{4,0},{5,1},{6,2},{7,3},{8,12},{9,13},{10,... | collective-permute-start | bytes 1572872 | tf_op jit(solution)/shard_map/ppermute | solution.py:427
  135.6 6.4 %collective-permute-start.22 = (bf16[512,1024]{1,0:T(8,128)(2,1)S(1)}, bf16[512,1024]{1,0:T(8,128)(2,1)S(1)}, u32[]{:S(2)}, u32[]{:S(2)}) collective-permute-start(bf16[512,1024]{1,0:T(8,128)(2,1)S(1)} %get-tuple-element.46.a_mine.aq_mine), channel_id=1, source_target_pairs={{0,4},{1,5},{2,6},{3,7},{4,0},{5,1},{6,2},{7,3},{8,12},{9,13},{10,... | collective-permute-start | bytes 3145736 | tf_op jit(solution)/shard_map/ppermute | solution.py:427
  135.8 6.2 %collective-permute-start.21 = (bf16[512,1024]{1,0:T(8,128)(2,1)S(1)}, bf16[512,1024]{1,0:T(8,128)(2,1)S(1)}, u32[]{:S(2)}, u32[]{:S(2)}) collective-permute-start(bf16[512,1024]{1,0:T(8,128)(2,1)S(1)} %get-tuple-element.58.j_mine.jq_mine), channel_id=1, source_target_pairs={{0,4},{1,5},{2,6},{3,7},{4,0},{5,1},{6,2},{7,3},{8,12},{9,13},{10,... | collective-permute-start | bytes 3145736 | tf_op jit(solution)/shard_map/ppermute | solution.py:427
  136.2 5.8 %collective-permute-start.20 = (bf16[512,1024]{1,0:T(8,128)(2,1)S(1)}, bf16[512,1024]{1,0:T(8,128)(2,1)S(1)}, u32[]{:S(2)}, u32[]{:S(2)}) collective-permute-start(bf16[512,1024]{1,0:T(8,128)(2,1)S(1)} %collective-permute-done.13.c_mine), channel_id=1, source_target_pairs={{0,4},{1,5},{2,6},{3,7},{4,0},{5,1},{6,2},{7,3},{8,12},{9,13},{10,... | collective-permute-start | bytes 3145736 | tf_op jit(solution)/shard_map/ppermute | solution.py:427
  137.7 26.9 %collective-permute-start.24 = (bf16[512,1024]{1,0:T(8,128)(2,1)S(1)}, bf16[512,1024]{1,0:T(8,128)(2,1)S(1)}, u32[]{:S(2)}, u32[]{:S(2)}) collective-permute-start(bf16[512,1024]{1,0:T(8,128)(2,1)S(1)} %get-tuple-element.46.a_mine.aq_mine), channel_id=1, source_target_pairs={{0,8},{1,9},{4,12},{5,13},{8,16},{9,17},{12,20},{13,21},{16,24},{1... | collective-permute-start | bytes 3145736 | tf_op jit(solution)/shard_map/ppermute | solution.py:427
  152.7 11.9 %collective-permute-start.23 = (bf16[256,1024]{1,0:T(8,128)(2,1)S(1)}, bf16[256,1024]{1,0:T(8,128)(2,1)S(1)}, u32[]{:S(2)}, u32[]{:S(2)}) collective-permute-start(bf16[256,1024]{1,0:T(8,128)(2,1)S(1)} %get-tuple-element.47), channel_id=1, source_target_pairs={{0,3},{1,6},{4,2},{5,7},{8,11},{9,14},{12,10},{13,15},{16,19},{17,... | collective-permute-start | bytes 1572872 | tf_op jit(solution)/shard_map/ppermute | solution.py:427
  164.7 18.5 %collective-permute-start.25 = (bf16[512,1024]{1,0:T(8,128)(2,1)S(1)}, bf16[512,1024]{1,0:T(8,128)(2,1)S(1)}, u32[]{:S(2)}, u32[]{:S(2)}) collective-permute-start(bf16[512,1024]{1,0:T(8,128)(2,1)S(1)} %collective-permute-done.24.a_mine), channel_id=1, source_target_pairs={{0,4},{1,5},{2,6},{3,7},{4,0},{5,1},{6,2},{7,3},{8,12},{9,13},{10,... | collective-permute-start | bytes 3145736 | tf_op jit(solution)/shard_map/ppermute | solution.py:427
  180.7 26.9 %collective-permute-start.28 = (bf16[512,1024]{1,0:T(8,128)(2,1)S(1)}, bf16[512,1024]{1,0:T(8,128)(2,1)S(1)}, u32[]{:S(2)}, u32[]{:S(2)}) collective-permute-start(bf16[512,1024]{1,0:T(8,128)(2,1)S(1)} %get-tuple-element.58.j_mine.jq_mine), channel_id=1, source_target_pairs={{0,8},{1,9},{4,12},{5,13},{8,16},{9,17},{12,20},{13,21},{16,24},{1... | collective-permute-start | bytes 3145736 | tf_op jit(solution)/shard_map/ppermute | solution.py:427
  185.2 24.4 %collective-permute-start.27 = (bf16[2,256,1024]{2,1,0:T(8,128)(2,1)S(1)}, bf16[2,256,1024]{2,1,0:T(8,128)(2,1)S(1)}, u32[]{:S(2)}, u32[]{:S(2)}) collective-permute-start(bf16[2,256,1024]{2,1,0:T(8,128)(2,1)S(1)} %get-tuple-element.52), channel_id=1, source_target_pairs={{0,1},{1,5},{4,0},{5,4},{8,9},{9,13},{12,8},{13,12},{16,17},{17,21... | collective-permute-start | bytes 3145736 | tf_op jit(solution)/shard_map/ppermute | solution.py:427
  185.4 24.2 %collective-permute-start.26 = (bf16[256,1024]{1,0:T(8,128)(2,1)S(1)}, bf16[256,1024]{1,0:T(8,128)(2,1)S(1)}, u32[]{:S(2)}, u32[]{:S(2)}) collective-permute-start(bf16[256,1024]{1,0:T(8,128)(2,1)S(1)} %get-tuple-element.51), channel_id=1, source_target_pairs={{0,3},{1,6},{4,2},{5,7},{8,11},{9,14},{12,10},{13,15},{16,19},{17,... | collective-permute-start | bytes 1572872 | tf_op jit(solution)/shard_map/ppermute | solution.py:427
  209.5 13.0 %collective-permute-start.30 = (bf16[256,1024]{1,0:T(8,128)(2,1)S(1)}, bf16[256,1024]{1,0:T(8,128)(2,1)S(1)}, u32[]{:S(2)}, u32[]{:S(2)}) collective-permute-start(bf16[256,1024]{1,0:T(8,128)(2,1)S(1)} %get-tuple-element.63), channel_id=1, source_target_pairs={{0,1},{1,5},{4,0},{5,4},{8,9},{9,13},{12,8},{13,12},{16,17},{17,21... | collective-permute-start | bytes 1572872 | tf_op jit(solution)/shard_map/ppermute | solution.py:427
  212.5 22.9 %collective-permute-start.29 = (bf16[256,1024]{1,0:T(8,128)(2,1)S(1)}, bf16[256,1024]{1,0:T(8,128)(2,1)S(1)}, u32[]{:S(2)}, u32[]{:S(2)}) collective-permute-start(bf16[256,1024]{1,0:T(8,128)(2,1)S(1)} %get-tuple-element.61), channel_id=1, source_target_pairs={{0,3},{1,6},{4,2},{5,7},{8,11},{9,14},{12,10},{13,15},{16,19},{17,... | collective-permute-start | bytes 1572872 | tf_op jit(solution)/shard_map/ppermute | solution.py:427
